TPU v7x, 32 devices: a whole 2x2x4 slice. The times are simulated.
32 devices in a mesh: groups: 2 (over y), chain: 4 (over z), clus: 4 (over x, core).
Axes of the slice: x: 2, y: 2, z: 4, core: 2. Of those that a mesh axis runs over, the one named last changes fastest.
Arguments:
- embeddings: bfloat16 [16384, 768], P(('groups', 'chain', 'clus')), parts along dimension 0
- dest: int32 [16384], P(('groups', 'chain', 'clus')), parts along dimension 0, may hold values from 0 to 8191, as said below
- sizes: int32 [8], P('groups'), parts along dimension 0, may hold values from 256 to 2048, as said below
Outputs:
- best: float32 [8, 2048], P(('groups', 'clus'), 'chain'), parts along dimension 0
There are 2 independent parts, one for each index of `groups`. A program takes and returns all parts, laid end to end along the dimension named above; each array names one. Nothing has to cross between parts.
Inputs may be any that keep to these rules, and one draw needn't show every extreme that they name: `dest`: a permutation of the slots of the group; every data shard of 512 rows holds exactly 16 rows for each aligned run of 256 slots. `sizes`: some cluster has exactly 2048 members.
All inputs are finite; a program needn't handle non-finite values.
Results may differ from a plain program's by a relative error of at most 0.00054.
Values may be sent and summed in bfloat16 or wider, within the bound.
No kernel may reach another device: no remote copies, remote signals or barrier semaphores. Data moves between devices by JAX's collectives and lax.ppermute only.
A program may use at most 64 MiB of HBM per device.

v0:
```python
import jax
import jax.numpy as jnp
from jax import lax
from jax.sharding import PartitionSpec as P


def local(embeddings, dest, sizes):
    chain_len = lax.axis_size("chain")
    clus_len = lax.axis_size("clus")
    shard_count = chain_len * clus_len
    rows = embeddings.shape[0]
    sent_each = rows // shard_count
    cluster_rows = rows * chain_len
    cluster = dest // cluster_rows
    within = dest % cluster_rows
    owner = within // rows
    slot = within % rows
    target = owner * clus_len + cluster
    onehot = (target[:, None] == jnp.arange(shard_count, dtype=jnp.int32)[None, :]).astype(
        jnp.int32
    )
    rank_of = jnp.sum(jnp.cumsum(onehot, axis=0) * onehot, axis=1) - 1
    placed = target * sent_each + rank_of
    counter = jnp.arange(rows, dtype=jnp.int32)
    order = jnp.zeros((rows,), jnp.int32).at[placed].set(counter)
    send_rows = embeddings[order]
    send_slots = slot[order]
    got_rows, got_slots = (
        lax.all_to_all(send_rows, ("chain", "clus"), split_axis=0, concat_axis=0, tiled=True),
        lax.all_to_all(send_slots, ("chain", "clus"), split_axis=0, concat_axis=0, tiled=True),
    )
    inverse = jnp.zeros((rows,), jnp.int32).at[got_slots].set(counter)
    local_rows = got_rows[inverse].astype(jnp.float32)
    units = (
        local_rows * lax.rsqrt(jnp.sum(local_rows * local_rows, axis=1, keepdims=True) + 1e-06)
    ).astype(jnp.bfloat16)
    my_chain = lax.axis_index("chain")
    my_clus = lax.axis_index("clus")
    members = jnp.sum(jnp.where(jnp.arange(sizes.shape[0], dtype=jnp.int32) == my_clus, sizes, 0))
    mine = my_chain * rows + counter
    start_best = jnp.full((rows,), -1.0, jnp.float32)
    piece = lax.all_gather(units, "chain", axis=0, tiled=True)
    keys = jnp.arange(piece.shape[0], dtype=jnp.int32)

    def work(running):
        scores = lax.dot_general(
            units, piece, (((1,), (1,)), ((), ())), preferred_element_type=jnp.float32
        )
        masked = jnp.where(keys[None, :] < mine[:, None], scores, -2.0)
        return jnp.maximum(running, jnp.max(masked, axis=1))

    found = lax.cond(jnp.min(keys) < jnp.max(mine), work, lambda running: running, start_best)
    found = jnp.where(mine < members, found, jnp.zeros_like(found))
    return found.reshape(1, rows)


def solution(mesh):
    return jax.shard_map(
        local,
        mesh=mesh,
        in_specs=(
            P(("groups", "chain", "clus"), None),
            P(("groups", "chain", "clus")),
            P("groups"),
        ),
        out_specs=P(("groups", "clus"), "chain"),
        check_vma=False,
    )
```

profile of v0, /device:TPU:0, one launch (start us, length us, event | category | flops | bytes accessed | tf_op | source)
XLA Modules:
  0.0 131.5 jit_solution(8219045768172798503)
XLA Ops:
  6.5 0.0 copy-start
  6.5 0.8 add_select_fusion
  7.3 1.2 reduce-window.6
  8.5 0.2 slice_reduce_fusion
  8.7 0.1 fusion.3
  8.9 2.4 %scatter_custom_fusion = s32[512]{0:T(512)S(1)} fusion(s32[512]{0:T(512)S(1)} %compare_select_fusion.3, s32[512]{0:T(512)S(1)} %iota.24, s32[]{:T(128)} %constant.72.clone.1), kind=kCustom, calls=%fused_computation.46 | custom fusion | bytes 2052 | tf_op jit(solution)/shard_map/scatter | solution.py:25
  11.3 3.5 %gather_fusion.1 = s32[512]{0:T(512)S(1)} fusion(s32[512]{0:T(512)S(1)} %get-tuple-element.20, s32[1024]{0:T(1024)S(1)} %pad_clamp_fusion.1), kind=kCustom, calls=%fused_computation.1 | custom fusion | bytes 6144 | tf_op jit(solution)/shard_map/gather | solution.py:27
  14.8 0.7 all_to_all.19
  15.5 7.4 %all-to-all-start.1 = ((s32[16,32,1]{1,2,0:T(1,128)}), s32[16,32,1]{1,2,0:T(1,128)S(1)}, u32[]{:S(2)}, u32[]{:S(2)}) async-start(s32[16,32,1]{1,2,0:T(1,128)} %bitcast.4), calls=%async_computation.1 | async-start | bytes 16384 | tf_op jit(solution)/shard_map/all_to_all | solution.py:30
  22.9 0.0 copy-done
  22.9 2.7 %gather_fusion = bf16[512,768]{1,0:T(8,128)(2,1)} fusion(bf16[512,768]{1,0:T(8,128)(2,1)S(1)} %copy-done, s32[1024]{0:T(1024)S(1)} %pad_clamp_fusion.1), kind=kCustom, calls=%fused_computation | custom fusion | bytes 1574912 | tf_op jit(solution)/shard_map/gather | solution.py:26
  25.6 3.7 %all-to-all-done.1 = s32[16,32,1]{1,2,0:T(1,128)S(1)} async-done(((s32[16,32,1]{1,2,0:T(1,128)}), s32[16,32,1]{1,2,0:T(1,128)S(1)}, u32[]{:S(2)}, u32[]{:S(2)}) %all-to-all-start.1) | async-done | bytes 2080 | tf_op jit(solution)/shard_map/all_to_all | solution.py:30
  29.3 3.6 %all-to-all-start = ((bf16[16,32,768]{2,1,0:T(8,128)(2,1)}), bf16[16,32,768]{2,1,0:T(8,128)(2,1)S(1)}, u32[]{:S(2)}, u32[]{:S(2)}) async-start(bf16[16,32,768]{2,1,0:T(8,128)(2,1)} %bitcast.2), calls=%async_computation | async-start | bytes 1572864 | tf_op jit(solution)/shard_map/all_to_all | solution.py:29
  32.9 0.0 all-gather.2.cloned.1.call-start
  32.9 0.5 broadcast.105
  33.5 0.7 reduce.5
  34.1 0.1 all_to_all.21
  34.2 2.4 %scatter_custom_fusion.1 = s32[512]{0:T(512)S(1)} fusion(s32[512]{0:T(512)S(1)} %bitcast.28, s32[512]{0:T(512)S(1)} %iota.25, s32[]{:T(128)} %constant.72.clone.1), kind=kCustom, calls=%fused_computation.49 | custom fusion | bytes 2052 | tf_op jit(solution)/shard_map/scatter | solution.py:32
  36.7 14.9 %all-to-all-done = bf16[16,32,768]{2,1,0:T(8,128)(2,1)S(1)} async-done(((bf16[16,32,768]{2,1,0:T(8,128)(2,1)}), bf16[16,32,768]{2,1,0:T(8,128)(2,1)S(1)}, u32[]{:S(2)}, u32[]{:S(2)}) %all-to-all-start) | async-done | bytes 786464 | tf_op jit(solution)/shard_map/all_to_all | solution.py:29
  51.6 2.0 %gather_fusion.2 = bf16[512,768]{1,0:T(8,128)(2,1)S(1)} fusion(bf16[512,768]{1,0:T(8,128)(2,1)S(1)} %bitcast.26, s32[1024]{0:T(1024)S(1)} %pad_clamp_fusion), kind=kCustom, calls=%fused_computation.2 | custom fusion | bytes 1574912 | tf_op jit(solution)/shard_map/gather | solution.py:33
  53.6 0.0 copy-start.1
  53.6 0.2 fusion
  53.8 1.1 fusion.1
  54.9 0.0 all-gather.2.cloned.1.call-update
  54.9 0.6 fusion.9
  56.2 0.0 copy-done.1
  56.3 0.7 fusion.14
  56.9 62.5 %all-gather.2.cloned.1.call-done = bf16[2048,768]{1,0:T(8,128)(2,1)} async-done(((bf16[512,768]{1,0:T(8,128)(2,1)}), bf16[2048,768]{1,0:T(8,128)(2,1)}) %all-gather.2.cloned.1.call-update) | async-done | bytes 3145744 | tf_op jit(solution)/shard_map/all_gather | solution.py:42
  119.4 4.1 %conditional.1 = (f32[512]{0:T(512)S(1)}) conditional(s32[]{:T(128)} %convert_element_type.14, () %tuple.11, (s32[2048]{0:T(1024)S(1)}, s32[512]{0:T(512)S(1)}, bf16[512,768]{1,0:T(8,128)(2,1)}, bf16[2048,768]{1,0:T(8,128)(2,1)}) %tuple.12), branch_computations={%region_8.9_spmd, %region_9.11_spmd} | conditional | flops 1613758464 | bytes 3948552 | solution.py:52
  119.4 4.1 %select_reduce_fusion = f32[512]{0:T(512)S(1)} fusion(bf16[512,768]{1,0:T(8,128)(2,1)} %get-tuple-element.18, bf16[2048,768]{1,0:T(8,128)(2,1)} %get-tuple-element.19, s32[2048]{0:T(1024)S(1)} %get-tuple-element.16, s32[512]{0:T(512)S(1)} %get-tuple-element.17), kind=kOutput, calls=%fused_computation.5 | convolution fusion | flops 1613757952 | bytes 3944448 | tf_op jit(solution)/shard_map/cond/branch_1_fun/dot_general | solution.py:46
  123.4 1.2 compare_select_fusion.4
  (15 shorter events, 0.1 us)
Async XLA Ops:
  6.5 16.3 %copy-start = (bf16[512,768]{1,0:T(8,128)(2,1)S(1)}, bf16[512,768]{1,0:T(8,128)(2,1)}, u32[]{:S(2)}) copy-start(bf16[512,768]{1,0:T(8,128)(2,1)} %param.5) | copy-start | bytes 2359300
  15.5 13.8 %all-to-all-start.1 = ((s32[16,32,1]{1,2,0:T(1,128)}), s32[16,32,1]{1,2,0:T(1,128)S(1)}, u32[]{:S(2)}, u32[]{:S(2)}) async-start(s32[16,32,1]{1,2,0:T(1,128)} %bitcast.4), calls=%async_computation.1 | async-start | bytes 16384 | tf_op jit(solution)/shard_map/all_to_all | solution.py:30
  29.3 22.3 %all-to-all-start = ((bf16[16,32,768]{2,1,0:T(8,128)(2,1)}), bf16[16,32,768]{2,1,0:T(8,128)(2,1)S(1)}, u32[]{:S(2)}, u32[]{:S(2)}) async-start(bf16[16,32,768]{2,1,0:T(8,128)(2,1)} %bitcast.2), calls=%async_computation | async-start | bytes 1572864 | tf_op jit(solution)/shard_map/all_to_all | solution.py:29
  32.9 86.5 %all-gather.2.cloned.1.call-start = ((), (), s32[]{:S(2)}) async-start(), calls=%async_computation.2 | async-start | bytes 3932160 | tf_op jit(solution)/shard_map/all_gather | solution.py:42
  53.6 2.7 %copy-start.1 = (s32[4]{0:T(128)S(1)}, s32[4]{0:T(128)}, u32[]{:S(2)}) copy-start(s32[4]{0:T(128)} %param.7) | copy-start | bytes 52
Sparse Core Ops, SparseCore 0:
  55.1 64.2 all-gather.1
where the time goes:
time: 132 us; the launch traced here: 131 us
  waiting for transfers between devices  81 us (61%)
  local copies, waits for them, and re-layouts  14.6 us (11%)
  between operations  14.2 us (11%)
  starting transfers between devices  11 us (8%)
  other arithmetic  6.6 us (5%)
  matrix products  4.06 us (3%)
    all_gather x1, waiting for transfers between devices, local(): piece = lax.all_gather(units, 'chain', axis=0, tiled=True)  62.5 us
    all_to_all x1, waiting for transfers between devices, local(): lax.all_to_all(send_rows, ('chain', 'clus'), split_axis=0, concat_axis=0,...  14.9 us
    all_to_all x1, starting transfers between devices, local(): lax.all_to_all(send_slots, ('chain', 'clus'), split_axis=0, concat_axis=0...  7.36 us
    dot_general x1, matrix products, work(): lax.dot_general(units, piece, (((1,), (1,)), ((), ())), preferred_element...  4.06 us
    all_to_all x1, waiting for transfers between devices, local(): lax.all_to_all(send_slots, ('chain', 'clus'), split_axis=0, concat_axis=0...  3.68 us
    all_to_all x1, starting transfers between devices, local(): lax.all_to_all(send_rows, ('chain', 'clus'), split_axis=0, concat_axis=0,...  3.61 us
    gather x1, local copies, waits for them, and re-layouts, local(): send_slots = slot[order]  3.49 us
    gather x1, local copies, waits for them, and re-layouts, local(): send_rows = embeddings[order]  2.71 us
  transfers between devices with their start and end apart: 3, of which 3 were waited for; matrix products, arithmetic and copies ran while one was open for 6% of the time, Pallas kernels for 0%

commit v1 on v0

v1 whole, which is shorter than its diff:
```python
import functools

import jax
import jax.numpy as jnp
from jax import lax
from jax.experimental import pallas as pl
from jax.experimental.pallas import tpu as pltpu
from jax.sharding import PartitionSpec as P

PIECE = 16
VMEM = pl.BlockSpec(memory_space=pltpu.VMEM)
SMEM = pl.BlockSpec(memory_space=pltpu.SMEM)


def sort_kernel(run_slots, dest_ref, rows_ref, units_ref, slots_ref):
    rows = rows_ref.shape[0]
    runs = rows // PIECE
    dest = dest_ref[...]
    run = dest // run_slots
    within = dest % run_slots
    member = lax.broadcasted_iota(jnp.int32, (runs, rows), 0) == run
    before = lax.broadcasted_iota(jnp.int32, (rows, rows), 0) < lax.broadcasted_iota(
        jnp.int32, (rows, rows), 1
    )
    earlier = jnp.dot(
        member.astype(jnp.float32).astype(jnp.bfloat16),
        before.astype(jnp.float32).astype(jnp.bfloat16),
        preferred_element_type=jnp.float32,
    )
    rank = jnp.sum(jnp.where(member, earlier, 0.0), axis=0, keepdims=True).astype(jnp.int32)
    placed = run * PIECE + rank
    hot = (lax.broadcasted_iota(jnp.int32, (rows, rows), 0) == placed).astype(jnp.float32)
    hot = hot.astype(jnp.bfloat16)
    x = rows_ref[...].astype(jnp.float32)
    units = (x * lax.rsqrt(jnp.sum(x * x, axis=1, keepdims=True) + 1e-06)).astype(jnp.bfloat16)
    units_ref[...] = jnp.dot(hot, units, preferred_element_type=jnp.float32).astype(jnp.bfloat16)
    halves = jnp.concatenate(
        [jnp.broadcast_to(within // 256, (8, rows)), jnp.broadcast_to(within % 256, (8, rows))], axis=0
    )
    moved = lax.dot_general(
        halves.astype(jnp.float32).astype(jnp.bfloat16),
        hot,
        (((1,), (1,)), ((), ())),
        preferred_element_type=jnp.float32,
    )
    slots_ref[...] = (moved[0:1, :] * 256.0 + moved[8:9, :]).astype(jnp.int32)


def best_kernel(info_ref, slots_ref, keys_ref, out_ref, query_ref):
    shards, depth, width = keys_ref.shape
    queries = out_ref.shape[1]
    run_slots = shards * PIECE
    unit = min(run_slots, queries)
    first = info_ref[0]
    members = info_ref[1]
    first_run = first // run_slots

    def run_rows(run):
        start = pl.multiple_of(run * PIECE, PIECE)
        return keys_ref[:, pl.ds(start, PIECE), :].reshape(run_slots, width)

    def run_positions(run):
        start = pl.multiple_of(run * PIECE, PIECE)
        tile = slots_ref[pl.ds(start, PIECE), :]
        wide = jnp.broadcast_to(tile[None], (shards, PIECE, shards)).reshape(run_slots, shards)
        lane = lax.broadcasted_iota(jnp.int32, (run_slots, shards), 1)
        row = lax.broadcasted_iota(jnp.int32, (run_slots, shards), 0)
        picked = jnp.sum(jnp.where(lane == row // PIECE, wide, 0), axis=1, keepdims=True)
        return picked + run * run_slots

    for index in range(queries // unit):
        run = first_run + index
        lanes = lax.broadcasted_iota(jnp.int32, (run_slots, unit), 1) + (first + index * unit)
        hot = (run_positions(run) == lanes).astype(jnp.float32).astype(jnp.bfloat16)
        query_ref[:, index * unit : (index + 1) * unit] = lax.dot_general(
            run_rows(run), hot, (((0,), (0,)), ((), ())), preferred_element_type=jnp.float32
        ).astype(jnp.bfloat16)

    def fold(scores):
        return jnp.max(scores.reshape(run_slots // 8, 8, queries), axis=0)

    def step(run, running):
        scores = jnp.dot(run_rows(run), query_ref[...], preferred_element_type=jnp.float32)
        return jnp.maximum(running, fold(scores))

    running = lax.fori_loop(0, first_run, step, jnp.full((8, queries), -1.0, jnp.float32))
    position = first + lax.broadcasted_iota(jnp.int32, (1, queries), 1)
    for index in range(queries // unit):
        run = first_run + index
        scores = jnp.dot(run_rows(run), query_ref[...], preferred_element_type=jnp.float32)
        masked = jnp.where(run_positions(run) < position, scores, -2.0)
        running = jnp.maximum(running, fold(masked))
    found = jnp.max(running, axis=0, keepdims=True)
    out_ref[...] = jnp.where(position < members, found, 0.0)


def local(embeddings, dest, sizes):
    chain_len = lax.axis_size("chain")
    clus_len = lax.axis_size("clus")
    shards = chain_len * clus_len
    rows, width = embeddings.shape
    clusters = sizes.shape[0]
    parts = chain_len // clusters
    run_slots = shards * PIECE
    depth = rows // chain_len
    my_chain = lax.axis_index("chain")
    my_clus = lax.axis_index("clus")
    cluster = my_chain // parts
    part = my_chain % parts

    units, slots = pl.pallas_call(
        functools.partial(sort_kernel, run_slots),
        out_shape=(
            jax.ShapeDtypeStruct((rows, width), jnp.bfloat16),
            jax.ShapeDtypeStruct((1, rows), jnp.int32),
        ),
        in_specs=[VMEM, VMEM],
        out_specs=(VMEM, VMEM),
        compiler_params=pltpu.CompilerParams(vmem_limit_bytes=32 * 2**20),
        name="sort_units",
    )(dest.reshape(1, rows), embeddings)

    slots = lax.all_gather(slots, ("chain", "clus"), axis=0, tiled=True)
    slots = slots.reshape(chain_len, clus_len, clusters, -1, PIECE)
    slots = lax.dynamic_index_in_dim(slots, cluster, 2, keepdims=False)
    slots = slots.transpose(2, 3, 1, 0).reshape(-1, shards)

    got = lax.all_to_all(units, "chain", split_axis=0, concat_axis=0, tiled=True)
    keys = lax.all_gather(got, "clus", axis=0, tiled=True).reshape(shards, depth, width)
    if parts > 1:
        pieces = []
        for wanted in range(parts):
            block = keys
            for other in range(parts):
                if other != wanted:
                    pairs = [(c * parts + wanted, c * parts + other) for c in range(clusters)]
                    came = lax.ppermute(keys, "chain", pairs)
                    block = jnp.where(part == other, came, block)
            pieces.append(block)
        keys = jnp.concatenate(pieces, axis=1)

    first = (part * clus_len + my_clus) * rows
    ids = jnp.arange(clusters, dtype=jnp.int32)
    members = jnp.sum(jnp.where(ids == cluster, sizes, 0))
    info = jnp.stack([first, members]).astype(jnp.int32)
    found = pl.pallas_call(
        best_kernel,
        out_shape=jax.ShapeDtypeStruct((1, rows), jnp.float32),
        in_specs=[SMEM, VMEM, VMEM],
        out_specs=VMEM,
        scratch_shapes=[pltpu.VMEM((width, rows), jnp.bfloat16)],
        compiler_params=pltpu.CompilerParams(vmem_limit_bytes=48 * 2**20),
        name="best_of_earlier",
    )(info, slots, keys)

    pairs = []
    for z in range(chain_len):
        for k in range(clus_len):
            pairs.append((z * clus_len + k, ((z % parts) * clus_len + k) * clus_len + z // parts))
    return lax.ppermute(found, ("chain", "clus"), pairs)


def solution(mesh):
    return jax.shard_map(
        local,
        mesh=mesh,
        in_specs=(
            P(("groups", "chain", "clus"), None),
            P(("groups", "chain", "clus")),
            P("groups"),
        ),
        out_specs=P(("groups", "clus"), "chain"),
        check_vma=False,
    )
```

time: 132 us -> 82.7 us (0.63)
  the two profiles are of different devices: /device:TPU:0 before, /device:TPU:7 now
where the time goes in v1:
time: 82.7 us; the launch traced here: 82.4 us
  blocking collectives  43.3 us (52%)
  between operations  13.5 us (16%)
  waiting for transfers between devices  11 us (13%)
  Pallas kernels  4.86 us (6%)
  local copies, waits for them, and re-layouts  4.62 us (6%)
  starting transfers between devices  3.74 us (5%)
  other arithmetic  1.43 us (2%)
    all_to_all x1, blocking collectives, local(): lax.all_to_all(units, 'chain', split_axis=0, concat_axis=0, tiled=True)  23.8 us
    all_gather x1, blocking collectives, local(): slots = lax.all_gather(slots, ('chain', 'clus'), axis=0, tiled=True)  19.6 us
    all_gather x1, waiting for transfers between devices, local(): lax.all_gather(got, 'clus', axis=0, tiled=True)  7.13 us
    unnamed x9, local copies, waits for them, and re-layouts  4.3 us
    pallas_call x1, Pallas kernels, local(): pl.pallas_call(best_kernel, out_shape=jax.ShapeDtypeStruct((1, rows), jnp...  3.95 us
    ppermute x1, waiting for transfers between devices, local(): return lax.ppermute(found, ('chain', 'clus'), pairs)  3.86 us
    ppermute x1, starting transfers between devices, local(): return lax.ppermute(found, ('chain', 'clus'), pairs)  3.74 us
  transfers between devices with their start and end apart: 2, of which 2 were waited for; matrix products, arithmetic and copies ran while one was open for 2% of the time, Pallas kernels for 0%

profile of v1, /device:TPU:7, one launch (start us, length us, event | category | flops | bytes accessed | tf_op | source)
XLA Modules:
  0.0 82.4 jit_solution(14418685437468975571)
XLA Ops:
  6.5 0.0 copy-start.3
  6.5 0.0 all-gather.3.cloned.1.call-start
  6.5 0.0 copy-start.1
  6.5 1.1 %copy-done.1 = bf16[512,768]{1,0:T(8,128)(2,1)S(1)} copy-done((bf16[512,768]{1,0:T(8,128)(2,1)S(1)}, bf16[512,768]{1,0:T(8,128)(2,1)}, u32[]{:S(2)}) %copy-start.1) | copy-done | bytes 786456
  7.7 0.0 copy-start.2
  7.7 0.7 copy-done.2
  8.4 0.9 %sort_units.1 = (bf16[512,768]{1,0:T(8,128)(2,1)S(1)}, s32[1,512]{1,0:T(1,128)S(1)}) custom-call(s32[1,512]{1,0:T(1,128)S(1)} %bitcast.17, bf16[512,768]{1,0:T(8,128)(2,1)S(1)} %copy-done.1), custom_call_target="tpu_custom_call" | custom-call | tf_op jit(solution)/shard_map/sort_units/pallas_call | solution.py:111
  9.3 23.8 %all_to_all.12 = bf16[4,128,768]{2,1,0:T(8,128)(2,1)} all-to-all(bf16[4,128,768]{2,1,0:T(8,128)(2,1)S(1)} %bitcast.16), channel_id=1, replica_groups=mesh['groups'=2,'chain'=4,'clus'=4] {'chain'}, dimensions={0} | all-to-all | bytes 1572864 | tf_op jit(solution)/shard_map/all_to_all | solution.py:128
  33.0 0.0 all-gather.3.cloned.1.call-update
  33.1 19.6 %all-gather = s32[16,1,512]{2,1,0:T(1,128)S(1)} all-gather(s32[1,1,512]{2,1,0:T(1,128)S(1)} %bitcast.18), channel_id=1, replica_groups=mesh['groups'=2,'chain'=4,'clus'=4] {'chain','clus'}, dimensions={0}, use_global_device_ids=true | all-gather | bytes 34816 | tf_op jit(solution)/shard_map/all_gather | solution.py:123
  52.6 0.1 reduce
  52.7 0.1 reshape.15
  52.9 0.1 reshape.16
  53.0 0.1 copy.8.slots_ref
  53.1 0.0 copy-done.3
  53.1 0.6 fusion
  53.7 0.7 pad_add_fusion.info_ref
  54.4 7.1 %all-gather.3.cloned.1.call-done = bf16[2048,768]{1,0:T(8,128)(2,1)} async-done(((bf16[512,768]{1,0:T(8,128)(2,1)}), bf16[2048,768]{1,0:T(8,128)(2,1)}) %all-gather.3.cloned.1.call-update) | async-done | bytes 3145744 | tf_op jit(solution)/shard_map/all_gather | solution.py:129
  61.6 0.0 copy-start
  61.6 1.9 %copy-done = bf16[2048,768]{1,0:T(8,128)(2,1)S(1)} copy-done((bf16[2048,768]{1,0:T(8,128)(2,1)S(1)}, bf16[2048,768]{1,0:T(8,128)(2,1)}, u32[]{:S(2)}) %copy-start) | copy-done | bytes 3145752
  63.5 3.9 %best_of_earlier.1 = f32[1,512]{1,0:T(1,128)S(1)} custom-call(s32[2]{0:T(128)S(1)} %pad_add_fusion.info_ref, s32[128,16]{1,0:T(8,128)S(1)} %copy.8.slots_ref, bf16[16,128,768]{2,1,0:T(8,128)(2,1)S(1)} %bitcast.15), custom_call_target="tpu_custom_call" | custom-call | tf_op jit(solution)/shard_map/best_of_earlier/pallas_call | solution.py:146
  67.4 3.7 %collective-permute-start = (f32[1,512]{1,0:T(1,128)S(1)}, f32[1,512]{1,0:T(1,128)S(1)}, u32[]{:S(2)}, u32[]{:S(2)}) collective-permute-start(f32[1,512]{1,0:T(1,128)S(1)} %best_of_earlier.1), channel_id=1, source_target_pairs={{0,0},{1,4},{2,8},{3,12},{4,1},{5,5},{6,9},{7,13},{8,2},{9,6},{10,... | collective-permute-start | bytes 6152 | tf_op jit(solution)/shard_map/ppermute | solution.py:160
  71.1 3.9 %collective-permute-done = f32[1,512]{1,0:T(1,128)S(1)} collective-permute-done((f32[1,512]{1,0:T(1,128)S(1)}, f32[1,512]{1,0:T(1,128)S(1)}, u32[]{:S(2)}, u32[]{:S(2)}) %collective-permute-start) | collective-permute-done | bytes 2080 | tf_op jit(solution)/shard_map/ppermute | solution.py:160
  75.0 0.6 copy.10
  (2 shorter events, 0.0 us)
Async XLA Ops:
  6.5 46.5 %copy-start.3 = (s32[4]{0:T(128)S(1)}, s32[4]{0:T(128)}, u32[]{:S(2)}) copy-start(s32[4]{0:T(128)} %param.5) | copy-start | bytes 52
  6.5 55.0 %all-gather.3.cloned.1.call-start = ((), (), s32[]{:S(2)}) async-start(), calls=%async_computation.1 | async-start | bytes 3932160 | tf_op jit(solution)/shard_map/all_gather | solution.py:129
  6.5 1.1 %copy-start.1 = (bf16[512,768]{1,0:T(8,128)(2,1)S(1)}, bf16[512,768]{1,0:T(8,128)(2,1)}, u32[]{:S(2)}) copy-start(bf16[512,768]{1,0:T(8,128)(2,1)} %rows_ref.1) | copy-start | bytes 2359300
  7.7 0.7 copy-start.2
  61.6 1.9 %copy-start = (bf16[2048,768]{1,0:T(8,128)(2,1)S(1)}, bf16[2048,768]{1,0:T(8,128)(2,1)}, u32[]{:S(2)}) copy-start(bf16[2048,768]{1,0:T(8,128)(2,1)} %all-gather.3.cloned.1.call-done) | copy-start | bytes 9437188
  67.4 7.6 %collective-permute-start = (f32[1,512]{1,0:T(1,128)S(1)}, f32[1,512]{1,0:T(1,128)S(1)}, u32[]{:S(2)}, u32[]{:S(2)}) collective-permute-start(f32[1,512]{1,0:T(1,128)S(1)} %best_of_earlier.1), channel_id=1, source_target_pairs={{0,0},{1,4},{2,8},{3,12},{4,1},{5,5},{6,9},{7,13},{8,2},{9,6},{10,... | collective-permute-start | bytes 6152 | tf_op jit(solution)/shard_map/ppermute | solution.py:160
Sparse Core Ops, SparseCore 0:
  33.2 28.3 all-gather.2

commit v2 on v1

--- a/solution.py
+++ b/solution.py
@@ -10,6 +10,11 @@
 PIECE = 16
 VMEM = pl.BlockSpec(memory_space=pltpu.VMEM)
 SMEM = pl.BlockSpec(memory_space=pltpu.SMEM)
+HBM = pl.BlockSpec(memory_space=pltpu.HBM)
+
+
+def as_bf16(mask):
+    return mask.astype(jnp.float32).astype(jnp.bfloat16)
 
 
 def sort_kernel(run_slots, dest_ref, rows_ref, units_ref, slots_ref):
@@ -94,7 +99,7 @@
     out_ref[...] = jnp.where(position < members, found, 0.0)
 
 
-def local(embeddings, dest, sizes):
+def local_plane(embeddings, dest, sizes):
     chain_len = lax.axis_size("chain")
     clus_len = lax.axis_size("clus")
     shards = chain_len * clus_len
@@ -160,9 +165,182 @@
     return lax.ppermute(found, ("chain", "clus"), pairs)
 
 
+def lengths(embeddings):
+    chain_len = lax.axis_size("chain")
+    clus_len = lax.axis_size("clus")
+    return chain_len, clus_len, embeddings.shape[0], embeddings.shape[1]
+
+
+def send_kernel(run_slots, cluster_runs, dest_ref, rows_ref, *rest):
+    block_refs, (x_ref, sem) = rest[:-2], rest[-2:]
+    copy = pltpu.make_async_copy(rows_ref, x_ref, sem)
+    copy.start()
+    my_clus = lax.axis_index("clus")
+    rows, width = x_ref.shape
+    runs = rows // PIECE
+    depth = rows // len(block_refs)
+    dest = dest_ref[...]
+    run = lax.div(dest, run_slots)
+    within = lax.rem(dest, run_slots)
+    run = (lax.div(run, cluster_runs) ^ my_clus) * cluster_runs + lax.rem(run, cluster_runs)
+    member = lax.broadcasted_iota(jnp.int32, (runs, rows), 0) == run
+    before = lax.broadcasted_iota(jnp.int32, (rows, rows), 0) < lax.broadcasted_iota(
+        jnp.int32, (rows, rows), 1
+    )
+    earlier = jnp.dot(as_bf16(member), as_bf16(before), preferred_element_type=jnp.float32)
+    rank = jnp.sum(jnp.where(member, earlier, 0.0), axis=0, keepdims=True).astype(jnp.int32)
+    hot = as_bf16(lax.broadcasted_iota(jnp.int32, (rows, rows), 0) == run * PIECE + rank)
+    moved = lax.dot_general(
+        jnp.broadcast_to(within, (8, rows)).astype(jnp.float32).astype(jnp.bfloat16),
+        hot,
+        (((1,), (1,)), ((), ())),
+        preferred_element_type=jnp.float32,
+    ).astype(jnp.bfloat16)
+    copy.wait()
+    x = x_ref[...].astype(jnp.float32)
+    units = (x * lax.rsqrt(jnp.sum(x * x, axis=1, keepdims=True) + 1e-06)).astype(jnp.bfloat16)
+    for index, block_ref in enumerate(block_refs):
+        low = index * depth
+        block_ref[0:depth, :] = jnp.dot(
+            hot[low : low + depth], units, preferred_element_type=jnp.float32
+        ).astype(jnp.bfloat16)
+        block_ref[depth : depth + 8, :] = jnp.zeros((8, width), jnp.bfloat16)
+        block_ref[depth : depth + 8, 0:depth] = moved[:, low : low + depth]
+
+
+def home_kernel(sizes_ref, *rest):
+    chain_len = lax.axis_size("chain")
+    chunk_refs = rest[-1 - chain_len : -1]
+    keys_ref = rest[-1]
+    blocks = rest[: -1 - chain_len]
+    count = len(blocks)
+    width = keys_ref.shape[1]
+    run_slots = count * PIECE
+    depth = blocks[0].shape[0] - 8
+    runs = depth // PIECE
+    chunk = chunk_refs[0].shape[1]
+    my_clus = lax.axis_index("clus")
+    my_chain = lax.axis_index("chain")
+    home = home_of(chain_len, my_clus)
+    members = sizes_ref[my_clus]
+
+    @pl.when(my_chain != home)
+    def _():
+        for ref in chunk_refs:
+            ref[...] = jnp.zeros_like(ref)
+
+    @pl.when(my_chain == home)
+    def _():
+        slots = jnp.concatenate([ref[depth : depth + 8, 0:depth][0:1] for ref in blocks], axis=0)
+        lane = lax.broadcasted_iota(jnp.int32, (count, run_slots), 1)
+        mine = lax.div(lane, PIECE) == lax.broadcasted_iota(jnp.int32, (count, run_slots), 0)
+        from_lane = lax.broadcasted_iota(jnp.int32, (depth, run_slots), 0)
+        to_lane = lax.rem(lax.broadcasted_iota(jnp.int32, (depth, run_slots), 1), PIECE)
+        place = lax.broadcasted_iota(jnp.int32, (run_slots, run_slots), 0)
+        key_at = lax.broadcasted_iota(jnp.int32, (run_slots, run_slots), 0)
+        query_at = lax.broadcasted_iota(jnp.int32, (run_slots, run_slots), 1)
+        results = []
+        for run in range(runs):
+            low = run * PIECE
+            spread = jnp.dot(
+                slots, as_bf16(from_lane == to_lane + low), preferred_element_type=jnp.float32
+            )
+            slot = jnp.sum(jnp.where(mine, spread, 0.0), axis=0, keepdims=True).astype(jnp.int32)
+            rows = jnp.concatenate([ref[low : low + PIECE, :] for ref in blocks], axis=0)
+            base = run * run_slots
+            keys_ref[base : base + run_slots, :] = jnp.dot(
+                as_bf16(place == slot), rows, preferred_element_type=jnp.float32
+            ).astype(jnp.bfloat16)
+            scores = lax.dot_general(
+                keys_ref[0 : base + run_slots, :],
+                keys_ref[base : base + run_slots, :],
+                (((1,), (1,)), ((), ())),
+                preferred_element_type=jnp.float32,
+            )
+            best = jnp.where(key_at < query_at, scores[base:], -2.0)
+            best = jnp.max(best.reshape(run_slots // 8, 8, run_slots), axis=0)
+            if run:
+                best = jnp.maximum(best, jnp.max(scores[:base].reshape(base // 8, 8, run_slots), axis=0))
+            best = jnp.maximum(jnp.max(best, axis=0, keepdims=True), -1.0)
+            position = base + lax.broadcasted_iota(jnp.int32, (1, run_slots), 1)
+            results.append(jnp.where(position < members, best, 0.0))
+        whole = jnp.concatenate(results, axis=1)
+        for step, ref in enumerate(chunk_refs):
+            for place_of in range(chain_len):
+                @pl.when(lax.rem(home + step, chain_len) == place_of)
+                def _():
+                    ref[...] = whole[:, place_of * chunk : (place_of + 1) * chunk]
+
+
+def home_of(chain_len, clus):
+    return chain_len // 2 - 1 + clus % 2
+
+
+def local_home(embeddings, dest, sizes):
+    chain_len, clus_len, rows, width = lengths(embeddings)
+    shards = chain_len * clus_len
+    run_slots = shards * PIECE
+    depth = rows // clus_len
+    block = jax.ShapeDtypeStruct((depth + 8, width), jnp.bfloat16)
+    blocks = pl.pallas_call(
+        functools.partial(send_kernel, run_slots, depth // PIECE),
+        out_shape=(block,) * clus_len,
+        in_specs=[VMEM, HBM],
+        out_specs=(VMEM,) * clus_len,
+        scratch_shapes=[pltpu.VMEM((rows, width), jnp.bfloat16), pltpu.SemaphoreType.DMA],
+        compiler_params=pltpu.CompilerParams(vmem_limit_bytes=32 * 2**20),
+        name="send_blocks",
+    )(dest.reshape(1, rows), embeddings)
+
+    def at(chain, clus):
+        return chain * clus_len + clus
+
+    def to_home(block, step, flip):
+        pairs = []
+        for k in range(clus_len):
+            home = home_of(chain_len, k)
+            source = home + step if k % 2 else home - step
+            pairs.append((at(source % chain_len, k ^ flip), at(home, k)))
+        return lax.ppermute(block, ("chain", "clus"), pairs)
+
+    def across(block, flip):
+        pairs = [(at(z, k), at(z, k ^ flip)) for z in range(chain_len) for k in range(clus_len)]
+        return lax.ppermute(block, ("chain", "clus"), pairs)
+
+    crossed = [across(blocks[flip], flip) for flip in range(2, clus_len)]
+    keys = [blocks[0]]
+    for step in range(1, chain_len):
+        keys.append(to_home(blocks[0], step, 0))
+        keys.append(to_home(blocks[1], step, 1))
+    keys.append(across(blocks[1], 1))
+    for came in crossed:
+        keys.append(came)
+        for step in range(1, chain_len):
+            keys.append(to_home(came, step, 0))
+
+    chunk = rows
+    chunks = pl.pallas_call(
+        home_kernel,
+        out_shape=(jax.ShapeDtypeStruct((1, chunk), jnp.float32),) * chain_len,
+        in_specs=[SMEM] + [VMEM] * len(keys),
+        out_specs=(VMEM,) * chain_len,
+        scratch_shapes=[pltpu.VMEM((chain_len * chunk, width), jnp.bfloat16)],
+        compiler_params=pltpu.CompilerParams(vmem_limit_bytes=40 * 2**20),
+        name="best_at_home",
+    )(sizes, *keys)
+    found = chunks[0]
+    for step in range(1, chain_len):
+        pairs = []
+        for k in range(clus_len):
+            home = home_of(chain_len, k)
+            pairs.append((at(home, k), at((home + step) % chain_len, k)))
+        found = found + lax.ppermute(chunks[step], ("chain", "clus"), pairs)
+    return found
+
+
 def solution(mesh):
     return jax.shard_map(
-        local,
+        local_home if mesh.shape["chain"] == mesh.shape["clus"] == 4 else local_plane,
         mesh=mesh,
         in_specs=(
             P(("groups", "chain", "clus"), None),

time: 82.7 us -> 49.9 us (0.60)
  the two profiles are of different devices: /device:TPU:7 before, /device:TPU:0 now
where the time goes in v2:
time: 49.9 us; the launch traced here: 49.5 us
  starting transfers between devices  30.5 us (61%)
  waiting for transfers between devices  14.5 us (29%)
  Pallas kernels  1.89 us (4%)
  local copies, waits for them, and re-layouts  1.82 us (4%)
  other arithmetic  0.59 us (1%)
    ppermute x12, starting transfers between devices, to_home(): return lax.ppermute(block, ('chain', 'clus'), pairs)  22.3 us
    ppermute x3, waiting for transfers between devices, local_home(): found = found + lax.ppermute(chunks[step], ('chain', 'clus'), pairs)  11.3 us
    ppermute x3, starting transfers between devices, across(): return lax.ppermute(block, ('chain', 'clus'), pairs)  5.58 us
    ppermute x12, waiting for transfers between devices, to_home(): return lax.ppermute(block, ('chain', 'clus'), pairs)  3.14 us
    ppermute x3, starting transfers between devices, local_home(): found = found + lax.ppermute(chunks[step], ('chain', 'clus'), pairs)  2.62 us
    unnamed x6, local copies, waits for them, and re-layouts  1.82 us
    pallas_call x1, Pallas kernels, local_home(): pl.pallas_call(functools.partial(send_kernel, run_slots, depth // PIECE),...  1.31 us
  transfers between devices with their start and end apart: 18, of which 2 were waited for; matrix products, arithmetic and copies ran while one was open for 0% of the time, Pallas kernels for 0%

profile of v2, /device:TPU:0, one launch (start us, length us, event | category | flops | bytes accessed | tf_op | source)
XLA Modules:
  0.0 49.5 jit_solution(2522014632119180906)
XLA Ops:
  0.0 0.0 copy-start
  0.0 1.1 %copy-done = bf16[512,768]{1,0:T(8,128)(2,1)S(1)} copy-done((bf16[512,768]{1,0:T(8,128)(2,1)S(1)}, bf16[512,768]{1,0:T(8,128)(2,1)}, u32[]{:S(2)}) %copy-start) | copy-done | bytes 786456
  1.1 0.0 copy-start.1
  1.1 0.7 %copy-done.1 = s32[512]{0:T(512)S(1)} copy-done((s32[512]{0:T(512)S(1)}, s32[512]{0:T(512)}, u32[]{:S(2)}) %copy-start.1) | copy-done | bytes 2072
  1.8 1.3 %send_blocks.1 = (bf16[136,768]{1,0:T(8,128)(2,1)S(1)}, bf16[136,768]{1,0:T(8,128)(2,1)S(1)}, bf16[136,768]{1,0:T(8,128)(2,1)S(1)}, bf16[136,768]{1,0:T(8,128)(2,1)S(1)}) custom-call(s32[1,512]{1,0:T(1,128)S(1)} %bitcast.1, bf16[512,768]{1,0:T(8,128)(2,1)S(1)} %copy-done), custom_call_target="tpu_custom_call" | custom-call | tf_op jit(solution)/shard_map/send_blocks/pallas_call | solution.py:285
  3.1 4.9 %collective-permute-start = (bf16[136,768]{1,0:T(8,128)(2,1)S(1)}, bf16[136,768]{1,0:T(8,128)(2,1)S(1)}, u32[]{:S(2)}, u32[]{:S(2)}) collective-permute-start(bf16[136,768]{1,0:T(8,128)(2,1)S(1)} %get-tuple-element.13.rest_0_), channel_id=1, source_target_pairs={{0,4},{13,9},{2,6},{15,11},{16,20},{29,25},{18,22},{31,27}} | collective-permute-start | bytes 626696 | tf_op jit(solution)/shard_map/ppermute | solution.py:304
  8.1 0.7 %collective-permute-start.1 = (bf16[136,768]{1,0:T(8,128)(2,1)S(1)}, bf16[136,768]{1,0:T(8,128)(2,1)S(1)}, u32[]{:S(2)}, u32[]{:S(2)}) collective-permute-start(bf16[136,768]{1,0:T(8,128)(2,1)S(1)} %get-tuple-element.14), channel_id=1, source_target_pairs={{1,4},{12,9},{3,6},{14,11},{17,20},{28,25},{19,22},{30,27}} | collective-permute-start | bytes 626696 | tf_op jit(solution)/shard_map/ppermute | solution.py:304
  8.8 0.7 %collective-permute-start.2 = (bf16[136,768]{1,0:T(8,128)(2,1)S(1)}, bf16[136,768]{1,0:T(8,128)(2,1)S(1)}, u32[]{:S(2)}, u32[]{:S(2)}) collective-permute-start(bf16[136,768]{1,0:T(8,128)(2,1)S(1)} %get-tuple-element.13.rest_0_), channel_id=1, source_target_pairs={{12,4},{1,9},{14,6},{3,11},{28,20},{17,25},{30,22},{19,27}} | collective-permute-start | bytes 626696 | tf_op jit(solution)/shard_map/ppermute | solution.py:304
  9.4 3.0 %collective-permute-start.3 = (bf16[136,768]{1,0:T(8,128)(2,1)S(1)}, bf16[136,768]{1,0:T(8,128)(2,1)S(1)}, u32[]{:S(2)}, u32[]{:S(2)}) collective-permute-start(bf16[136,768]{1,0:T(8,128)(2,1)S(1)} %get-tuple-element.14), channel_id=1, source_target_pairs={{13,4},{0,9},{15,6},{2,11},{29,20},{16,25},{31,22},{18,27}} | collective-permute-start | bytes 626696 | tf_op jit(solution)/shard_map/ppermute | solution.py:304
  12.4 0.0 copy-start.2
  12.4 1.6 %collective-permute-start.7 = (bf16[136,768]{1,0:T(8,128)(2,1)S(1)}, bf16[136,768]{1,0:T(8,128)(2,1)S(1)}, u32[]{:S(2)}, u32[]{:S(2)}) collective-permute-start(bf16[136,768]{1,0:T(8,128)(2,1)S(1)} %get-tuple-element.15), channel_id=1, source_target_pairs={{0,2},{1,3},{2,0},{3,1},{4,6},{5,7},{6,4},{7,5},{8,10},{9,11},{10,... | collective-permute-start | bytes 626696 | tf_op jit(solution)/shard_map/ppermute | solution.py:308
  14.0 0.0 collective-permute-done.rest_1_
  14.0 0.7 %collective-permute-start.4 = (bf16[136,768]{1,0:T(8,128)(2,1)S(1)}, bf16[136,768]{1,0:T(8,128)(2,1)S(1)}, u32[]{:S(2)}, u32[]{:S(2)}) collective-permute-start(bf16[136,768]{1,0:T(8,128)(2,1)S(1)} %get-tuple-element.13.rest_0_), channel_id=1, source_target_pairs={{8,4},{5,9},{10,6},{7,11},{24,20},{21,25},{26,22},{23,27}} | collective-permute-start | bytes 626696 | tf_op jit(solution)/shard_map/ppermute | solution.py:304
  14.7 0.0 collective-permute-done.1.rest_2_
  14.7 0.7 %collective-permute-start.5 = (bf16[136,768]{1,0:T(8,128)(2,1)S(1)}, bf16[136,768]{1,0:T(8,128)(2,1)S(1)}, u32[]{:S(2)}, u32[]{:S(2)}) collective-permute-start(bf16[136,768]{1,0:T(8,128)(2,1)S(1)} %get-tuple-element.14), channel_id=1, source_target_pairs={{9,4},{4,9},{11,6},{6,11},{25,20},{20,25},{27,22},{22,27}} | collective-permute-start | bytes 626696 | tf_op jit(solution)/shard_map/ppermute | solution.py:304
  15.4 0.0 collective-permute-done.2.rest_3_
  15.4 4.0 %collective-permute-start.11 = (bf16[136,768]{1,0:T(8,128)(2,1)S(1)}, bf16[136,768]{1,0:T(8,128)(2,1)S(1)}, u32[]{:S(2)}, u32[]{:S(2)}) collective-permute-start(bf16[136,768]{1,0:T(8,128)(2,1)S(1)} %get-tuple-element.16), channel_id=1, source_target_pairs={{0,3},{1,2},{2,1},{3,0},{4,7},{5,6},{6,5},{7,4},{8,11},{9,10},{10,... | collective-permute-start | bytes 626696 | tf_op jit(solution)/shard_map/ppermute | solution.py:308
  19.4 0.0 collective-permute-done.3.rest_4_
  19.4 0.0 collective-permute-start.6
  19.4 0.0 collective-permute-done.7.rest_8_
  19.4 4.6 %collective-permute-start.8 = (bf16[136,768]{1,0:T(8,128)(2,1)S(1)}, bf16[136,768]{1,0:T(8,128)(2,1)S(1)}, u32[]{:S(2)}, u32[]{:S(2)}) collective-permute-start(bf16[136,768]{1,0:T(8,128)(2,1)S(1)} %collective-permute-done.7.rest_8_), channel_id=1, source_target_pairs={{0,4},{13,9},{2,6},{15,11},{16,20},{29,25},{18,22},{31,27}} | collective-permute-start | bytes 626696 | tf_op jit(solution)/shard_map/ppermute | solution.py:304
  24.0 0.0 collective-permute-done.4.rest_5_
  24.0 0.7 %collective-permute-start.9 = (bf16[136,768]{1,0:T(8,128)(2,1)S(1)}, bf16[136,768]{1,0:T(8,128)(2,1)S(1)}, u32[]{:S(2)}, u32[]{:S(2)}) collective-permute-start(bf16[136,768]{1,0:T(8,128)(2,1)S(1)} %collective-permute-done.7.rest_8_), channel_id=1, source_target_pairs={{12,4},{1,9},{14,6},{3,11},{28,20},{17,25},{30,22},{19,27}} | collective-permute-start | bytes 626696 | tf_op jit(solution)/shard_map/ppermute | solution.py:304
  24.7 0.0 collective-permute-done.5.rest_6_
  24.7 0.7 %collective-permute-start.10 = (bf16[136,768]{1,0:T(8,128)(2,1)S(1)}, bf16[136,768]{1,0:T(8,128)(2,1)S(1)}, u32[]{:S(2)}, u32[]{:S(2)}) collective-permute-start(bf16[136,768]{1,0:T(8,128)(2,1)S(1)} %collective-permute-done.7.rest_8_), channel_id=1, source_target_pairs={{8,4},{5,9},{10,6},{7,11},{24,20},{21,25},{26,22},{23,27}} | collective-permute-start | bytes 626696 | tf_op jit(solution)/shard_map/ppermute | solution.py:304
  25.4 0.0 collective-permute-done.11.rest_12_
  25.4 4.4 %collective-permute-start.12 = (bf16[136,768]{1,0:T(8,128)(2,1)S(1)}, bf16[136,768]{1,0:T(8,128)(2,1)S(1)}, u32[]{:S(2)}, u32[]{:S(2)}) collective-permute-start(bf16[136,768]{1,0:T(8,128)(2,1)S(1)} %collective-permute-done.11.rest_12_), channel_id=1, source_target_pairs={{0,4},{13,9},{2,6},{15,11},{16,20},{29,25},{18,22},{31,27}} | collective-permute-start | bytes 626696 | tf_op jit(solution)/shard_map/ppermute | solution.py:304
  29.8 0.0 collective-permute-done.6.rest_7_
  29.8 0.7 %collective-permute-start.13 = (bf16[136,768]{1,0:T(8,128)(2,1)S(1)}, bf16[136,768]{1,0:T(8,128)(2,1)S(1)}, u32[]{:S(2)}, u32[]{:S(2)}) collective-permute-start(bf16[136,768]{1,0:T(8,128)(2,1)S(1)} %collective-permute-done.11.rest_12_), channel_id=1, source_target_pairs={{12,4},{1,9},{14,6},{3,11},{28,20},{17,25},{30,22},{19,27}} | collective-permute-start | bytes 626696 | tf_op jit(solution)/shard_map/ppermute | solution.py:304
  30.5 0.0 collective-permute-done.8.rest_9_
  30.5 0.7 %collective-permute-start.14 = (bf16[136,768]{1,0:T(8,128)(2,1)S(1)}, bf16[136,768]{1,0:T(8,128)(2,1)S(1)}, u32[]{:S(2)}, u32[]{:S(2)}) collective-permute-start(bf16[136,768]{1,0:T(8,128)(2,1)S(1)} %collective-permute-done.11.rest_12_), channel_id=1, source_target_pairs={{8,4},{5,9},{10,6},{7,11},{24,20},{21,25},{26,22},{23,27}} | collective-permute-start | bytes 626696 | tf_op jit(solution)/shard_map/ppermute | solution.py:304
  31.2 0.0 collective-permute-done.9.rest_10_
  31.2 0.0 collective-permute-done.10.rest_11_
  31.2 3.1 %collective-permute-done.12.rest_13_ = bf16[136,768]{1,0:T(8,128)(2,1)S(1)} collective-permute-done((bf16[136,768]{1,0:T(8,128)(2,1)S(1)}, bf16[136,768]{1,0:T(8,128)(2,1)S(1)}, u32[]{:S(2)}, u32[]{:S(2)}) %collective-permute-start.12) | collective-permute-done | bytes 208928 | tf_op jit(solution)/shard_map/ppermute | solution.py:304
  34.3 0.0 collective-permute-done.13.rest_14_
  34.3 0.0 collective-permute-done.14.rest_15_
  34.3 0.0 copy-done.2
  34.3 0.6 %best_at_home.1 = (f32[1,512]{1,0:T(1,128)S(1)}, f32[1,512]{1,0:T(1,128)S(1)}, f32[1,512]{1,0:T(1,128)S(1)}, f32[1,512]{1,0:T(1,128)S(1)}) custom-call(s32[4]{0:T(128)S(1)} %copy-done.2, bf16[136,768]{1,0:T(8,128)(2,1)S(1)} %get-tuple-element.13.rest_0_, bf16[136,768]{1,0:T(8,128)(2,1)S(1)} %collective-permute-done.rest_1_, ...), custom_call_target="tpu_custom_call" | custom-call | tf_op jit(solution)/shard_map/best_at_home/pallas_call | solution.py:322
  34.9 1.3 %collective-permute-start.17 = (f32[1,512]{1,0:T(1,128)S(1)}, f32[1,512]{1,0:T(1,128)S(1)}, u32[]{:S(2)}, u32[]{:S(2)}) collective-permute-start(f32[1,512]{1,0:T(1,128)S(1)} %get-tuple-element.20), channel_id=1, source_target_pairs={{4,0},{9,5},{6,2},{11,7},{20,16},{25,21},{22,18},{27,23}} | collective-permute-start | bytes 6152 | tf_op jit(solution)/shard_map/ppermute | solution.py:337
  36.2 0.7 %collective-permute-start.16 = (f32[1,512]{1,0:T(1,128)S(1)}, f32[1,512]{1,0:T(1,128)S(1)}, u32[]{:S(2)}, u32[]{:S(2)}) collective-permute-start(f32[1,512]{1,0:T(1,128)S(1)} %get-tuple-element.19), channel_id=1, source_target_pairs={{4,12},{9,1},{6,14},{11,3},{20,28},{25,17},{22,30},{27,19}} | collective-permute-start | bytes 6152 | tf_op jit(solution)/shard_map/ppermute | solution.py:337
  36.9 0.7 %collective-permute-start.15 = (f32[1,512]{1,0:T(1,128)S(1)}, f32[1,512]{1,0:T(1,128)S(1)}, u32[]{:S(2)}, u32[]{:S(2)}) collective-permute-start(f32[1,512]{1,0:T(1,128)S(1)} %get-tuple-element.18), channel_id=1, source_target_pairs={{4,8},{9,13},{6,10},{11,15},{20,24},{25,29},{22,26},{27,31}} | collective-permute-start | bytes 6152 | tf_op jit(solution)/shard_map/ppermute | solution.py:337
  37.5 11.3 %collective-permute-done.17 = f32[1,512]{1,0:T(1,128)S(1)} collective-permute-done((f32[1,512]{1,0:T(1,128)S(1)}, f32[1,512]{1,0:T(1,128)S(1)}, u32[]{:S(2)}, u32[]{:S(2)}) %collective-permute-start.17) | collective-permute-done | bytes 2080 | tf_op jit(solution)/shard_map/ppermute | solution.py:337
  48.9 0.0 collective-permute-done.16
  48.9 0.0 collective-permute-done.15
  48.9 0.6 %add_add_fusion = f32[1,512]{1,0:T(1,128)} fusion(f32[1,512]{1,0:T(1,128)S(1)} %collective-permute-done.17, f32[1,512]{1,0:T(1,128)S(1)} %collective-permute-done.16, f32[1,512]{1,0:T(1,128)S(1)} %get-tuple-element.17, f32[1,512]{1,0:T(1,128)S(1)} %collective-permute-done.15), kind=kLoop, calls=%fused_computation | loop fusion | flops 1536 | bytes 10240 | tf_op jit(solution)/shard_map/add | solution.py:337
Async XLA Ops:
  0.0 1.1 %copy-start = (bf16[512,768]{1,0:T(8,128)(2,1)S(1)}, bf16[512,768]{1,0:T(8,128)(2,1)}, u32[]{:S(2)}) copy-start(bf16[512,768]{1,0:T(8,128)(2,1)} %rows_ref.1) | copy-start | bytes 2359300
  1.1 0.7 %copy-start.1 = (s32[512]{0:T(512)S(1)}, s32[512]{0:T(512)}, u32[]{:S(2)}) copy-start(s32[512]{0:T(512)} %param.4) | copy-start | bytes 6148
  3.1 10.9 %collective-permute-start = (bf16[136,768]{1,0:T(8,128)(2,1)S(1)}, bf16[136,768]{1,0:T(8,128)(2,1)S(1)}, u32[]{:S(2)}, u32[]{:S(2)}) collective-permute-start(bf16[136,768]{1,0:T(8,128)(2,1)S(1)} %get-tuple-element.13.rest_0_), channel_id=1, source_target_pairs={{0,4},{13,9},{2,6},{15,11},{16,20},{29,25},{18,22},{31,27}} | collective-permute-start | bytes 626696 | tf_op jit(solution)/shard_map/ppermute | solution.py:304
  8.1 6.6 %collective-permute-start.1 = (bf16[136,768]{1,0:T(8,128)(2,1)S(1)}, bf16[136,768]{1,0:T(8,128)(2,1)S(1)}, u32[]{:S(2)}, u32[]{:S(2)}) collective-permute-start(bf16[136,768]{1,0:T(8,128)(2,1)S(1)} %get-tuple-element.14), channel_id=1, source_target_pairs={{1,4},{12,9},{3,6},{14,11},{17,20},{28,25},{19,22},{30,27}} | collective-permute-start | bytes 626696 | tf_op jit(solution)/shard_map/ppermute | solution.py:304
  8.8 6.6 %collective-permute-start.2 = (bf16[136,768]{1,0:T(8,128)(2,1)S(1)}, bf16[136,768]{1,0:T(8,128)(2,1)S(1)}, u32[]{:S(2)}, u32[]{:S(2)}) collective-permute-start(bf16[136,768]{1,0:T(8,128)(2,1)S(1)} %get-tuple-element.13.rest_0_), channel_id=1, source_target_pairs={{12,4},{1,9},{14,6},{3,11},{28,20},{17,25},{30,22},{19,27}} | collective-permute-start | bytes 626696 | tf_op jit(solution)/shard_map/ppermute | solution.py:304
  9.4 10.0 %collective-permute-start.3 = (bf16[136,768]{1,0:T(8,128)(2,1)S(1)}, bf16[136,768]{1,0:T(8,128)(2,1)S(1)}, u32[]{:S(2)}, u32[]{:S(2)}) collective-permute-start(bf16[136,768]{1,0:T(8,128)(2,1)S(1)} %get-tuple-element.14), channel_id=1, source_target_pairs={{13,4},{0,9},{15,6},{2,11},{29,20},{16,25},{31,22},{18,27}} | collective-permute-start | bytes 626696 | tf_op jit(solution)/shard_map/ppermute | solution.py:304
  12.4 21.9 %copy-start.2 = (s32[4]{0:T(128)S(1)}, s32[4]{0:T(128)}, u32[]{:S(2)}) copy-start(s32[4]{0:T(128)} %sizes_ref.1) | copy-start | bytes 52
  12.4 7.0 %collective-permute-start.7 = (bf16[136,768]{1,0:T(8,128)(2,1)S(1)}, bf16[136,768]{1,0:T(8,128)(2,1)S(1)}, u32[]{:S(2)}, u32[]{:S(2)}) collective-permute-start(bf16[136,768]{1,0:T(8,128)(2,1)S(1)} %get-tuple-element.15), channel_id=1, source_target_pairs={{0,2},{1,3},{2,0},{3,1},{4,6},{5,7},{6,4},{7,5},{8,10},{9,11},{10,... | collective-permute-start | bytes 626696 | tf_op jit(solution)/shard_map/ppermute | solution.py:308
  14.0 10.0 %collective-permute-start.4 = (bf16[136,768]{1,0:T(8,128)(2,1)S(1)}, bf16[136,768]{1,0:T(8,128)(2,1)S(1)}, u32[]{:S(2)}, u32[]{:S(2)}) collective-permute-start(bf16[136,768]{1,0:T(8,128)(2,1)S(1)} %get-tuple-element.13.rest_0_), channel_id=1, source_target_pairs={{8,4},{5,9},{10,6},{7,11},{24,20},{21,25},{26,22},{23,27}} | collective-permute-start | bytes 626696 | tf_op jit(solution)/shard_map/ppermute | solution.py:304
  14.7 10.0 %collective-permute-start.5 = (bf16[136,768]{1,0:T(8,128)(2,1)S(1)}, bf16[136,768]{1,0:T(8,128)(2,1)S(1)}, u32[]{:S(2)}, u32[]{:S(2)}) collective-permute-start(bf16[136,768]{1,0:T(8,128)(2,1)S(1)} %get-tuple-element.14), channel_id=1, source_target_pairs={{9,4},{4,9},{11,6},{6,11},{25,20},{20,25},{27,22},{22,27}} | collective-permute-start | bytes 626696 | tf_op jit(solution)/shard_map/ppermute | solution.py:304
  15.4 10.0 %collective-permute-start.11 = (bf16[136,768]{1,0:T(8,128)(2,1)S(1)}, bf16[136,768]{1,0:T(8,128)(2,1)S(1)}, u32[]{:S(2)}, u32[]{:S(2)}) collective-permute-start(bf16[136,768]{1,0:T(8,128)(2,1)S(1)} %get-tuple-element.16), channel_id=1, source_target_pairs={{0,3},{1,2},{2,1},{3,0},{4,7},{5,6},{6,5},{7,4},{8,11},{9,10},{10,... | collective-permute-start | bytes 626696 | tf_op jit(solution)/shard_map/ppermute | solution.py:308
  19.4 10.4 %collective-permute-start.6 = (bf16[136,768]{1,0:T(8,128)(2,1)S(1)}, bf16[136,768]{1,0:T(8,128)(2,1)S(1)}, u32[]{:S(2)}, u32[]{:S(2)}) collective-permute-start(bf16[136,768]{1,0:T(8,128)(2,1)S(1)} %get-tuple-element.14), channel_id=1, source_target_pairs={{0,1},{1,0},{2,3},{3,2},{4,5},{5,4},{6,7},{7,6},{8,9},{9,8},{10,11... | collective-permute-start | bytes 626696 | tf_op jit(solution)/shard_map/ppermute | solution.py:308
  19.4 11.1 %collective-permute-start.8 = (bf16[136,768]{1,0:T(8,128)(2,1)S(1)}, bf16[136,768]{1,0:T(8,128)(2,1)S(1)}, u32[]{:S(2)}, u32[]{:S(2)}) collective-permute-start(bf16[136,768]{1,0:T(8,128)(2,1)S(1)} %collective-permute-done.7.rest_8_), channel_id=1, source_target_pairs={{0,4},{13,9},{2,6},{15,11},{16,20},{29,25},{18,22},{31,27}} | collective-permute-start | bytes 626696 | tf_op jit(solution)/shard_map/ppermute | solution.py:304
  24.0 7.2 %collective-permute-start.9 = (bf16[136,768]{1,0:T(8,128)(2,1)S(1)}, bf16[136,768]{1,0:T(8,128)(2,1)S(1)}, u32[]{:S(2)}, u32[]{:S(2)}) collective-permute-start(bf16[136,768]{1,0:T(8,128)(2,1)S(1)} %collective-permute-done.7.rest_8_), channel_id=1, source_target_pairs={{12,4},{1,9},{14,6},{3,11},{28,20},{17,25},{30,22},{19,27}} | collective-permute-start | bytes 626696 | tf_op jit(solution)/shard_map/ppermute | solution.py:304
  24.7 6.5 %collective-permute-start.10 = (bf16[136,768]{1,0:T(8,128)(2,1)S(1)}, bf16[136,768]{1,0:T(8,128)(2,1)S(1)}, u32[]{:S(2)}, u32[]{:S(2)}) collective-permute-start(bf16[136,768]{1,0:T(8,128)(2,1)S(1)} %collective-permute-done.7.rest_8_), channel_id=1, source_target_pairs={{8,4},{5,9},{10,6},{7,11},{24,20},{21,25},{26,22},{23,27}} | collective-permute-start | bytes 626696 | tf_op jit(solution)/shard_map/ppermute | solution.py:304
  25.4 8.9 %collective-permute-start.12 = (bf16[136,768]{1,0:T(8,128)(2,1)S(1)}, bf16[136,768]{1,0:T(8,128)(2,1)S(1)}, u32[]{:S(2)}, u32[]{:S(2)}) collective-permute-start(bf16[136,768]{1,0:T(8,128)(2,1)S(1)} %collective-permute-done.11.rest_12_), channel_id=1, source_target_pairs={{0,4},{13,9},{2,6},{15,11},{16,20},{29,25},{18,22},{31,27}} | collective-permute-start | bytes 626696 | tf_op jit(solution)/shard_map/ppermute | solution.py:304
  29.8 4.5 %collective-permute-start.13 = (bf16[136,768]{1,0:T(8,128)(2,1)S(1)}, bf16[136,768]{1,0:T(8,128)(2,1)S(1)}, u32[]{:S(2)}, u32[]{:S(2)}) collective-permute-start(bf16[136,768]{1,0:T(8,128)(2,1)S(1)} %collective-permute-done.11.rest_12_), channel_id=1, source_target_pairs={{12,4},{1,9},{14,6},{3,11},{28,20},{17,25},{30,22},{19,27}} | collective-permute-start | bytes 626696 | tf_op jit(solution)/shard_map/ppermute | solution.py:304
  30.5 3.8 %collective-permute-start.14 = (bf16[136,768]{1,0:T(8,128)(2,1)S(1)}, bf16[136,768]{1,0:T(8,128)(2,1)S(1)}, u32[]{:S(2)}, u32[]{:S(2)}) collective-permute-start(bf16[136,768]{1,0:T(8,128)(2,1)S(1)} %collective-permute-done.11.rest_12_), channel_id=1, source_target_pairs={{8,4},{5,9},{10,6},{7,11},{24,20},{21,25},{26,22},{23,27}} | collective-permute-start | bytes 626696 | tf_op jit(solution)/shard_map/ppermute | solution.py:304
  34.9 14.0 %collective-permute-start.17 = (f32[1,512]{1,0:T(1,128)S(1)}, f32[1,512]{1,0:T(1,128)S(1)}, u32[]{:S(2)}, u32[]{:S(2)}) collective-permute-start(f32[1,512]{1,0:T(1,128)S(1)} %get-tuple-element.20), channel_id=1, source_target_pairs={{4,0},{9,5},{6,2},{11,7},{20,16},{25,21},{22,18},{27,23}} | collective-permute-start | bytes 6152 | tf_op jit(solution)/shard_map/ppermute | solution.py:337
  36.2 12.7 %collective-permute-start.16 = (f32[1,512]{1,0:T(1,128)S(1)}, f32[1,512]{1,0:T(1,128)S(1)}, u32[]{:S(2)}, u32[]{:S(2)}) collective-permute-start(f32[1,512]{1,0:T(1,128)S(1)} %get-tuple-element.19), channel_id=1, source_target_pairs={{4,12},{9,1},{6,14},{11,3},{20,28},{25,17},{22,30},{27,19}} | collective-permute-start | bytes 6152 | tf_op jit(solution)/shard_map/ppermute | solution.py:337
  36.9 12.0 %collective-permute-start.15 = (f32[1,512]{1,0:T(1,128)S(1)}, f32[1,512]{1,0:T(1,128)S(1)}, u32[]{:S(2)}, u32[]{:S(2)}) collective-permute-start(f32[1,512]{1,0:T(1,128)S(1)} %get-tuple-element.18), channel_id=1, source_target_pairs={{4,8},{9,13},{6,10},{11,15},{20,24},{25,29},{22,26},{27,31}} | collective-permute-start | bytes 6152 | tf_op jit(solution)/shard_map/ppermute | solution.py:337

commit v3 on v1

--- a/solution.py
+++ b/solution.py
@@ -10,6 +10,11 @@
 PIECE = 16
 VMEM = pl.BlockSpec(memory_space=pltpu.VMEM)
 SMEM = pl.BlockSpec(memory_space=pltpu.SMEM)
+HBM = pl.BlockSpec(memory_space=pltpu.HBM)
+
+
+def as_bf16(mask):
+    return mask.astype(jnp.float32).astype(jnp.bfloat16)
 
 
 def sort_kernel(run_slots, dest_ref, rows_ref, units_ref, slots_ref):
@@ -94,7 +99,7 @@
     out_ref[...] = jnp.where(position < members, found, 0.0)
 
 
-def local(embeddings, dest, sizes):
+def local_plane(embeddings, dest, sizes):
     chain_len = lax.axis_size("chain")
     clus_len = lax.axis_size("clus")
     shards = chain_len * clus_len
@@ -160,9 +165,198 @@
     return lax.ppermute(found, ("chain", "clus"), pairs)
 
 
+def send_kernel(run_slots, cluster_runs, dest_hbm, rows_hbm, *rest):
+    block_refs, (dest_ref, rows_ref, sems) = rest[:-3], rest[-3:]
+    dest_copy = pltpu.make_async_copy(dest_hbm, dest_ref, sems.at[0])
+    rows_copy = pltpu.make_async_copy(rows_hbm, rows_ref, sems.at[1])
+    dest_copy.start()
+    rows_copy.start()
+    rows, width = rows_ref.shape
+    runs = rows // PIECE
+    depth = rows // len(block_refs)
+    upper = lax.axis_index("chain") >= lax.axis_size("chain") // 2
+    code = lax.axis_index("clus") // 2 * 2 + upper.astype(jnp.int32)
+    before = lax.broadcasted_iota(jnp.int32, (rows, rows), 0) < lax.broadcasted_iota(
+        jnp.int32, (rows, rows), 1
+    )
+    dest_copy.wait()
+    dest = dest_ref[...]
+    run = lax.div(dest, run_slots)
+    within = lax.rem(dest, run_slots)
+    run = (lax.div(run, cluster_runs) ^ code) * cluster_runs + lax.rem(run, cluster_runs)
+    member = lax.broadcasted_iota(jnp.int32, (runs, rows), 0) == run
+    earlier = jnp.dot(as_bf16(member), as_bf16(before), preferred_element_type=jnp.float32)
+    rank = jnp.sum(jnp.where(member, earlier, 0.0), axis=0, keepdims=True).astype(jnp.int32)
+    hot = as_bf16(lax.broadcasted_iota(jnp.int32, (rows, rows), 0) == run * PIECE + rank)
+    moved = lax.dot_general(
+        jnp.broadcast_to(within, (8, rows)).astype(jnp.float32).astype(jnp.bfloat16),
+        hot,
+        (((1,), (1,)), ((), ())),
+        preferred_element_type=jnp.float32,
+    ).astype(jnp.bfloat16)
+    rows_copy.wait()
+    x = rows_ref[...].astype(jnp.float32)
+    units = (x * lax.rsqrt(jnp.sum(x * x, axis=1, keepdims=True) + 1e-06)).astype(jnp.bfloat16)
+    for index, block_ref in enumerate(block_refs):
+        low = index * depth
+        block_ref[0:depth, :] = jnp.dot(
+            hot[low : low + depth], units, preferred_element_type=jnp.float32
+        ).astype(jnp.bfloat16)
+        block_ref[depth : depth + 8, :] = jnp.zeros((8, width), jnp.bfloat16)
+        block_ref[depth : depth + 8, 0:depth] = moved[:, low : low + depth]
+
+
+def home_kernel(height, sizes_ref, *rest):
+    refs, (first_ref, second_ref, keys_ref) = rest[:-3], rest[-3:]
+    blocks = []
+    for ref in refs:
+        blocks += [(ref, low) for low in range(0, ref.shape[0], height)]
+    count = len(blocks)
+    run_slots = count * PIECE
+    depth = height - 8
+    runs = depth // PIECE
+    chunk = first_ref.shape[1]
+    chunk_runs = chunk // run_slots
+    clus = lax.axis_index("clus")
+    chain = lax.axis_index("chain")
+    half = lax.axis_size("chain") // 2
+    is_home = jnp.logical_or(chain == half - 1, chain == half)
+    members = sizes_ref[clus // 2 * 2 + (chain >= half).astype(jnp.int32)]
+
+    @pl.when(jnp.logical_not(is_home))
+    def _():
+        first_ref[...] = jnp.zeros_like(first_ref)
+        second_ref[...] = jnp.zeros_like(second_ref)
+
+    @pl.when(is_home)
+    def _():
+        for index, (ref, low) in enumerate(blocks):
+            for run in range(runs):
+                at = run * run_slots + index * PIECE
+                keys_ref[at : at + PIECE, :] = ref[low + run * PIECE : low + (run + 1) * PIECE, :]
+
+    def answer(wanted, out_ref):
+        slots = jnp.concatenate(
+            [ref[low + depth : low + depth + 8, 0:depth][0:1] for ref, low in blocks], axis=0
+        )
+        block_of = lax.broadcasted_iota(jnp.int32, (run_slots, count), 0) // PIECE
+        mine = block_of == lax.broadcasted_iota(jnp.int32, (run_slots, count), 1)
+        in_block = lax.broadcasted_iota(jnp.int32, (run_slots, depth), 0) % PIECE
+        lane = lax.broadcasted_iota(jnp.int32, (run_slots, depth), 1)
+        query_at = lax.broadcasted_iota(jnp.int32, (run_slots, run_slots), 1)
+        for index in range(chunk_runs):
+            run = wanted * chunk_runs + index
+            base = run * run_slots
+            spread = lax.dot_general(
+                as_bf16(lane == in_block + run * PIECE),
+                slots,
+                (((1,), (1,)), ((), ())),
+                preferred_element_type=jnp.float32,
+            )
+            slot = jnp.sum(jnp.where(mine, spread, 0.0), axis=1, keepdims=True).astype(jnp.int32)
+            queries = lax.dot_general(
+                keys_ref[base : base + run_slots, :],
+                as_bf16(slot == query_at),
+                (((0,), (0,)), ((), ())),
+                preferred_element_type=jnp.float32,
+            ).astype(jnp.bfloat16)
+            scores = jnp.dot(
+                keys_ref[0 : base + run_slots, :], queries, preferred_element_type=jnp.float32
+            )
+            best = jnp.where(slot < query_at, scores[base:], -2.0)
+            best = jnp.max(best.reshape(run_slots // 8, 8, run_slots), axis=0)
+            if run:
+                best = jnp.maximum(best, jnp.max(scores[:base].reshape(base // 8, 8, run_slots), axis=0))
+            best = jnp.maximum(jnp.max(best, axis=0, keepdims=True), -1.0)
+            position = base + lax.broadcasted_iota(jnp.int32, (1, run_slots), 1)
+            out_ref[:, index * run_slots : (index + 1) * run_slots] = jnp.where(
+                position < members, best, 0.0
+            )
+
+    for core in range(2):
+        @pl.when(jnp.logical_and(is_home, clus % 2 == core))
+        def _():
+            answer(core, first_ref)
+            answer(2 * half - 1 - core, second_ref)
+
+
+def local_home(embeddings, dest, sizes):
+    chain_len = lax.axis_size("chain")
+    clus_len = lax.axis_size("clus")
+    rows, width = embeddings.shape
+    run_slots = chain_len * clus_len * PIECE
+    depth = rows // clus_len
+    height = depth + 8
+    block = jax.ShapeDtypeStruct((height, width), jnp.bfloat16)
+    blocks = pl.pallas_call(
+        functools.partial(send_kernel, run_slots, depth // PIECE),
+        out_shape=(block,) * clus_len,
+        in_specs=[HBM, HBM],
+        out_specs=(VMEM,) * clus_len,
+        scratch_shapes=[
+            pltpu.VMEM((1, rows), jnp.int32),
+            pltpu.VMEM((rows, width), jnp.bfloat16),
+            pltpu.SemaphoreType.DMA((2,)),
+        ],
+        compiler_params=pltpu.CompilerParams(vmem_limit_bytes=58 * 2**20),
+        name="send_blocks",
+    )(dest.reshape(1, rows), embeddings)
+
+    def permute(value, moves):
+        pairs = [(a * clus_len + b, c * clus_len + d) for a, b, c, d in moves]
+        return lax.ppermute(value, ("chain", "clus"), pairs)
+
+    def to_home(value, moves, flip):
+        return permute(value, [(a, k, b, k ^ flip) for a, b in moves for k in range(clus_len)])
+
+    low, high, top = chain_len // 2 - 1, chain_len // 2, chain_len - 1
+    near = [(0, low), (top, high)]
+    far = [(0, high), (top, low)]
+    middle = [(low, high), (high, low)]
+    stay = [(low, low), (high, high)]
+
+    def swap(values):
+        value = jnp.concatenate(values, axis=0)
+        return permute(value, [(z, k, z, k ^ 1) for z in (low, high) for k in range(clus_len)])
+
+    far_across = to_home(blocks[3], far, 2)
+    far_along = to_home(blocks[1], far, 0)
+    stay_across = to_home(blocks[2], stay, 2)
+    near_across = to_home(blocks[2], near, 2)
+    middle_across = to_home(blocks[3], middle, 2)
+    near_along = to_home(blocks[0], near, 0)
+    middle_along = to_home(blocks[1], middle, 0)
+    batches = [
+        [blocks[0], stay_across, far_across],
+        [far_along, near_across, middle_across],
+        [near_along, middle_along],
+    ]
+    keys = []
+    for batch in batches:
+        keys.append(swap(batch))
+        keys += batch
+
+    answers = pl.pallas_call(
+        functools.partial(home_kernel, height),
+        out_shape=(jax.ShapeDtypeStruct((1, rows), jnp.float32),) * 2,
+        in_specs=[SMEM] + [VMEM] * len(keys),
+        out_specs=(VMEM, VMEM),
+        scratch_shapes=[pltpu.VMEM((chain_len * rows, width), jnp.bfloat16)],
+        compiler_params=pltpu.CompilerParams(vmem_limit_bytes=40 * 2**20),
+        name="best_at_home",
+    )(sizes, *keys)
+    moves = [[], []]
+    for k in range(clus_len):
+        for core in range(2):
+            source = (low + k % 2, k // 2 * 2 + core)
+            moves[0].append(source + (core, k))
+            moves[1].append(source + (top - core, k))
+    return permute(answers[0], moves[0]) + permute(answers[1], moves[1])
+
+
 def solution(mesh):
     return jax.shard_map(
-        local,
+        local_home if mesh.shape["chain"] == mesh.shape["clus"] == 4 else local_plane,
         mesh=mesh,
         in_specs=(
             P(("groups", "chain", "clus"), None),

time: 82.7 us -> 47.9 us (0.58)
  the two profiles are of different devices: /device:TPU:7 before, /device:TPU:0 now
where the time goes in v3:
time: 47.9 us; the launch traced here: 47.5 us
  starting transfers between devices  26.4 us (55%)
  waiting for transfers between devices  16.9 us (35%)
  Pallas kernels  3.33 us (7%)
  other arithmetic  0.7 us (1%)
    ppermute x12, starting transfers between devices, permute(): return lax.ppermute(value, ('chain', 'clus'), pairs)  26.4 us
    ppermute x12, waiting for transfers between devices, permute(): return lax.ppermute(value, ('chain', 'clus'), pairs)  16.9 us
    pallas_call x1, Pallas kernels, local_home(): pl.pallas_call(functools.partial(send_kernel, run_slots, depth // PIECE),...  2.75 us
  transfers between devices with their start and end apart: 12, of which 3 were waited for; matrix products, arithmetic and copies ran while one was open for 0% of the time, Pallas kernels for 0%

profile of v3, /device:TPU:0, one launch (start us, length us, event | category | flops | bytes accessed | tf_op | source)
XLA Modules:
  0.0 47.5 jit_solution(9908253091475865073)
XLA Ops:
  0.0 2.7 %send_blocks.1 = (bf16[136,768]{1,0:T(8,128)(2,1)}, bf16[136,768]{1,0:T(8,128)(2,1)}, bf16[136,768]{1,0:T(8,128)(2,1)}, bf16[136,768]{1,0:T(8,128)(2,1)}) custom-call(s32[1,512]{1,0:T(1,128)} %bitcast.1, bf16[512,768]{1,0:T(8,128)(2,1)} %rows_hbm.1), custom_call_target="tpu_custom_call" | custom-call | tf_op jit(solution)/shard_map/send_blocks/pallas_call | solution.py:291
  2.8 0.0 copy-start
  2.8 6.1 %collective-permute-start.3 = (bf16[136,768]{1,0:T(8,128)(2,1)}, bf16[136,768]{1,0:T(8,128)(2,1)S(1)}, u32[]{:S(2)}, u32[]{:S(2)}) collective-permute-start(bf16[136,768]{1,0:T(8,128)(2,1)} %get-tuple-element.14), channel_id=1, source_target_pairs={{0,8},{1,9},{2,10},{3,11},{12,4},{13,5},{14,6},{15,7},{16,24},{17,... | collective-permute-start | bytes 626696 | tf_op jit(solution)/shard_map/ppermute | solution.py:307
  8.9 1.3 %collective-permute-start.4 = (bf16[136,768]{1,0:T(8,128)(2,1)}, bf16[136,768]{1,0:T(8,128)(2,1)S(1)}, u32[]{:S(2)}, u32[]{:S(2)}) collective-permute-start(bf16[136,768]{1,0:T(8,128)(2,1)} %get-tuple-element.12), channel_id=1, source_target_pairs={{0,6},{1,7},{2,4},{3,5},{12,10},{13,11},{14,8},{15,9},{16,22},{17,... | collective-permute-start | bytes 626696 | tf_op jit(solution)/shard_map/ppermute | solution.py:307
  10.2 0.7 %collective-permute-start.5 = (bf16[136,768]{1,0:T(8,128)(2,1)}, bf16[136,768]{1,0:T(8,128)(2,1)S(1)}, u32[]{:S(2)}, u32[]{:S(2)}) collective-permute-start(bf16[136,768]{1,0:T(8,128)(2,1)} %get-tuple-element.13), channel_id=1, source_target_pairs={{4,10},{5,11},{6,8},{7,9},{8,6},{9,7},{10,4},{11,5},{20,26},{21,27... | collective-permute-start | bytes 626696 | tf_op jit(solution)/shard_map/ppermute | solution.py:307
  10.8 0.7 %collective-permute-start = (bf16[136,768]{1,0:T(8,128)(2,1)}, bf16[136,768]{1,0:T(8,128)(2,1)S(1)}, u32[]{:S(2)}, u32[]{:S(2)}) collective-permute-start(bf16[136,768]{1,0:T(8,128)(2,1)} %get-tuple-element.12), channel_id=1, source_target_pairs={{4,6},{5,7},{6,4},{7,5},{8,10},{9,11},{10,8},{11,9},{20,22},{21,23... | collective-permute-start | bytes 626696 | tf_op jit(solution)/shard_map/ppermute | solution.py:307
  11.5 6.6 %collective-permute-start.1 = (bf16[136,768]{1,0:T(8,128)(2,1)}, bf16[136,768]{1,0:T(8,128)(2,1)S(1)}, u32[]{:S(2)}, u32[]{:S(2)}) collective-permute-start(bf16[136,768]{1,0:T(8,128)(2,1)} %get-tuple-element.13), channel_id=1, source_target_pairs={{0,10},{1,11},{2,8},{3,9},{12,6},{13,7},{14,4},{15,5},{16,26},{17,... | collective-permute-start | bytes 626696 | tf_op jit(solution)/shard_map/ppermute | solution.py:307
  18.1 0.0 collective-permute-done.3.rest_5_
  18.1 0.7 %collective-permute-start.8 = (bf16[136,768]{1,0:T(8,128)(2,1)}, bf16[136,768]{1,0:T(8,128)(2,1)S(1)}, u32[]{:S(2)}, u32[]{:S(2)}) collective-permute-start(bf16[136,768]{1,0:T(8,128)(2,1)} %get-tuple-element.14), channel_id=1, source_target_pairs={{4,8},{5,9},{6,10},{7,11},{8,4},{9,5},{10,6},{11,7},{20,24},{21,25... | collective-permute-start | bytes 626696 | tf_op jit(solution)/shard_map/ppermute | solution.py:307
  18.8 1.7 %collective-permute-done.4.rest_6_ = bf16[136,768]{1,0:T(8,128)(2,1)S(1)} collective-permute-done((bf16[136,768]{1,0:T(8,128)(2,1)}, bf16[136,768]{1,0:T(8,128)(2,1)S(1)}, u32[]{:S(2)}, u32[]{:S(2)}) %collective-permute-start.4) | collective-permute-done | bytes 208928 | tf_op jit(solution)/shard_map/ppermute | solution.py:307
  20.5 6.4 %collective-permute-start.7 = (bf16[136,768]{1,0:T(8,128)(2,1)}, bf16[136,768]{1,0:T(8,128)(2,1)S(1)}, u32[]{:S(2)}, u32[]{:S(2)}) collective-permute-start(bf16[136,768]{1,0:T(8,128)(2,1)} %get-tuple-element.11.rest_1_), channel_id=1, source_target_pairs={{0,4},{1,5},{2,6},{3,7},{12,8},{13,9},{14,10},{15,11},{16,20},{17,... | collective-permute-start | bytes 626696 | tf_op jit(solution)/shard_map/ppermute | solution.py:307
  26.9 0.0 collective-permute-done.5.rest_7_
  26.9 0.0 copy-start.1
  27.0 0.7 %collective-permute-start.6 = (bf16[408,768]{1,0:T(8,128)(2,1)S(1)}, bf16[408,768]{1,0:T(8,128)(2,1)S(1)}, u32[]{:S(2)}, u32[]{:S(2)}) collective-permute-start(bf16[408,768]{1,0:T(8,128)(2,1)S(1)} %pad_maximum_fusion.1), channel_id=1, source_target_pairs={{4,5},{5,4},{6,7},{7,6},{8,9},{9,8},{10,11},{11,10},{20,21},{21,20... | collective-permute-start | bytes 1880072 | tf_op jit(solution)/shard_map/ppermute | solution.py:307
  27.7 0.0 collective-permute-done.rest_2_
  27.7 0.0 collective-permute-done.1.rest_3_
  27.7 0.0 copy-done
  27.8 0.7 %collective-permute-start.2 = (bf16[408,768]{1,0:T(8,128)(2,1)S(1)}, bf16[408,768]{1,0:T(8,128)(2,1)S(1)}, u32[]{:S(2)}, u32[]{:S(2)}) collective-permute-start(bf16[408,768]{1,0:T(8,128)(2,1)S(1)} %pad_maximum_fusion), channel_id=1, source_target_pairs={{4,5},{5,4},{6,7},{7,6},{8,9},{9,8},{10,11},{11,10},{20,21},{21,20... | collective-permute-start | bytes 1880072 | tf_op jit(solution)/shard_map/ppermute | solution.py:307
  28.5 2.0 %collective-permute-done.7.rest_9_ = bf16[136,768]{1,0:T(8,128)(2,1)S(1)} collective-permute-done((bf16[136,768]{1,0:T(8,128)(2,1)}, bf16[136,768]{1,0:T(8,128)(2,1)S(1)}, u32[]{:S(2)}, u32[]{:S(2)}) %collective-permute-start.7) | collective-permute-done | bytes 208928 | tf_op jit(solution)/shard_map/ppermute | solution.py:307
  30.5 0.0 collective-permute-done.8.rest_10_
  30.5 0.7 %collective-permute-start.9 = (bf16[272,768]{1,0:T(8,128)(2,1)S(1)}, bf16[272,768]{1,0:T(8,128)(2,1)S(1)}, u32[]{:S(2)}, u32[]{:S(2)}) collective-permute-start(bf16[272,768]{1,0:T(8,128)(2,1)S(1)} %pad_maximum_fusion.2), channel_id=1, source_target_pairs={{4,5},{5,4},{6,7},{7,6},{8,9},{9,8},{10,11},{11,10},{20,21},{21,20... | collective-permute-start | bytes 1253384 | tf_op jit(solution)/shard_map/ppermute | solution.py:307
  31.2 0.0 collective-permute-done.9.rest_8_
  31.2 0.0 collective-permute-done.6.rest_4_
  31.2 0.0 collective-permute-done.2.rest_0_
  31.3 0.0 copy-done.1
  31.3 0.6 %best_at_home.1 = (f32[1,512]{1,0:T(1,128)S(1)}, f32[1,512]{1,0:T(1,128)S(1)}) custom-call(s32[4]{0:T(128)S(1)} %copy-done.1, bf16[408,768]{1,0:T(8,128)(2,1)S(1)} %collective-permute-done.2.rest_0_, bf16[136,768]{1,0:T(8,128)(2,1)S(1)} %copy-done, bf16[136,768]{1,0:T(8,128)(2,1)S(1)} %collective-permute-done.rest_2_, ...), custom_call_target="tpu_custom_call" | custom-call | tf_op jit(solution)/shard_map/best_at_home/pallas_call | solution.py:339
  31.8 1.3 %collective-permute-start.10 = (f32[1,512]{1,0:T(1,128)S(1)}, f32[1,512]{1,0:T(1,128)S(1)}, u32[]{:S(2)}, u32[]{:S(2)}) collective-permute-start(f32[1,512]{1,0:T(1,128)S(1)} %get-tuple-element.15), channel_id=1, source_target_pairs={{4,0},{5,4},{8,1},{9,5},{6,2},{7,6},{10,3},{11,7},{20,16},{21,20},... | collective-permute-start | bytes 6152 | tf_op jit(solution)/shard_map/ppermute | solution.py:307
  33.1 0.7 %collective-permute-start.11 = (f32[1,512]{1,0:T(1,128)S(1)}, f32[1,512]{1,0:T(1,128)S(1)}, u32[]{:S(2)}, u32[]{:S(2)}) collective-permute-start(f32[1,512]{1,0:T(1,128)S(1)} %get-tuple-element.16), channel_id=1, source_target_pairs={{4,12},{5,8},{8,13},{9,9},{6,14},{7,10},{10,15},{11,11},{20,28},{2... | collective-permute-start | bytes 6152 | tf_op jit(solution)/shard_map/ppermute | solution.py:307
  33.8 13.1 %collective-permute-done.10 = f32[1,512]{1,0:T(1,128)S(1)} collective-permute-done((f32[1,512]{1,0:T(1,128)S(1)}, f32[1,512]{1,0:T(1,128)S(1)}, u32[]{:S(2)}, u32[]{:S(2)}) %collective-permute-start.10) | collective-permute-done | bytes 2080 | tf_op jit(solution)/shard_map/ppermute | solution.py:307
  47.0 0.0 collective-permute-done.11
  47.0 0.6 %add.3 = f32[1,512]{1,0:T(1,128)} add(f32[1,512]{1,0:T(1,128)S(1)} %collective-permute-done.10, f32[1,512]{1,0:T(1,128)S(1)} %collective-permute-done.11) | non-fusion elementwise | flops 512 | bytes 6144 | tf_op jit(solution)/shard_map/add | solution.py:354
  (3 shorter events, 0.1 us)
Async XLA Ops:
  2.8 24.9 %copy-start = (bf16[136,768]{1,0:T(8,128)(2,1)S(1)}, bf16[136,768]{1,0:T(8,128)(2,1)}, u32[]{:S(2)}) copy-start(bf16[136,768]{1,0:T(8,128)(2,1)} %get-tuple-element.11.rest_1_) | copy-start | bytes 626692
  2.8 15.4 %collective-permute-start.3 = (bf16[136,768]{1,0:T(8,128)(2,1)}, bf16[136,768]{1,0:T(8,128)(2,1)S(1)}, u32[]{:S(2)}, u32[]{:S(2)}) collective-permute-start(bf16[136,768]{1,0:T(8,128)(2,1)} %get-tuple-element.14), channel_id=1, source_target_pairs={{0,8},{1,9},{2,10},{3,11},{12,4},{13,5},{14,6},{15,7},{16,24},{17,... | collective-permute-start | bytes 626696 | tf_op jit(solution)/shard_map/ppermute | solution.py:307
  8.9 11.7 %collective-permute-start.4 = (bf16[136,768]{1,0:T(8,128)(2,1)}, bf16[136,768]{1,0:T(8,128)(2,1)S(1)}, u32[]{:S(2)}, u32[]{:S(2)}) collective-permute-start(bf16[136,768]{1,0:T(8,128)(2,1)} %get-tuple-element.12), channel_id=1, source_target_pairs={{0,6},{1,7},{2,4},{3,5},{12,10},{13,11},{14,8},{15,9},{16,22},{17,... | collective-permute-start | bytes 626696 | tf_op jit(solution)/shard_map/ppermute | solution.py:307
  10.2 16.7 %collective-permute-start.5 = (bf16[136,768]{1,0:T(8,128)(2,1)}, bf16[136,768]{1,0:T(8,128)(2,1)S(1)}, u32[]{:S(2)}, u32[]{:S(2)}) collective-permute-start(bf16[136,768]{1,0:T(8,128)(2,1)} %get-tuple-element.13), channel_id=1, source_target_pairs={{4,10},{5,11},{6,8},{7,9},{8,6},{9,7},{10,4},{11,5},{20,26},{21,27... | collective-permute-start | bytes 626696 | tf_op jit(solution)/shard_map/ppermute | solution.py:307
  10.8 16.8 %collective-permute-start = (bf16[136,768]{1,0:T(8,128)(2,1)}, bf16[136,768]{1,0:T(8,128)(2,1)S(1)}, u32[]{:S(2)}, u32[]{:S(2)}) collective-permute-start(bf16[136,768]{1,0:T(8,128)(2,1)} %get-tuple-element.12), channel_id=1, source_target_pairs={{4,6},{5,7},{6,4},{7,5},{8,10},{9,11},{10,8},{11,9},{20,22},{21,23... | collective-permute-start | bytes 626696 | tf_op jit(solution)/shard_map/ppermute | solution.py:307
  11.5 16.1 %collective-permute-start.1 = (bf16[136,768]{1,0:T(8,128)(2,1)}, bf16[136,768]{1,0:T(8,128)(2,1)S(1)}, u32[]{:S(2)}, u32[]{:S(2)}) collective-permute-start(bf16[136,768]{1,0:T(8,128)(2,1)} %get-tuple-element.13), channel_id=1, source_target_pairs={{0,10},{1,11},{2,8},{3,9},{12,6},{13,7},{14,4},{15,5},{16,26},{17,... | collective-permute-start | bytes 626696 | tf_op jit(solution)/shard_map/ppermute | solution.py:307
  18.1 12.4 %collective-permute-start.8 = (bf16[136,768]{1,0:T(8,128)(2,1)}, bf16[136,768]{1,0:T(8,128)(2,1)S(1)}, u32[]{:S(2)}, u32[]{:S(2)}) collective-permute-start(bf16[136,768]{1,0:T(8,128)(2,1)} %get-tuple-element.14), channel_id=1, source_target_pairs={{4,8},{5,9},{6,10},{7,11},{8,4},{9,5},{10,6},{11,7},{20,24},{21,25... | collective-permute-start | bytes 626696 | tf_op jit(solution)/shard_map/ppermute | solution.py:307
  20.5 10.0 %collective-permute-start.7 = (bf16[136,768]{1,0:T(8,128)(2,1)}, bf16[136,768]{1,0:T(8,128)(2,1)S(1)}, u32[]{:S(2)}, u32[]{:S(2)}) collective-permute-start(bf16[136,768]{1,0:T(8,128)(2,1)} %get-tuple-element.11.rest_1_), channel_id=1, source_target_pairs={{0,4},{1,5},{2,6},{3,7},{12,8},{13,9},{14,10},{15,11},{16,20},{17,... | collective-permute-start | bytes 626696 | tf_op jit(solution)/shard_map/ppermute | solution.py:307
  26.9 4.3 %copy-start.1 = (s32[4]{0:T(128)S(1)}, s32[4]{0:T(128)}, u32[]{:S(2)}) copy-start(s32[4]{0:T(128)} %sizes_ref.1) | copy-start | bytes 52
  27.0 4.3 %collective-permute-start.6 = (bf16[408,768]{1,0:T(8,128)(2,1)S(1)}, bf16[408,768]{1,0:T(8,128)(2,1)S(1)}, u32[]{:S(2)}, u32[]{:S(2)}) collective-permute-start(bf16[408,768]{1,0:T(8,128)(2,1)S(1)} %pad_maximum_fusion.1), channel_id=1, source_target_pairs={{4,5},{5,4},{6,7},{7,6},{8,9},{9,8},{10,11},{11,10},{20,21},{21,20... | collective-permute-start | bytes 1880072 | tf_op jit(solution)/shard_map/ppermute | solution.py:307
  27.8 3.5 %collective-permute-start.2 = (bf16[408,768]{1,0:T(8,128)(2,1)S(1)}, bf16[408,768]{1,0:T(8,128)(2,1)S(1)}, u32[]{:S(2)}, u32[]{:S(2)}) collective-permute-start(bf16[408,768]{1,0:T(8,128)(2,1)S(1)} %pad_maximum_fusion), channel_id=1, source_target_pairs={{4,5},{5,4},{6,7},{7,6},{8,9},{9,8},{10,11},{11,10},{20,21},{21,20... | collective-permute-start | bytes 1880072 | tf_op jit(solution)/shard_map/ppermute | solution.py:307
  30.5 0.7 %collective-permute-start.9 = (bf16[272,768]{1,0:T(8,128)(2,1)S(1)}, bf16[272,768]{1,0:T(8,128)(2,1)S(1)}, u32[]{:S(2)}, u32[]{:S(2)}) collective-permute-start(bf16[272,768]{1,0:T(8,128)(2,1)S(1)} %pad_maximum_fusion.2), channel_id=1, source_target_pairs={{4,5},{5,4},{6,7},{7,6},{8,9},{9,8},{10,11},{11,10},{20,21},{21,20... | collective-permute-start | bytes 1253384 | tf_op jit(solution)/shard_map/ppermute | solution.py:307
  31.8 15.1 %collective-permute-start.10 = (f32[1,512]{1,0:T(1,128)S(1)}, f32[1,512]{1,0:T(1,128)S(1)}, u32[]{:S(2)}, u32[]{:S(2)}) collective-permute-start(f32[1,512]{1,0:T(1,128)S(1)} %get-tuple-element.15), channel_id=1, source_target_pairs={{4,0},{5,4},{8,1},{9,5},{6,2},{7,6},{10,3},{11,7},{20,16},{21,20},... | collective-permute-start | bytes 6152 | tf_op jit(solution)/shard_map/ppermute | solution.py:307
  33.1 13.8 %collective-permute-start.11 = (f32[1,512]{1,0:T(1,128)S(1)}, f32[1,512]{1,0:T(1,128)S(1)}, u32[]{:S(2)}, u32[]{:S(2)}) collective-permute-start(f32[1,512]{1,0:T(1,128)S(1)} %get-tuple-element.16), channel_id=1, source_target_pairs={{4,12},{5,8},{8,13},{9,9},{6,14},{7,10},{10,15},{11,11},{20,28},{2... | collective-permute-start | bytes 6152 | tf_op jit(solution)/shard_map/ppermute | solution.py:307

commit v4 on v3

--- a/solution.py
+++ b/solution.py
@@ -7,6 +7,7 @@
 from jax.experimental.pallas import tpu as pltpu
 from jax.sharding import PartitionSpec as P
 
+TILE = 8
 PIECE = 16
 VMEM = pl.BlockSpec(memory_space=pltpu.VMEM)
 SMEM = pl.BlockSpec(memory_space=pltpu.SMEM)
@@ -165,17 +166,20 @@
     return lax.ppermute(found, ("chain", "clus"), pairs)
 
 
-def send_kernel(run_slots, cluster_runs, dest_hbm, rows_hbm, *rest):
-    block_refs, (dest_ref, rows_ref, sems) = rest[:-3], rest[-3:]
+def send_kernel(run_slots, cluster_runs, dest_hbm, rows_hbm, kept_ref, given_ref, *scratch):
+    dest_ref, rows_ref, sems = scratch
     dest_copy = pltpu.make_async_copy(dest_hbm, dest_ref, sems.at[0])
     rows_copy = pltpu.make_async_copy(rows_hbm, rows_ref, sems.at[1])
     dest_copy.start()
     rows_copy.start()
     rows, width = rows_ref.shape
     runs = rows // PIECE
-    depth = rows // len(block_refs)
+    half = rows // 2
+    depth = half // 2
+    clus = lax.axis_index("clus")
+    core = clus % 2
     upper = lax.axis_index("chain") >= lax.axis_size("chain") // 2
-    code = lax.axis_index("clus") // 2 * 2 + upper.astype(jnp.int32)
+    code = (clus // 2 ^ core) * 2 + upper.astype(jnp.int32)
     before = lax.broadcasted_iota(jnp.int32, (rows, rows), 0) < lax.broadcasted_iota(
         jnp.int32, (rows, rows), 1
     )
@@ -189,31 +193,48 @@
     rank = jnp.sum(jnp.where(member, earlier, 0.0), axis=0, keepdims=True).astype(jnp.int32)
     hot = as_bf16(lax.broadcasted_iota(jnp.int32, (rows, rows), 0) == run * PIECE + rank)
     moved = lax.dot_general(
-        jnp.broadcast_to(within, (8, rows)).astype(jnp.float32).astype(jnp.bfloat16),
+        jnp.broadcast_to(within, (TILE, rows)).astype(jnp.float32).astype(jnp.bfloat16),
         hot,
         (((1,), (1,)), ((), ())),
         preferred_element_type=jnp.float32,
-    ).astype(jnp.bfloat16)
+    )
     rows_copy.wait()
     x = rows_ref[...].astype(jnp.float32)
     units = (x * lax.rsqrt(jnp.sum(x * x, axis=1, keepdims=True) + 1e-06)).astype(jnp.bfloat16)
-    for index, block_ref in enumerate(block_refs):
+    for index, ref in enumerate((kept_ref, given_ref)):
+        low = index * half
+        ref[0:half, :] = jnp.dot(
+            hot[low : low + half], units, preferred_element_type=jnp.float32
+        ).astype(jnp.bfloat16)
+        line = lax.broadcasted_iota(jnp.int32, (TILE, half), 0) == index
+        ref[half : half + TILE, :] = jnp.zeros((TILE, width), jnp.bfloat16)
+        ref[half : half + TILE, 0:half] = jnp.where(line, moved[:, low : low + half], 0.0).astype(
+            jnp.bfloat16
+        )
+
+
+def merge_kernel(kept_ref, came_ref, near_ref, far_ref):
+    half = kept_ref.shape[0] - TILE
+    depth = half // 2
+    slots = kept_ref[half : half + TILE, 0:half].astype(jnp.float32)
+    slots = (slots + came_ref[half : half + TILE, 0:half].astype(jnp.float32)).astype(jnp.bfloat16)
+    for index, ref in enumerate((near_ref, far_ref)):
         low = index * depth
-        block_ref[0:depth, :] = jnp.dot(
-            hot[low : low + depth], units, preferred_element_type=jnp.float32
-        ).astype(jnp.bfloat16)
-        block_ref[depth : depth + 8, :] = jnp.zeros((8, width), jnp.bfloat16)
-        block_ref[depth : depth + 8, 0:depth] = moved[:, low : low + depth]
+        ref[0:depth, :] = kept_ref[low : low + depth, :]
+        ref[depth:half, :] = came_ref[low : low + depth, :]
+        ref[half : half + TILE, :] = jnp.zeros((TILE, ref.shape[1]), jnp.bfloat16)
+        ref[half : half + TILE, 0:depth] = slots[:, low : low + depth]
 
 
 def home_kernel(height, sizes_ref, *rest):
     refs, (first_ref, second_ref, keys_ref) = rest[:-3], rest[-3:]
     blocks = []
+    depth = (height - TILE) // 2
     for ref in refs:
-        blocks += [(ref, low) for low in range(0, ref.shape[0], height)]
+        for low in range(0, ref.shape[0], height):
+            blocks += [(ref, low, low + 2 * depth, 0), (ref, low + depth, low + 2 * depth, 1)]
     count = len(blocks)
     run_slots = count * PIECE
-    depth = height - 8
     runs = depth // PIECE
     chunk = first_ref.shape[1]
     chunk_runs = chunk // run_slots
@@ -230,14 +251,14 @@
 
     @pl.when(is_home)
     def _():
-        for index, (ref, low) in enumerate(blocks):
+        for index, (ref, low, _, _) in enumerate(blocks):
             for run in range(runs):
                 at = run * run_slots + index * PIECE
                 keys_ref[at : at + PIECE, :] = ref[low + run * PIECE : low + (run + 1) * PIECE, :]
 
     def answer(wanted, out_ref):
         slots = jnp.concatenate(
-            [ref[low + depth : low + depth + 8, 0:depth][0:1] for ref, low in blocks], axis=0
+            [ref[at : at + TILE, 0:depth][line : line + 1] for ref, _, at, line in blocks], axis=0
         )
         block_of = lax.broadcasted_iota(jnp.int32, (run_slots, count), 0) // PIECE
         mine = block_of == lax.broadcasted_iota(jnp.int32, (run_slots, count), 1)
@@ -285,20 +306,19 @@
     clus_len = lax.axis_size("clus")
     rows, width = embeddings.shape
     run_slots = chain_len * clus_len * PIECE
-    depth = rows // clus_len
-    height = depth + 8
+    height = rows // 2 + TILE
     block = jax.ShapeDtypeStruct((height, width), jnp.bfloat16)
-    blocks = pl.pallas_call(
-        functools.partial(send_kernel, run_slots, depth // PIECE),
-        out_shape=(block,) * clus_len,
+    kept, given = pl.pallas_call(
+        functools.partial(send_kernel, run_slots, rows // clus_len // PIECE),
+        out_shape=(block, block),
         in_specs=[HBM, HBM],
-        out_specs=(VMEM,) * clus_len,
+        out_specs=(VMEM, VMEM),
         scratch_shapes=[
             pltpu.VMEM((1, rows), jnp.int32),
             pltpu.VMEM((rows, width), jnp.bfloat16),
             pltpu.SemaphoreType.DMA((2,)),
         ],
-        compiler_params=pltpu.CompilerParams(vmem_limit_bytes=58 * 2**20),
+        compiler_params=pltpu.CompilerParams(vmem_limit_bytes=62_400_000),
         name="send_blocks",
     )(dest.reshape(1, rows), embeddings)
 
@@ -306,35 +326,32 @@
         pairs = [(a * clus_len + b, c * clus_len + d) for a, b, c, d in moves]
         return lax.ppermute(value, ("chain", "clus"), pairs)
 
-    def to_home(value, moves, flip):
-        return permute(value, [(a, k, b, k ^ flip) for a, b in moves for k in range(clus_len)])
+    def to_home(value, moves):
+        columns = range(clus_len)
+        return permute(value, [(a, k, b, k ^ (2 * (k % 2))) for a, b in moves for k in columns])
 
     low, high, top = chain_len // 2 - 1, chain_len // 2, chain_len - 1
-    near = [(0, low), (top, high)]
-    far = [(0, high), (top, low)]
-    middle = [(low, high), (high, low)]
-    stay = [(low, low), (high, high)]
-
-    def swap(values):
-        value = jnp.concatenate(values, axis=0)
-        return permute(value, [(z, k, z, k ^ 1) for z in (low, high) for k in range(clus_len)])
-
-    far_across = to_home(blocks[3], far, 2)
-    far_along = to_home(blocks[1], far, 0)
-    stay_across = to_home(blocks[2], stay, 2)
-    near_across = to_home(blocks[2], near, 2)
-    middle_across = to_home(blocks[3], middle, 2)
-    near_along = to_home(blocks[0], near, 0)
-    middle_along = to_home(blocks[1], middle, 0)
-    batches = [
-        [blocks[0], stay_across, far_across],
-        [far_along, near_across, middle_across],
-        [near_along, middle_along],
-    ]
+
+    def swap(values, planes):
+        value = jnp.concatenate(values, axis=0) if len(values) > 1 else values[0]
+        return permute(value, [(z, k, z, k ^ 1) for z in planes for k in range(clus_len)])
+
+    near, far = pl.pallas_call(
+        merge_kernel,
+        out_shape=(block, block),
+        in_specs=[VMEM, VMEM],
+        out_specs=(VMEM, VMEM),
+        compiler_params=pltpu.CompilerParams(vmem_limit_bytes=16 * 2**20),
+        name="merge_blocks",
+    )(kept, swap([given], range(chain_len)))
+
+    from_far = to_home(far, [(0, high), (top, low)])
+    from_middle = to_home(far, [(low, high), (high, low)])
+    from_near = to_home(near, [(0, low), (top, high)])
+    from_plane = to_home(near, [(low, low), (high, high)])
     keys = []
-    for batch in batches:
-        keys.append(swap(batch))
-        keys += batch
+    for batch in ([from_plane, from_far], [from_near], [from_middle]):
+        keys += batch + [swap(batch, (low, high))]
 
     answers = pl.pallas_call(
         functools.partial(home_kernel, height),

time: 47.9 us -> 49 us (1.023)
  waiting for transfers between devices: 16.9 us -> 30.4 us
  starting transfers between devices: 26.4 us -> 13.1 us
  local copies, waits for them, and re-layouts: 0.01 us -> 1.01 us
    ppermute x12 -> x10, waiting for transfers between devices: 16.9 us -> 30.4 us  [permute(): return lax.ppermute(value, ('chain', 'clus'), pairs)]
    ppermute x12 -> x10, starting transfers between devices: 26.4 us -> 13.1 us  [permute(): return lax.ppermute(value, ('chain', 'clus'), pairs)]
    unnamed x4, local copies, waits for them, and re-layouts: 0.01 us -> 1.01 us
    pallas_call x1 -> x2, Pallas kernels: 2.75 us -> 2.8 us  [the longest x1 2.75 us: local_home(): pl.pallas_call(functools.partial(send_kernel, run_slots, rows // clus_len...]
  transfers between devices with their start and end apart: 12 -> 10, of which waited for: 3 -> 4; matrix products, arithmetic and copies ran while one was open for 0% -> 0% of each run, Pallas kernels for 0% -> 0%
where the time goes in v4:
time: 49 us; the launch traced here: 48.7 us
  waiting for transfers between devices  30.4 us (62%)
  starting transfers between devices  13.1 us (27%)
  Pallas kernels  3.38 us (7%)
  local copies, waits for them, and re-layouts  1.01 us (2%)
  other arithmetic  0.64 us (1%)
    ppermute x10, waiting for transfers between devices, permute(): return lax.ppermute(value, ('chain', 'clus'), pairs)  30.4 us
    ppermute x10, starting transfers between devices, permute(): return lax.ppermute(value, ('chain', 'clus'), pairs)  13.1 us
    pallas_call x1, Pallas kernels, local_home(): pl.pallas_call(functools.partial(send_kernel, run_slots, rows // clus_len...  2.75 us
    unnamed x4, local copies, waits for them, and re-layouts  1.01 us
  transfers between devices with their start and end apart: 10, of which 4 were waited for; matrix products, arithmetic and copies ran while one was open for 0% of the time, Pallas kernels for 0%

profile of v4, /device:TPU:0, one launch (start us, length us, event | category | flops | bytes accessed | tf_op | source)
XLA Modules:
  0.0 48.7 jit_solution(1986984785267364852)
XLA Ops:
  0.0 2.7 %send_blocks.1 = (bf16[264,768]{1,0:T(8,128)(2,1)}, bf16[264,768]{1,0:T(8,128)(2,1)}) custom-call(s32[1,512]{1,0:T(1,128)} %bitcast.1, bf16[512,768]{1,0:T(8,128)(2,1)} %rows_hbm.1), custom_call_target="tpu_custom_call" | custom-call | tf_op jit(solution)/shard_map/send_blocks/pallas_call | solution.py:311
  2.8 0.5 %collective-permute-start = (bf16[264,768]{1,0:T(8,128)(2,1)}, bf16[264,768]{1,0:T(8,128)(2,1)S(1)}, u32[]{:S(2)}, u32[]{:S(2)}) collective-permute-start(bf16[264,768]{1,0:T(8,128)(2,1)} %get-tuple-element.12), channel_id=1, source_target_pairs={{0,1},{1,0},{2,3},{3,2},{4,5},{5,4},{6,7},{7,6},{8,9},{9,8},{10,11... | collective-permute-start | bytes 1216520 | tf_op jit(solution)/shard_map/ppermute | solution.py:327
  3.3 1.6 %collective-permute-done.came_ref = bf16[264,768]{1,0:T(8,128)(2,1)S(1)} collective-permute-done((bf16[264,768]{1,0:T(8,128)(2,1)}, bf16[264,768]{1,0:T(8,128)(2,1)S(1)}, u32[]{:S(2)}, u32[]{:S(2)}) %collective-permute-start) | collective-permute-done | bytes 405536 | tf_op jit(solution)/shard_map/ppermute | solution.py:327
  4.9 0.0 copy-start
  4.9 1.0 %copy-done = bf16[264,768]{1,0:T(8,128)(2,1)S(1)} copy-done((bf16[264,768]{1,0:T(8,128)(2,1)S(1)}, bf16[264,768]{1,0:T(8,128)(2,1)}, u32[]{:S(2)}) %copy-start) | copy-done | bytes 405528
  5.9 0.1 merge_blocks.1
  5.9 0.7 %collective-permute-start.1 = (bf16[264,768]{1,0:T(8,128)(2,1)S(1)}, bf16[264,768]{1,0:T(8,128)(2,1)S(1)}, u32[]{:S(2)}, u32[]{:S(2)}) collective-permute-start(bf16[264,768]{1,0:T(8,128)(2,1)S(1)} %get-tuple-element.13), channel_id=1, source_target_pairs={{4,4},{5,7},{6,6},{7,5},{8,8},{9,11},{10,10},{11,9},{20,20},{21,23... | collective-permute-start | bytes 1216520 | tf_op jit(solution)/shard_map/ppermute | solution.py:327
  6.6 0.0 copy-start.1
  6.6 5.9 %collective-permute-start.2 = (bf16[264,768]{1,0:T(8,128)(2,1)S(1)}, bf16[264,768]{1,0:T(8,128)(2,1)S(1)}, u32[]{:S(2)}, u32[]{:S(2)}) collective-permute-start(bf16[264,768]{1,0:T(8,128)(2,1)S(1)} %get-tuple-element.14), channel_id=1, source_target_pairs={{0,8},{1,11},{2,10},{3,9},{12,4},{13,7},{14,6},{15,5},{16,24},{17,... | collective-permute-start | bytes 1216520 | tf_op jit(solution)/shard_map/ppermute | solution.py:327
  12.5 1.3 %collective-permute-start.4 = (bf16[264,768]{1,0:T(8,128)(2,1)S(1)}, bf16[264,768]{1,0:T(8,128)(2,1)S(1)}, u32[]{:S(2)}, u32[]{:S(2)}) collective-permute-start(bf16[264,768]{1,0:T(8,128)(2,1)S(1)} %get-tuple-element.13), channel_id=1, source_target_pairs={{0,4},{1,7},{2,6},{3,5},{12,8},{13,11},{14,10},{15,9},{16,20},{17,... | collective-permute-start | bytes 1216520 | tf_op jit(solution)/shard_map/ppermute | solution.py:327
  13.8 0.7 %collective-permute-start.6 = (bf16[264,768]{1,0:T(8,128)(2,1)S(1)}, bf16[264,768]{1,0:T(8,128)(2,1)S(1)}, u32[]{:S(2)}, u32[]{:S(2)}) collective-permute-start(bf16[264,768]{1,0:T(8,128)(2,1)S(1)} %get-tuple-element.14), channel_id=1, source_target_pairs={{4,8},{5,11},{6,10},{7,9},{8,4},{9,7},{10,6},{11,5},{20,24},{21,27... | collective-permute-start | bytes 1216520 | tf_op jit(solution)/shard_map/ppermute | solution.py:327
  14.5 0.0 collective-permute-done.1.rest_0_
  14.5 6.1 %collective-permute-done.2.rest_1_ = bf16[264,768]{1,0:T(8,128)(2,1)S(1)} collective-permute-done((bf16[264,768]{1,0:T(8,128)(2,1)S(1)}, bf16[264,768]{1,0:T(8,128)(2,1)S(1)}, u32[]{:S(2)}, u32[]{:S(2)}) %collective-permute-start.2) | collective-permute-done | bytes 405536 | tf_op jit(solution)/shard_map/ppermute | solution.py:327
  20.6 0.1 pad_maximum_fusion
  20.7 0.7 %collective-permute-start.3 = (bf16[528,768]{1,0:T(8,128)(2,1)S(1)}, bf16[528,768]{1,0:T(8,128)(2,1)S(1)}, u32[]{:S(2)}, u32[]{:S(2)}) collective-permute-start(bf16[528,768]{1,0:T(8,128)(2,1)S(1)} %pad_maximum_fusion), channel_id=1, source_target_pairs={{4,5},{5,4},{6,7},{7,6},{8,9},{9,8},{10,11},{11,10},{20,21},{21,20... | collective-permute-start | bytes 2433032 | tf_op jit(solution)/shard_map/ppermute | solution.py:327
  21.4 7.9 %collective-permute-done.4.rest_3_ = bf16[264,768]{1,0:T(8,128)(2,1)S(1)} collective-permute-done((bf16[264,768]{1,0:T(8,128)(2,1)S(1)}, bf16[264,768]{1,0:T(8,128)(2,1)S(1)}, u32[]{:S(2)}, u32[]{:S(2)}) %collective-permute-start.4) | collective-permute-done | bytes 405536 | tf_op jit(solution)/shard_map/ppermute | solution.py:327
  29.3 0.7 %collective-permute-start.5 = (bf16[264,768]{1,0:T(8,128)(2,1)S(1)}, bf16[264,768]{1,0:T(8,128)(2,1)S(1)}, u32[]{:S(2)}, u32[]{:S(2)}) collective-permute-start(bf16[264,768]{1,0:T(8,128)(2,1)S(1)} %collective-permute-done.4.rest_3_), channel_id=1, source_target_pairs={{4,5},{5,4},{6,7},{7,6},{8,9},{9,8},{10,11},{11,10},{20,21},{21,20... | collective-permute-start | bytes 1216520 | tf_op jit(solution)/shard_map/ppermute | solution.py:327
  30.0 0.0 collective-permute-done.6.rest_5_
  30.0 0.7 %collective-permute-start.7 = (bf16[264,768]{1,0:T(8,128)(2,1)S(1)}, bf16[264,768]{1,0:T(8,128)(2,1)S(1)}, u32[]{:S(2)}, u32[]{:S(2)}) collective-permute-start(bf16[264,768]{1,0:T(8,128)(2,1)S(1)} %collective-permute-done.6.rest_5_), channel_id=1, source_target_pairs={{4,5},{5,4},{6,7},{7,6},{8,9},{9,8},{10,11},{11,10},{20,21},{21,20... | collective-permute-start | bytes 1216520 | tf_op jit(solution)/shard_map/ppermute | solution.py:327
  30.7 0.0 collective-permute-done.5.rest_4_
  30.7 0.0 collective-permute-done.7.rest_6_
  30.7 0.0 collective-permute-done.3.rest_2_
  30.8 0.0 copy-done.1
  30.8 0.6 %best_at_home.1 = (f32[1,512]{1,0:T(1,128)S(1)}, f32[1,512]{1,0:T(1,128)S(1)}) custom-call(s32[4]{0:T(128)S(1)} %copy-done.1, bf16[264,768]{1,0:T(8,128)(2,1)S(1)} %collective-permute-done.1.rest_0_, bf16[264,768]{1,0:T(8,128)(2,1)S(1)} %collective-permute-done.2.rest_1_, bf16[528,768]{1,0:T(8,128)(2,1)S(1)} %collective-permute-done.3.rest_2_, ...), custom_call_target="tpu_custom_call" | custom-call | tf_op jit(solution)/shard_map/best_at_home/pallas_call | solution.py:356
  31.4 1.3 %collective-permute-start.8 = (f32[1,512]{1,0:T(1,128)S(1)}, f32[1,512]{1,0:T(1,128)S(1)}, u32[]{:S(2)}, u32[]{:S(2)}) collective-permute-start(f32[1,512]{1,0:T(1,128)S(1)} %get-tuple-element.15), channel_id=1, source_target_pairs={{4,0},{5,4},{8,1},{9,5},{6,2},{7,6},{10,3},{11,7},{20,16},{21,20},... | collective-permute-start | bytes 6152 | tf_op jit(solution)/shard_map/ppermute | solution.py:327
  32.7 0.7 %collective-permute-start.9 = (f32[1,512]{1,0:T(1,128)S(1)}, f32[1,512]{1,0:T(1,128)S(1)}, u32[]{:S(2)}, u32[]{:S(2)}) collective-permute-start(f32[1,512]{1,0:T(1,128)S(1)} %get-tuple-element.16), channel_id=1, source_target_pairs={{4,12},{5,8},{8,13},{9,9},{6,14},{7,10},{10,15},{11,11},{20,28},{2... | collective-permute-start | bytes 6152 | tf_op jit(solution)/shard_map/ppermute | solution.py:327
  33.3 14.8 %collective-permute-done.8 = f32[1,512]{1,0:T(1,128)S(1)} collective-permute-done((f32[1,512]{1,0:T(1,128)S(1)}, f32[1,512]{1,0:T(1,128)S(1)}, u32[]{:S(2)}, u32[]{:S(2)}) %collective-permute-start.8) | collective-permute-done | bytes 2080 | tf_op jit(solution)/shard_map/ppermute | solution.py:327
  48.1 0.0 collective-permute-done.9
  48.1 0.6 %add.3 = f32[1,512]{1,0:T(1,128)} add(f32[1,512]{1,0:T(1,128)S(1)} %collective-permute-done.8, f32[1,512]{1,0:T(1,128)S(1)} %collective-permute-done.9) | non-fusion elementwise | flops 512 | bytes 6144 | tf_op jit(solution)/shard_map/add | solution.py:371
Async XLA Ops:
  2.8 2.1 %collective-permute-start = (bf16[264,768]{1,0:T(8,128)(2,1)}, bf16[264,768]{1,0:T(8,128)(2,1)S(1)}, u32[]{:S(2)}, u32[]{:S(2)}) collective-permute-start(bf16[264,768]{1,0:T(8,128)(2,1)} %get-tuple-element.12), channel_id=1, source_target_pairs={{0,1},{1,0},{2,3},{3,2},{4,5},{5,4},{6,7},{7,6},{8,9},{9,8},{10,11... | collective-permute-start | bytes 1216520 | tf_op jit(solution)/shard_map/ppermute | solution.py:327
  4.9 1.0 %copy-start = (bf16[264,768]{1,0:T(8,128)(2,1)S(1)}, bf16[264,768]{1,0:T(8,128)(2,1)}, u32[]{:S(2)}) copy-start(bf16[264,768]{1,0:T(8,128)(2,1)} %get-tuple-element.11.kept_ref) | copy-start | bytes 1216516
  5.9 8.6 %collective-permute-start.1 = (bf16[264,768]{1,0:T(8,128)(2,1)S(1)}, bf16[264,768]{1,0:T(8,128)(2,1)S(1)}, u32[]{:S(2)}, u32[]{:S(2)}) collective-permute-start(bf16[264,768]{1,0:T(8,128)(2,1)S(1)} %get-tuple-element.13), channel_id=1, source_target_pairs={{4,4},{5,7},{6,6},{7,5},{8,8},{9,11},{10,10},{11,9},{20,20},{21,23... | collective-permute-start | bytes 1216520 | tf_op jit(solution)/shard_map/ppermute | solution.py:327
  6.6 24.1 %copy-start.1 = (s32[4]{0:T(128)S(1)}, s32[4]{0:T(128)}, u32[]{:S(2)}) copy-start(s32[4]{0:T(128)} %sizes_ref.1) | copy-start | bytes 52
  6.6 14.0 %collective-permute-start.2 = (bf16[264,768]{1,0:T(8,128)(2,1)S(1)}, bf16[264,768]{1,0:T(8,128)(2,1)S(1)}, u32[]{:S(2)}, u32[]{:S(2)}) collective-permute-start(bf16[264,768]{1,0:T(8,128)(2,1)S(1)} %get-tuple-element.14), channel_id=1, source_target_pairs={{0,8},{1,11},{2,10},{3,9},{12,4},{13,7},{14,6},{15,5},{16,24},{17,... | collective-permute-start | bytes 1216520 | tf_op jit(solution)/shard_map/ppermute | solution.py:327
  12.5 16.8 %collective-permute-start.4 = (bf16[264,768]{1,0:T(8,128)(2,1)S(1)}, bf16[264,768]{1,0:T(8,128)(2,1)S(1)}, u32[]{:S(2)}, u32[]{:S(2)}) collective-permute-start(bf16[264,768]{1,0:T(8,128)(2,1)S(1)} %get-tuple-element.13), channel_id=1, source_target_pairs={{0,4},{1,7},{2,6},{3,5},{12,8},{13,11},{14,10},{15,9},{16,20},{17,... | collective-permute-start | bytes 1216520 | tf_op jit(solution)/shard_map/ppermute | solution.py:327
  13.8 16.2 %collective-permute-start.6 = (bf16[264,768]{1,0:T(8,128)(2,1)S(1)}, bf16[264,768]{1,0:T(8,128)(2,1)S(1)}, u32[]{:S(2)}, u32[]{:S(2)}) collective-permute-start(bf16[264,768]{1,0:T(8,128)(2,1)S(1)} %get-tuple-element.14), channel_id=1, source_target_pairs={{4,8},{5,11},{6,10},{7,9},{8,4},{9,7},{10,6},{11,5},{20,24},{21,27... | collective-permute-start | bytes 1216520 | tf_op jit(solution)/shard_map/ppermute | solution.py:327
  20.7 10.0 %collective-permute-start.3 = (bf16[528,768]{1,0:T(8,128)(2,1)S(1)}, bf16[528,768]{1,0:T(8,128)(2,1)S(1)}, u32[]{:S(2)}, u32[]{:S(2)}) collective-permute-start(bf16[528,768]{1,0:T(8,128)(2,1)S(1)} %pad_maximum_fusion), channel_id=1, source_target_pairs={{4,5},{5,4},{6,7},{7,6},{8,9},{9,8},{10,11},{11,10},{20,21},{21,20... | collective-permute-start | bytes 2433032 | tf_op jit(solution)/shard_map/ppermute | solution.py:327
  29.3 1.4 %collective-permute-start.5 = (bf16[264,768]{1,0:T(8,128)(2,1)S(1)}, bf16[264,768]{1,0:T(8,128)(2,1)S(1)}, u32[]{:S(2)}, u32[]{:S(2)}) collective-permute-start(bf16[264,768]{1,0:T(8,128)(2,1)S(1)} %collective-permute-done.4.rest_3_), channel_id=1, source_target_pairs={{4,5},{5,4},{6,7},{7,6},{8,9},{9,8},{10,11},{11,10},{20,21},{21,20... | collective-permute-start | bytes 1216520 | tf_op jit(solution)/shard_map/ppermute | solution.py:327
  30.0 0.7 %collective-permute-start.7 = (bf16[264,768]{1,0:T(8,128)(2,1)S(1)}, bf16[264,768]{1,0:T(8,128)(2,1)S(1)}, u32[]{:S(2)}, u32[]{:S(2)}) collective-permute-start(bf16[264,768]{1,0:T(8,128)(2,1)S(1)} %collective-permute-done.6.rest_5_), channel_id=1, source_target_pairs={{4,5},{5,4},{6,7},{7,6},{8,9},{9,8},{10,11},{11,10},{20,21},{21,20... | collective-permute-start | bytes 1216520 | tf_op jit(solution)/shard_map/ppermute | solution.py:327
  31.4 16.8 %collective-permute-start.8 = (f32[1,512]{1,0:T(1,128)S(1)}, f32[1,512]{1,0:T(1,128)S(1)}, u32[]{:S(2)}, u32[]{:S(2)}) collective-permute-start(f32[1,512]{1,0:T(1,128)S(1)} %get-tuple-element.15), channel_id=1, source_target_pairs={{4,0},{5,4},{8,1},{9,5},{6,2},{7,6},{10,3},{11,7},{20,16},{21,20},... | collective-permute-start | bytes 6152 | tf_op jit(solution)/shard_map/ppermute | solution.py:327
  32.7 15.5 %collective-permute-start.9 = (f32[1,512]{1,0:T(1,128)S(1)}, f32[1,512]{1,0:T(1,128)S(1)}, u32[]{:S(2)}, u32[]{:S(2)}) collective-permute-start(f32[1,512]{1,0:T(1,128)S(1)} %get-tuple-element.16), channel_id=1, source_target_pairs={{4,12},{5,8},{8,13},{9,9},{6,14},{7,10},{10,15},{11,11},{20,28},{2... | collective-permute-start | bytes 6152 | tf_op jit(solution)/shard_map/ppermute | solution.py:327

commit v5 on v1

--- a/solution.py
+++ b/solution.py
@@ -7,9 +7,16 @@
 from jax.experimental.pallas import tpu as pltpu
 from jax.sharding import PartitionSpec as P
 
+TILE = 8
+LANES = 128
 PIECE = 16
 VMEM = pl.BlockSpec(memory_space=pltpu.VMEM)
 SMEM = pl.BlockSpec(memory_space=pltpu.SMEM)
+HBM = pl.BlockSpec(memory_space=pltpu.HBM)
+
+
+def as_bf16(mask):
+    return mask.astype(jnp.float32).astype(jnp.bfloat16)
 
 
 def sort_kernel(run_slots, dest_ref, rows_ref, units_ref, slots_ref):
@@ -94,7 +101,7 @@
     out_ref[...] = jnp.where(position < members, found, 0.0)
 
 
-def local(embeddings, dest, sizes):
+def local_plane(embeddings, dest, sizes):
     chain_len = lax.axis_size("chain")
     clus_len = lax.axis_size("clus")
     shards = chain_len * clus_len
@@ -160,9 +167,229 @@
     return lax.ppermute(found, ("chain", "clus"), pairs)
 
 
+def send_kernel(run_slots, cluster_runs, dest_hbm, rows_hbm, kept_ref, slots_ref, given_ref, *scratch):
+    dest_ref, rows_ref, sems = scratch
+    dest_copy = pltpu.make_async_copy(dest_hbm, dest_ref, sems.at[0])
+    rows_copy = pltpu.make_async_copy(rows_hbm, rows_ref, sems.at[1])
+    dest_copy.start()
+    rows_copy.start()
+    rows, width = rows_ref.shape
+    runs = rows // PIECE
+    half = rows // 2
+    depth = half // 2
+    clus = lax.axis_index("clus")
+    upper = (lax.axis_index("chain") >= lax.axis_size("chain") // 2).astype(jnp.int32)
+    code = (clus // 2 ^ clus % 2 ^ upper) * 2 + upper
+    before = lax.broadcasted_iota(jnp.int32, (rows, rows), 0) < lax.broadcasted_iota(
+        jnp.int32, (rows, rows), 1
+    )
+    dest_copy.wait()
+    dest = dest_ref[...]
+    run = lax.div(dest, run_slots)
+    within = lax.rem(dest, run_slots)
+    run = (lax.div(run, cluster_runs) ^ code) * cluster_runs + lax.rem(run, cluster_runs)
+    member = lax.broadcasted_iota(jnp.int32, (runs, rows), 0) == run
+    earlier = jnp.dot(as_bf16(member), as_bf16(before), preferred_element_type=jnp.float32)
+    rank = jnp.sum(jnp.where(member, earlier, 0.0), axis=0, keepdims=True).astype(jnp.int32)
+    hot = as_bf16(lax.broadcasted_iota(jnp.int32, (rows, rows), 0) == run * PIECE + rank)
+    moved = lax.dot_general(
+        jnp.broadcast_to(within, (TILE, rows)).astype(jnp.float32).astype(jnp.bfloat16),
+        hot,
+        (((1,), (1,)), ((), ())),
+        preferred_element_type=jnp.float32,
+    )
+    rows_copy.wait()
+    x = rows_ref[...].astype(jnp.float32)
+    units = (x * lax.rsqrt(jnp.sum(x * x, axis=1, keepdims=True) + 1e-06)).astype(jnp.bfloat16)
+    for low, ref in ((0, kept_ref), (half, given_ref)):
+        ref[0:half, :] = jnp.dot(
+            hot[low : low + half], units, preferred_element_type=jnp.float32
+        ).astype(jnp.bfloat16)
+    line = lax.broadcasted_iota(jnp.int32, (TILE, half), 0)
+    slots_ref[...] = jnp.where(line == 0, moved[:, 0:half], 0.0)
+    given_ref[half : half + TILE, :] = jnp.zeros((TILE, width), jnp.bfloat16)
+    given_ref[half : half + TILE, 0:half] = jnp.where(line == 1, moved[:, half:rows], 0.0).astype(
+        jnp.bfloat16
+    )
+
+
+def merge_kernel(kept_ref, slots_ref, came_ref, near_ref, far_ref):
+    half, width = kept_ref.shape
+    depth = half // 2
+    slots = slots_ref[...] + came_ref[half : half + TILE, 0:half].astype(jnp.float32)
+    for low, ref in ((0, near_ref), (depth, far_ref)):
+        ref[0:depth, :] = kept_ref[low : low + depth, :]
+        ref[depth:half, :] = came_ref[low : low + depth, :]
+        ref[half : half + TILE, :] = jnp.zeros((TILE, width), jnp.bfloat16)
+        ref[half : half + TILE, 0:depth] = slots[:, low : low + depth].astype(jnp.bfloat16)
+
+
+def home_chain():
+    return lax.axis_size("chain") // 2 - 1 + lax.axis_index("clus") % 2
+
+
+def stage_kernel(run_slots, old, new, last, *rest):
+    sizes_ref, rest = (rest[0], rest[1:]) if last else (None, rest)
+    refs, rest = rest[: old + new], rest[old + new :]
+    old_states, rest = rest[: 2 * old], rest[2 * old :]
+    outs = rest[: 1 if last else 2 * (old + new)]
+    states = rest[len(outs) :] if last else outs
+    rows = refs[0].shape[0] - TILE
+    depth = rows // 2
+    runs = depth // PIECE
+    is_home = lax.axis_index("chain") == home_chain()
+
+    def halves(value):
+        best = value[:, 0:LANES]
+        for low in range(LANES, value.shape[1], LANES):
+            best = jnp.maximum(best, value[:, low : low + LANES])
+        return best
+
+    @pl.when(is_home)
+    def _():
+        for index in range(old):
+            states[2 * index][...] = old_states[2 * index][...]
+            states[2 * index + 1][...] = old_states[2 * index + 1][...]
+        diagonal = lax.broadcasted_iota(jnp.int32, (rows, rows), 0) == lax.broadcasted_iota(
+            jnp.int32, (rows, rows), 1
+        )
+        run_of = lax.broadcasted_iota(jnp.int32, (1, depth), 1) // PIECE
+        for index in range(old, old + new):
+            slots = refs[index][rows : rows + TILE, 0:depth].astype(jnp.float32)
+            start = (run_of * run_slots).astype(jnp.float32)
+            line = jnp.concatenate([slots[0:1] + start, slots[1:2] + start], axis=1)
+            column = jnp.sum(jnp.where(diagonal, line, 0.0), axis=1, keepdims=True)
+            states[2 * index][...] = jnp.broadcast_to(column, (rows, LANES))
+            block = refs[index][0:rows, :]
+            best = jnp.full((8, rows), -1.0, jnp.float32)
+            for other in range(index + 1):
+                scores = lax.dot_general(
+                    refs[other][0:rows, :],
+                    block,
+                    (((1,), (1,)), ((), ())),
+                    preferred_element_type=jnp.float32,
+                )
+                place = states[2 * other][...]
+                earlier = jnp.concatenate([place] * (rows // LANES), axis=1) < line
+                kept = jnp.where(earlier, scores, -2.0)
+                best = jnp.maximum(best, jnp.max(kept.reshape(rows // 8, 8, rows), axis=0))
+                if other < index:
+                    given = halves(jnp.where(earlier, -2.0, scores))
+                    states[2 * other + 1][...] = jnp.maximum(states[2 * other + 1][...], given)
+            best = jnp.max(best, axis=0, keepdims=True)
+            states[2 * index + 1][...] = halves(jnp.where(diagonal, best, -2.0))
+
+    if last:
+        (out_ref,) = outs
+        chunk = out_ref.shape[1]
+
+        @pl.when(jnp.logical_not(is_home))
+        def _():
+            out_ref[...] = jnp.zeros_like(out_ref)
+
+        @pl.when(is_home)
+        def _():
+            members = sizes_ref[lax.axis_index("clus")]
+            lane = lax.broadcasted_iota(jnp.int32, (run_slots, run_slots), 1)
+            for run in range(runs):
+                where = [
+                    (index, low + run * PIECE) for index in range(old + new) for low in (0, depth)
+                ]
+                place, best = (
+                    jnp.concatenate([states[2 * n + kind][at : at + PIECE, :] for n, at in where])
+                    for kind in range(2)
+                )
+                best = jnp.max(best, axis=1, keepdims=True)
+                place = jnp.concatenate([place] * (run_slots // LANES), axis=1)
+                base = run * run_slots
+                found = jnp.where(place == (lane + base).astype(jnp.float32), best, 0.0)
+                found = jnp.sum(found, axis=0, keepdims=True)
+                position = base + lax.broadcasted_iota(jnp.int32, (1, run_slots), 1)
+                found = jnp.where(position < members, found, 0.0)
+                row, low = base // chunk, base % chunk
+                out_ref[row : row + 1, low : low + run_slots] = found
+
+
+def local_home(embeddings, dest, sizes):
+    chain_len = lax.axis_size("chain")
+    clus_len = lax.axis_size("clus")
+    rows, width = embeddings.shape
+    half = rows // 2
+    run_slots = chain_len * clus_len * PIECE
+    block = jax.ShapeDtypeStruct((half + TILE, width), jnp.bfloat16)
+    kept, slots, given = pl.pallas_call(
+        functools.partial(send_kernel, run_slots, rows // clus_len // PIECE),
+        out_shape=(
+            jax.ShapeDtypeStruct((half, width), jnp.bfloat16),
+            jax.ShapeDtypeStruct((TILE, half), jnp.float32),
+            block,
+        ),
+        in_specs=[HBM, HBM],
+        out_specs=(VMEM, VMEM, VMEM),
+        scratch_shapes=[
+            pltpu.VMEM((1, rows), jnp.int32),
+            pltpu.VMEM((rows, width), jnp.bfloat16),
+            pltpu.SemaphoreType.DMA((2,)),
+        ],
+        compiler_params=pltpu.CompilerParams(vmem_limit_bytes=32 * 2**20),
+        name="send_blocks",
+    )(dest.reshape(1, rows), embeddings)
+
+    def permute(value, moves):
+        pairs = [(a * clus_len + b, c * clus_len + d) for a, b, c, d in moves]
+        return lax.ppermute(value, ("chain", "clus"), pairs)
+
+    low, high, top = chain_len // 2 - 1, chain_len // 2, chain_len - 1
+    swap = [(z, k, z, k ^ 1) for z in range(chain_len) for k in range(clus_len)]
+    near, far = pl.pallas_call(
+        merge_kernel,
+        out_shape=(block, block),
+        in_specs=[VMEM, VMEM, VMEM],
+        out_specs=(VMEM, VMEM),
+        compiler_params=pltpu.CompilerParams(vmem_limit_bytes=16 * 2**20),
+        name="merge_blocks",
+    )(kept, slots, permute(given, swap))
+
+    def to_home(value, moves, across):
+        pairs = []
+        for a, b in moves:
+            for x in range(clus_len // 2):
+                source = 2 * x + (across ^ (a >= high))
+                pairs.append((a, source, b, 2 * (x ^ across) + (b - low)))
+        return permute(value, pairs)
+
+    nearer, farther = [(0, low), (top, high)], [(0, high), (top, low)]
+    middle, plane = [(low, high), (high, low)], [(low, low), (high, high)]
+    stages = [
+        [near, to_home(near, plane, 1), to_home(far, farther, 0)],
+        [to_home(far, farther, 1), to_home(near, nearer, 0)],
+        [to_home(near, nearer, 1), to_home(far, middle, 0)],
+        [to_home(far, middle, 1)],
+    ]
+    blocks, states = [], []
+    state = jax.ShapeDtypeStruct((half, LANES), jnp.float32)
+    for number, arrived in enumerate(stages):
+        last = number == len(stages) - 1
+        old, new = len(blocks), len(arrived)
+        blocks = blocks + arrived
+        count = 2 * len(blocks)
+        outs = (jax.ShapeDtypeStruct((chain_len, rows), jnp.float32),) if last else (state,) * count
+        states = pl.pallas_call(
+            functools.partial(stage_kernel, run_slots, old, new, last),
+            out_shape=outs,
+            in_specs=[SMEM] * last + [VMEM] * (len(blocks) + len(states)),
+            out_specs=(VMEM,) * len(outs),
+            scratch_shapes=[pltpu.VMEM(state.shape, jnp.float32)] * (count if last else 0),
+            compiler_params=pltpu.CompilerParams(vmem_limit_bytes=32 * 2**20),
+            name="multiply_last" if last else "multiply_arrived",
+        )(*([sizes] if last else []), *blocks, *states)
+    found = lax.all_to_all(states[0], "chain", split_axis=0, concat_axis=0, tiled=True)
+    return jnp.sum(found, axis=0, keepdims=True)
+
+
 def solution(mesh):
     return jax.shard_map(
-        local,
+        local_home if mesh.shape["chain"] == mesh.shape["clus"] == 4 else local_plane,
         mesh=mesh,
         in_specs=(
             P(("groups", "chain", "clus"), None),

time: 82.7 us -> 47 us (0.57)
  the two profiles are of different devices: /device:TPU:7 before, /device:TPU:0 now
where the time goes in v5:
time: 47 us; the launch traced here: 46.7 us
  blocking collectives  18.7 us (40%)
  waiting for transfers between devices  11.5 us (24%)
  starting transfers between devices  11.3 us (24%)
  local copies, waits for them, and re-layouts  2.47 us (5%)
  Pallas kernels  1.96 us (4%)
  other arithmetic  0.6 us (1%)
    all_to_all x1, blocking collectives, local_home(): lax.all_to_all(states[0], 'chain', split_axis=0, concat_axis=0, tiled=True)  18.7 us
    ppermute x8, waiting for transfers between devices, permute(): return lax.ppermute(value, ('chain', 'clus'), pairs)  11.5 us
    ppermute x8, starting transfers between devices, permute(): return lax.ppermute(value, ('chain', 'clus'), pairs)  11.3 us
    unnamed x6, local copies, waits for them, and re-layouts  2.46 us
    pallas_call x1, Pallas kernels, local_home(): pl.pallas_call(functools.partial(send_kernel, run_slots, rows // clus_len...  1.32 us
  transfers between devices with their start and end apart: 8, of which 3 were waited for; matrix products, arithmetic and copies ran while one was open for 0% of the time, Pallas kernels for 0%

profile of v5, /device:TPU:0, one launch (start us, length us, event | category | flops | bytes accessed | tf_op | source)
XLA Modules:
  0.0 46.7 jit_solution(8310996023480444901)
XLA Ops:
  0.0 0.0 copy-start
  0.0 1.1 %copy-done = bf16[512,768]{1,0:T(8,128)(2,1)S(1)} copy-done((bf16[512,768]{1,0:T(8,128)(2,1)S(1)}, bf16[512,768]{1,0:T(8,128)(2,1)}, u32[]{:S(2)}) %copy-start) | copy-done | bytes 786456
  1.1 0.0 copy-start.1
  1.1 0.7 %copy-done.1 = s32[512]{0:T(512)S(1)} copy-done((s32[512]{0:T(512)S(1)}, s32[512]{0:T(512)}, u32[]{:S(2)}) %copy-start.1) | copy-done | bytes 2072
  1.8 1.3 %send_blocks.1 = (bf16[256,768]{1,0:T(8,128)(2,1)S(1)}, f32[8,256]{1,0:T(8,128)S(1)}, bf16[264,768]{1,0:T(8,128)(2,1)S(1)}) custom-call(s32[1,512]{1,0:T(1,128)S(1)} %bitcast.4, bf16[512,768]{1,0:T(8,128)(2,1)S(1)} %copy-done), custom_call_target="tpu_custom_call" | custom-call | tf_op jit(solution)/shard_map/send_blocks/pallas_call | solution.py:320
  3.1 0.5 %collective-permute-start = (bf16[264,768]{1,0:T(8,128)(2,1)S(1)}, bf16[264,768]{1,0:T(8,128)(2,1)S(1)}, u32[]{:S(2)}, u32[]{:S(2)}) collective-permute-start(bf16[264,768]{1,0:T(8,128)(2,1)S(1)} %get-tuple-element.42), channel_id=1, source_target_pairs={{0,1},{1,0},{2,3},{3,2},{4,5},{5,4},{6,7},{7,6},{8,9},{9,8},{10,11... | collective-permute-start | bytes 1216520 | tf_op jit(solution)/shard_map/ppermute | solution.py:340
  3.7 1.4 %collective-permute-done.came_ref = bf16[264,768]{1,0:T(8,128)(2,1)S(1)} collective-permute-done((bf16[264,768]{1,0:T(8,128)(2,1)S(1)}, bf16[264,768]{1,0:T(8,128)(2,1)S(1)}, u32[]{:S(2)}, u32[]{:S(2)}) %collective-permute-start) | collective-permute-done | bytes 405536 | tf_op jit(solution)/shard_map/ppermute | solution.py:340
  5.0 0.1 merge_blocks.1
  5.1 5.6 %collective-permute-start.2 = (bf16[264,768]{1,0:T(8,128)(2,1)S(1)}, bf16[264,768]{1,0:T(8,128)(2,1)S(1)}, u32[]{:S(2)}, u32[]{:S(2)}) collective-permute-start(bf16[264,768]{1,0:T(8,128)(2,1)S(1)} %get-tuple-element.44), channel_id=1, source_target_pairs={{0,9},{2,11},{13,4},{15,6},{16,25},{18,27},{29,20},{31,22}} | collective-permute-start | bytes 1216520 | tf_op jit(solution)/shard_map/ppermute | solution.py:340
  10.7 0.7 %collective-permute-start.1 = (bf16[264,768]{1,0:T(8,128)(2,1)S(1)}, bf16[264,768]{1,0:T(8,128)(2,1)S(1)}, u32[]{:S(2)}, u32[]{:S(2)}) collective-permute-start(bf16[264,768]{1,0:T(8,128)(2,1)S(1)} %get-tuple-element.43.rest_0_.rest_1_), channel_id=1, source_target_pairs={{5,6},{7,4},{8,11},{10,9},{21,22},{23,20},{24,27},{26,25}} | collective-permute-start | bytes 1216520 | tf_op jit(solution)/shard_map/ppermute | solution.py:340
  11.4 0.7 %collective-permute-start.3 = (bf16[264,768]{1,0:T(8,128)(2,1)S(1)}, bf16[264,768]{1,0:T(8,128)(2,1)S(1)}, u32[]{:S(2)}, u32[]{:S(2)}) collective-permute-start(bf16[264,768]{1,0:T(8,128)(2,1)S(1)} %get-tuple-element.44), channel_id=1, source_target_pairs={{1,11},{3,9},{12,6},{14,4},{17,27},{19,25},{28,22},{30,20}} | collective-permute-start | bytes 1216520 | tf_op jit(solution)/shard_map/ppermute | solution.py:340
  12.1 1.7 %collective-permute-start.4 = (bf16[264,768]{1,0:T(8,128)(2,1)S(1)}, bf16[264,768]{1,0:T(8,128)(2,1)S(1)}, u32[]{:S(2)}, u32[]{:S(2)}) collective-permute-start(bf16[264,768]{1,0:T(8,128)(2,1)S(1)} %get-tuple-element.43.rest_0_.rest_1_), channel_id=1, source_target_pairs={{0,4},{2,6},{13,9},{15,11},{16,20},{18,22},{29,25},{31,27}} | collective-permute-start | bytes 1216520 | tf_op jit(solution)/shard_map/ppermute | solution.py:340
  13.9 0.7 %collective-permute-start.6 = (bf16[264,768]{1,0:T(8,128)(2,1)S(1)}, bf16[264,768]{1,0:T(8,128)(2,1)S(1)}, u32[]{:S(2)}, u32[]{:S(2)}) collective-permute-start(bf16[264,768]{1,0:T(8,128)(2,1)S(1)} %get-tuple-element.44), channel_id=1, source_target_pairs={{4,9},{6,11},{9,4},{11,6},{20,25},{22,27},{25,20},{27,22}} | collective-permute-start | bytes 1216520 | tf_op jit(solution)/shard_map/ppermute | solution.py:340
  14.6 2.9 %collective-permute-done.2.rest_2_.rest_3_ = bf16[264,768]{1,0:T(8,128)(2,1)S(1)} collective-permute-done((bf16[264,768]{1,0:T(8,128)(2,1)S(1)}, bf16[264,768]{1,0:T(8,128)(2,1)S(1)}, u32[]{:S(2)}, u32[]{:S(2)}) %collective-permute-start.2) | collective-permute-done | bytes 405536 | tf_op jit(solution)/shard_map/ppermute | solution.py:340
  17.4 0.7 %collective-permute-start.5 = (bf16[264,768]{1,0:T(8,128)(2,1)S(1)}, bf16[264,768]{1,0:T(8,128)(2,1)S(1)}, u32[]{:S(2)}, u32[]{:S(2)}) collective-permute-start(bf16[264,768]{1,0:T(8,128)(2,1)S(1)} %get-tuple-element.43.rest_0_.rest_1_), channel_id=1, source_target_pairs={{1,6},{3,4},{12,11},{14,9},{17,22},{19,20},{28,27},{30,25}} | collective-permute-start | bytes 1216520 | tf_op jit(solution)/shard_map/ppermute | solution.py:340
  18.1 0.0 collective-permute-done.1.rest_1_.rest_2_
  18.1 0.7 %collective-permute-start.7 = (bf16[264,768]{1,0:T(8,128)(2,1)S(1)}, bf16[264,768]{1,0:T(8,128)(2,1)S(1)}, u32[]{:S(2)}, u32[]{:S(2)}) collective-permute-start(bf16[264,768]{1,0:T(8,128)(2,1)S(1)} %get-tuple-element.44), channel_id=1, source_target_pairs={{5,11},{7,9},{8,6},{10,4},{21,27},{23,25},{24,22},{26,20}} | collective-permute-start | bytes 1216520 | tf_op jit(solution)/shard_map/ppermute | solution.py:340
  18.9 0.0 collective-permute-done.3.rest_3_.rest_4_
  18.9 7.3 %collective-permute-done.4.rest_4_.rest_5_ = bf16[264,768]{1,0:T(8,128)(2,1)S(1)} collective-permute-done((bf16[264,768]{1,0:T(8,128)(2,1)S(1)}, bf16[264,768]{1,0:T(8,128)(2,1)S(1)}, u32[]{:S(2)}, u32[]{:S(2)}) %collective-permute-start.4) | collective-permute-done | bytes 405536 | tf_op jit(solution)/shard_map/ppermute | solution.py:340
  26.1 0.0 collective-permute-done.6.rest_6_.rest_7_
  26.1 0.0 collective-permute-done.5.rest_5_.rest_6_
  26.1 0.0 collective-permute-done.7.rest_8_
  26.1 0.0 copy-start.2
  26.2 0.6 %copy-done.2 = s32[4]{0:T(128)S(1)} copy-done((s32[4]{0:T(128)S(1)}, s32[4]{0:T(128)}, u32[]{:S(2)}) %copy-start.2) | copy-done | bytes 40
  26.8 0.6 %multiply_last.1 = f32[4,512]{1,0:T(4,128)S(1)} custom-call(s32[4]{0:T(128)S(1)} %copy-done.2, bf16[264,768]{1,0:T(8,128)(2,1)S(1)} %get-tuple-element.43.rest_0_.rest_1_, bf16[264,768]{1,0:T(8,128)(2,1)S(1)} %collective-permute-done.1.rest_1_.rest_2_, bf16[264,768]{1,0:T(8,128)(2,1)S(1)} %collective-permute-done.2.rest_2_.rest_3_, ...), custom_call_target="tpu_custom_call" | custom-call | tf_op jit(solution)/shard_map/multiply_last/pallas_call | solution.py:377
  27.4 18.7 %all_to_all.9 = f32[4,1,512]{2,1,0:T(1,128)S(1)} all-to-all(f32[4,1,512]{2,1,0:T(1,128)S(1)} %copy.4), channel_id=1, replica_groups=mesh['groups'=2,'chain'=4,'clus'=4] {'chain'}, dimensions={0} | all-to-all | bytes 16384 | tf_op jit(solution)/shard_map/all_to_all | solution.py:386
  46.1 0.6 %reduce_sum.9 = f32[512]{0:T(512)} reduce(f32[4,1,512]{2,1,0:T(1,128)S(1)} %all_to_all.9, f32[]{:T(128)} %constant.0.clone.1), dimensions={0,1}, to_apply=%region_0.0 | reduce | flops 1536 | bytes 10244 | tf_op jit(solution)/shard_map/reduce_sum | solution.py:387
  (4 shorter events, 0.0 us)
Async XLA Ops:
  0.0 1.1 %copy-start = (bf16[512,768]{1,0:T(8,128)(2,1)S(1)}, bf16[512,768]{1,0:T(8,128)(2,1)}, u32[]{:S(2)}) copy-start(bf16[512,768]{1,0:T(8,128)(2,1)} %rows_hbm.1) | copy-start | bytes 2359300
  1.1 0.7 %copy-start.1 = (s32[512]{0:T(512)S(1)}, s32[512]{0:T(512)}, u32[]{:S(2)}) copy-start(s32[512]{0:T(512)} %param.4) | copy-start | bytes 6148
  3.1 1.9 %collective-permute-start = (bf16[264,768]{1,0:T(8,128)(2,1)S(1)}, bf16[264,768]{1,0:T(8,128)(2,1)S(1)}, u32[]{:S(2)}, u32[]{:S(2)}) collective-permute-start(bf16[264,768]{1,0:T(8,128)(2,1)S(1)} %get-tuple-element.42), channel_id=1, source_target_pairs={{0,1},{1,0},{2,3},{3,2},{4,5},{5,4},{6,7},{7,6},{8,9},{9,8},{10,11... | collective-permute-start | bytes 1216520 | tf_op jit(solution)/shard_map/ppermute | solution.py:340
  5.1 12.4 %collective-permute-start.2 = (bf16[264,768]{1,0:T(8,128)(2,1)S(1)}, bf16[264,768]{1,0:T(8,128)(2,1)S(1)}, u32[]{:S(2)}, u32[]{:S(2)}) collective-permute-start(bf16[264,768]{1,0:T(8,128)(2,1)S(1)} %get-tuple-element.44), channel_id=1, source_target_pairs={{0,9},{2,11},{13,4},{15,6},{16,25},{18,27},{29,20},{31,22}} | collective-permute-start | bytes 1216520 | tf_op jit(solution)/shard_map/ppermute | solution.py:340
  10.7 7.4 %collective-permute-start.1 = (bf16[264,768]{1,0:T(8,128)(2,1)S(1)}, bf16[264,768]{1,0:T(8,128)(2,1)S(1)}, u32[]{:S(2)}, u32[]{:S(2)}) collective-permute-start(bf16[264,768]{1,0:T(8,128)(2,1)S(1)} %get-tuple-element.43.rest_0_.rest_1_), channel_id=1, source_target_pairs={{5,6},{7,4},{8,11},{10,9},{21,22},{23,20},{24,27},{26,25}} | collective-permute-start | bytes 1216520 | tf_op jit(solution)/shard_map/ppermute | solution.py:340
  11.4 7.4 %collective-permute-start.3 = (bf16[264,768]{1,0:T(8,128)(2,1)S(1)}, bf16[264,768]{1,0:T(8,128)(2,1)S(1)}, u32[]{:S(2)}, u32[]{:S(2)}) collective-permute-start(bf16[264,768]{1,0:T(8,128)(2,1)S(1)} %get-tuple-element.44), channel_id=1, source_target_pairs={{1,11},{3,9},{12,6},{14,4},{17,27},{19,25},{28,22},{30,20}} | collective-permute-start | bytes 1216520 | tf_op jit(solution)/shard_map/ppermute | solution.py:340
  12.1 14.0 %collective-permute-start.4 = (bf16[264,768]{1,0:T(8,128)(2,1)S(1)}, bf16[264,768]{1,0:T(8,128)(2,1)S(1)}, u32[]{:S(2)}, u32[]{:S(2)}) collective-permute-start(bf16[264,768]{1,0:T(8,128)(2,1)S(1)} %get-tuple-element.43.rest_0_.rest_1_), channel_id=1, source_target_pairs={{0,4},{2,6},{13,9},{15,11},{16,20},{18,22},{29,25},{31,27}} | collective-permute-start | bytes 1216520 | tf_op jit(solution)/shard_map/ppermute | solution.py:340
  13.9 12.3 %collective-permute-start.6 = (bf16[264,768]{1,0:T(8,128)(2,1)S(1)}, bf16[264,768]{1,0:T(8,128)(2,1)S(1)}, u32[]{:S(2)}, u32[]{:S(2)}) collective-permute-start(bf16[264,768]{1,0:T(8,128)(2,1)S(1)} %get-tuple-element.44), channel_id=1, source_target_pairs={{4,9},{6,11},{9,4},{11,6},{20,25},{22,27},{25,20},{27,22}} | collective-permute-start | bytes 1216520 | tf_op jit(solution)/shard_map/ppermute | solution.py:340
  17.4 8.7 %collective-permute-start.5 = (bf16[264,768]{1,0:T(8,128)(2,1)S(1)}, bf16[264,768]{1,0:T(8,128)(2,1)S(1)}, u32[]{:S(2)}, u32[]{:S(2)}) collective-permute-start(bf16[264,768]{1,0:T(8,128)(2,1)S(1)} %get-tuple-element.43.rest_0_.rest_1_), channel_id=1, source_target_pairs={{1,6},{3,4},{12,11},{14,9},{17,22},{19,20},{28,27},{30,25}} | collective-permute-start | bytes 1216520 | tf_op jit(solution)/shard_map/ppermute | solution.py:340
  18.1 8.0 %collective-permute-start.7 = (bf16[264,768]{1,0:T(8,128)(2,1)S(1)}, bf16[264,768]{1,0:T(8,128)(2,1)S(1)}, u32[]{:S(2)}, u32[]{:S(2)}) collective-permute-start(bf16[264,768]{1,0:T(8,128)(2,1)S(1)} %get-tuple-element.44), channel_id=1, source_target_pairs={{5,11},{7,9},{8,6},{10,4},{21,27},{23,25},{24,22},{26,20}} | collective-permute-start | bytes 1216520 | tf_op jit(solution)/shard_map/ppermute | solution.py:340
  26.1 0.7 %copy-start.2 = (s32[4]{0:T(128)S(1)}, s32[4]{0:T(128)}, u32[]{:S(2)}) copy-start(s32[4]{0:T(128)} %rest_0_.1) | copy-start | bytes 52

commit v6 on v5

--- a/solution.py
+++ b/solution.py
@@ -12,7 +12,6 @@
 PIECE = 16
 VMEM = pl.BlockSpec(memory_space=pltpu.VMEM)
 SMEM = pl.BlockSpec(memory_space=pltpu.SMEM)
-HBM = pl.BlockSpec(memory_space=pltpu.HBM)
 
 
 def as_bf16(mask):
@@ -167,12 +166,7 @@
     return lax.ppermute(found, ("chain", "clus"), pairs)
 
 
-def send_kernel(run_slots, cluster_runs, dest_hbm, rows_hbm, kept_ref, slots_ref, given_ref, *scratch):
-    dest_ref, rows_ref, sems = scratch
-    dest_copy = pltpu.make_async_copy(dest_hbm, dest_ref, sems.at[0])
-    rows_copy = pltpu.make_async_copy(rows_hbm, rows_ref, sems.at[1])
-    dest_copy.start()
-    rows_copy.start()
+def send_kernel(run_slots, cluster_runs, dest_ref, rows_ref, kept_ref, slots_ref, given_ref):
     rows, width = rows_ref.shape
     runs = rows // PIECE
     half = rows // 2
@@ -183,7 +177,6 @@
     before = lax.broadcasted_iota(jnp.int32, (rows, rows), 0) < lax.broadcasted_iota(
         jnp.int32, (rows, rows), 1
     )
-    dest_copy.wait()
     dest = dest_ref[...]
     run = lax.div(dest, run_slots)
     within = lax.rem(dest, run_slots)
@@ -198,7 +191,6 @@
         (((1,), (1,)), ((), ())),
         preferred_element_type=jnp.float32,
     )
-    rows_copy.wait()
     x = rows_ref[...].astype(jnp.float32)
     units = (x * lax.rsqrt(jnp.sum(x * x, axis=1, keepdims=True) + 1e-06)).astype(jnp.bfloat16)
     for low, ref in ((0, kept_ref), (half, given_ref)):
@@ -229,11 +221,15 @@
 
 
 def stage_kernel(run_slots, old, new, last, *rest):
-    sizes_ref, rest = (rest[0], rest[1:]) if last else (None, rest)
+    first = old == 0
+    count_ref, rest = (rest[0], rest[1:]) if first or last else (None, rest)
     refs, rest = rest[: old + new], rest[old + new :]
     old_states, rest = rest[: 2 * old], rest[2 * old :]
-    outs = rest[: 1 if last else 2 * (old + new)]
-    states = rest[len(outs) :] if last else outs
+    if last:
+        chunk_refs = rest[: -1 - 2 * (old + new)]
+        states, found_ref = rest[len(chunk_refs) : -1], rest[-1]
+    else:
+        states = rest[: 2 * (old + new)]
     rows = refs[0].shape[0] - TILE
     depth = rows // 2
     runs = depth // PIECE
@@ -244,6 +240,10 @@
         for low in range(LANES, value.shape[1], LANES):
             best = jnp.maximum(best, value[:, low : low + LANES])
         return best
+
+    if first:
+        members = count_ref[lax.axis_index("clus")].astype(jnp.float32)
+        rest[-1][...] = jnp.full_like(rest[-1], members)
 
     @pl.when(is_home)
     def _():
@@ -280,16 +280,16 @@
             states[2 * index + 1][...] = halves(jnp.where(diagonal, best, -2.0))
 
     if last:
-        (out_ref,) = outs
-        chunk = out_ref.shape[1]
+        chunk = found_ref.shape[1]
 
         @pl.when(jnp.logical_not(is_home))
         def _():
-            out_ref[...] = jnp.zeros_like(out_ref)
+            for ref in chunk_refs:
+                ref[...] = jnp.zeros_like(ref)
 
         @pl.when(is_home)
         def _():
-            members = sizes_ref[lax.axis_index("clus")]
+            members = jnp.concatenate([count_ref[0:1, :]] * (run_slots // LANES), axis=1)
             lane = lax.broadcasted_iota(jnp.int32, (run_slots, run_slots), 1)
             for run in range(runs):
                 where = [
@@ -302,12 +302,19 @@
                 best = jnp.max(best, axis=1, keepdims=True)
                 place = jnp.concatenate([place] * (run_slots // LANES), axis=1)
                 base = run * run_slots
-                found = jnp.where(place == (lane + base).astype(jnp.float32), best, 0.0)
-                found = jnp.sum(found, axis=0, keepdims=True)
-                position = base + lax.broadcasted_iota(jnp.int32, (1, run_slots), 1)
-                found = jnp.where(position < members, found, 0.0)
+                position = (lane + base).astype(jnp.float32)
+                found = jnp.sum(jnp.where(place == position, best, 0.0), axis=0, keepdims=True)
+                found = jnp.where(position[0:1] < members, found, 0.0)
                 row, low = base // chunk, base % chunk
-                out_ref[row : row + 1, low : low + run_slots] = found
+                found_ref[row : row + 1, low : low + run_slots] = found
+
+        chain_len = len(chunk_refs)
+        for home in (chain_len // 2 - 1, chain_len // 2):
+            @pl.when(lax.axis_index("chain") == home)
+            def _():
+                for step, ref in enumerate(chunk_refs):
+                    row = (home + step) % chain_len
+                    ref[...] = jnp.where(is_home, found_ref[row : row + 1, :], 0.0)
 
 
 def local_home(embeddings, dest, sizes):
@@ -324,13 +331,8 @@
             jax.ShapeDtypeStruct((TILE, half), jnp.float32),
             block,
         ),
-        in_specs=[HBM, HBM],
+        in_specs=[VMEM, VMEM],
         out_specs=(VMEM, VMEM, VMEM),
-        scratch_shapes=[
-            pltpu.VMEM((1, rows), jnp.int32),
-            pltpu.VMEM((rows, width), jnp.bfloat16),
-            pltpu.SemaphoreType.DMA((2,)),
-        ],
         compiler_params=pltpu.CompilerParams(vmem_limit_bytes=32 * 2**20),
         name="send_blocks",
     )(dest.reshape(1, rows), embeddings)
@@ -361,30 +363,42 @@
     nearer, farther = [(0, low), (top, high)], [(0, high), (top, low)]
     middle, plane = [(low, high), (high, low)], [(low, low), (high, high)]
     stages = [
-        [near, to_home(near, plane, 1), to_home(far, farther, 0)],
-        [to_home(far, farther, 1), to_home(near, nearer, 0)],
-        [to_home(near, nearer, 1), to_home(far, middle, 0)],
+        [near, to_home(far, farther, 0), to_home(near, nearer, 0)],
+        [to_home(far, farther, 1), to_home(near, nearer, 1)],
+        [to_home(far, middle, 0), to_home(near, plane, 1)],
         [to_home(far, middle, 1)],
     ]
     blocks, states = [], []
     state = jax.ShapeDtypeStruct((half, LANES), jnp.float32)
+    chunk = jax.ShapeDtypeStruct((1, rows), jnp.float32)
     for number, arrived in enumerate(stages):
-        last = number == len(stages) - 1
+        first, last = number == 0, number == len(stages) - 1
         old, new = len(blocks), len(arrived)
         blocks = blocks + arrived
-        count = 2 * len(blocks)
-        outs = (jax.ShapeDtypeStruct((chain_len, rows), jnp.float32),) if last else (state,) * count
+        outs = (chunk,) * chain_len if last else (state,) * (2 * len(blocks))
+        outs += (jax.ShapeDtypeStruct((TILE, LANES), jnp.float32),) * first
+        scratch = [pltpu.VMEM(state.shape, state.dtype)] * (2 * len(blocks))
+        scratch.append(pltpu.VMEM((chain_len, rows), jnp.float32))
+        count = [sizes] if first else [members] if last else []
         states = pl.pallas_call(
             functools.partial(stage_kernel, run_slots, old, new, last),
             out_shape=outs,
-            in_specs=[SMEM] * last + [VMEM] * (len(blocks) + len(states)),
+            in_specs=[SMEM] * first + [VMEM] * (last + len(blocks) + len(states)),
             out_specs=(VMEM,) * len(outs),
-            scratch_shapes=[pltpu.VMEM(state.shape, jnp.float32)] * (count if last else 0),
+            scratch_shapes=scratch * last,
             compiler_params=pltpu.CompilerParams(vmem_limit_bytes=32 * 2**20),
             name="multiply_last" if last else "multiply_arrived",
-        )(*([sizes] if last else []), *blocks, *states)
-    found = lax.all_to_all(states[0], "chain", split_axis=0, concat_axis=0, tiled=True)
-    return jnp.sum(found, axis=0, keepdims=True)
+        )(*count, *blocks, *states)
+        if first:
+            *states, members = states
+    found = states[0]
+    for step in range(1, chain_len):
+        moves = []
+        for k in range(clus_len):
+            home = low + k % 2
+            moves.append((home, k, (home + step) % chain_len, k))
+        found = found + permute(states[step], moves)
+    return found
 
 
 def solution(mesh):

time: 47 us -> 46.9 us (level)
  blocking collectives: 18.7 us -> 0 us
  waiting for transfers between devices: 11.5 us -> 28.7 us
  starting transfers between devices: 11.3 us -> 13.5 us
  local copies, waits for them, and re-layouts: 2.47 us -> 1.82 us
    all_to_all x1 -> x0, blocking collectives: 18.7 us -> none  [local_home(): lax.all_to_all(states[0], 'chain', split_axis=0, concat_axis=0, tiled=True)]
    ppermute x8 -> x11, waiting for transfers between devices: 11.5 us -> 28.7 us  [permute(): return lax.ppermute(value, ('chain', 'clus'), pairs)]
    ppermute x8 -> x11, starting transfers between devices: 11.3 us -> 13.5 us  [permute(): return lax.ppermute(value, ('chain', 'clus'), pairs)]
    unnamed x6, local copies, waits for them, and re-layouts: 2.46 us -> 1.82 us
    reduce_sum x1 -> x0, other arithmetic: 0.6 us -> none  [local_home(): return jnp.sum(found, axis=0, keepdims=True)]
    add x0 -> x1, other arithmetic: none -> 0.58 us  [local_home(): found = found + permute(states[step], moves)]
  transfers between devices with their start and end apart: 8 -> 11, of which waited for: 3 -> 4; matrix products, arithmetic and copies ran while one was open for 0% -> 0% of each run, Pallas kernels for 0% -> 1%
where the time goes in v6:
time: 46.9 us; the launch traced here: 46.6 us
  waiting for transfers between devices  28.7 us (61%)
  starting transfers between devices  13.5 us (29%)
  local copies, waits for them, and re-layouts  1.82 us (4%)
  Pallas kernels  1.79 us (4%)
  other arithmetic  0.58 us (1%)
    ppermute x11, waiting for transfers between devices, permute(): return lax.ppermute(value, ('chain', 'clus'), pairs)  28.7 us
    ppermute x11, starting transfers between devices, permute(): return lax.ppermute(value, ('chain', 'clus'), pairs)  13.5 us
    unnamed x6, local copies, waits for them, and re-layouts  1.82 us
    pallas_call x1, Pallas kernels, local_home(): pl.pallas_call(functools.partial(send_kernel, run_slots, rows // clus_len...  1.04 us
  transfers between devices with their start and end apart: 11, of which 4 were waited for; matrix products, arithmetic and copies ran while one was open for 0% of the time, Pallas kernels for 1%

profile of v6, /device:TPU:0, one launch (start us, length us, event | category | flops | bytes accessed | tf_op | source)
XLA Modules:
  0.0 46.6 jit_solution(7799962544815682531)
XLA Ops:
  0.0 0.0 copy-start
  0.0 1.1 %copy-done = bf16[512,768]{1,0:T(8,128)(2,1)S(1)} copy-done((bf16[512,768]{1,0:T(8,128)(2,1)S(1)}, bf16[512,768]{1,0:T(8,128)(2,1)}, u32[]{:S(2)}) %copy-start) | copy-done | bytes 786456
  1.1 0.0 copy-start.1
  1.1 0.7 %copy-done.1 = s32[512]{0:T(512)S(1)} copy-done((s32[512]{0:T(512)S(1)}, s32[512]{0:T(512)}, u32[]{:S(2)}) %copy-start.1) | copy-done | bytes 2072
  1.8 1.0 %send_blocks.1 = (bf16[256,768]{1,0:T(8,128)(2,1)S(1)}, f32[8,256]{1,0:T(8,128)S(1)}, bf16[264,768]{1,0:T(8,128)(2,1)S(1)}) custom-call(s32[1,512]{1,0:T(1,128)S(1)} %bitcast.1, bf16[512,768]{1,0:T(8,128)(2,1)S(1)} %copy-done), custom_call_target="tpu_custom_call" | custom-call | tf_op jit(solution)/shard_map/send_blocks/pallas_call | solution.py:327
  2.9 0.5 %collective-permute-start = (bf16[264,768]{1,0:T(8,128)(2,1)S(1)}, bf16[264,768]{1,0:T(8,128)(2,1)S(1)}, u32[]{:S(2)}, u32[]{:S(2)}) collective-permute-start(bf16[264,768]{1,0:T(8,128)(2,1)S(1)} %get-tuple-element.47), channel_id=1, source_target_pairs={{0,1},{1,0},{2,3},{3,2},{4,5},{5,4},{6,7},{7,6},{8,9},{9,8},{10,11... | collective-permute-start | bytes 1216520 | tf_op jit(solution)/shard_map/ppermute | solution.py:342
  3.4 1.4 %collective-permute-done.came_ref = bf16[264,768]{1,0:T(8,128)(2,1)S(1)} collective-permute-done((bf16[264,768]{1,0:T(8,128)(2,1)S(1)}, bf16[264,768]{1,0:T(8,128)(2,1)S(1)}, u32[]{:S(2)}, u32[]{:S(2)}) %collective-permute-start) | collective-permute-done | bytes 405536 | tf_op jit(solution)/shard_map/ppermute | solution.py:342
  4.7 0.1 merge_blocks.1
  4.8 0.0 copy-start.2
  4.8 5.6 %collective-permute-start.1 = (bf16[264,768]{1,0:T(8,128)(2,1)S(1)}, bf16[264,768]{1,0:T(8,128)(2,1)S(1)}, u32[]{:S(2)}, u32[]{:S(2)}) collective-permute-start(bf16[264,768]{1,0:T(8,128)(2,1)S(1)} %get-tuple-element.49), channel_id=1, source_target_pairs={{0,9},{2,11},{13,4},{15,6},{16,25},{18,27},{29,20},{31,22}} | collective-permute-start | bytes 1216520 | tf_op jit(solution)/shard_map/ppermute | solution.py:342
  10.5 1.3 %collective-permute-start.2 = (bf16[264,768]{1,0:T(8,128)(2,1)S(1)}, bf16[264,768]{1,0:T(8,128)(2,1)S(1)}, u32[]{:S(2)}, u32[]{:S(2)}) collective-permute-start(bf16[264,768]{1,0:T(8,128)(2,1)S(1)} %get-tuple-element.48.rest_1_.rest_0_), channel_id=1, source_target_pairs={{0,4},{2,6},{13,9},{15,11},{16,20},{18,22},{29,25},{31,27}} | collective-permute-start | bytes 1216520 | tf_op jit(solution)/shard_map/ppermute | solution.py:342
  11.8 0.7 %collective-permute-start.3 = (bf16[264,768]{1,0:T(8,128)(2,1)S(1)}, bf16[264,768]{1,0:T(8,128)(2,1)S(1)}, u32[]{:S(2)}, u32[]{:S(2)}) collective-permute-start(bf16[264,768]{1,0:T(8,128)(2,1)S(1)} %get-tuple-element.49), channel_id=1, source_target_pairs={{1,11},{3,9},{12,6},{14,4},{17,27},{19,25},{28,22},{30,20}} | collective-permute-start | bytes 1216520 | tf_op jit(solution)/shard_map/ppermute | solution.py:342
  12.5 0.7 %collective-permute-start.4 = (bf16[264,768]{1,0:T(8,128)(2,1)S(1)}, bf16[264,768]{1,0:T(8,128)(2,1)S(1)}, u32[]{:S(2)}, u32[]{:S(2)}) collective-permute-start(bf16[264,768]{1,0:T(8,128)(2,1)S(1)} %get-tuple-element.48.rest_1_.rest_0_), channel_id=1, source_target_pairs={{1,6},{3,4},{12,11},{14,9},{17,22},{19,20},{28,27},{30,25}} | collective-permute-start | bytes 1216520 | tf_op jit(solution)/shard_map/ppermute | solution.py:342
  13.2 0.7 %collective-permute-start.5 = (bf16[264,768]{1,0:T(8,128)(2,1)S(1)}, bf16[264,768]{1,0:T(8,128)(2,1)S(1)}, u32[]{:S(2)}, u32[]{:S(2)}) collective-permute-start(bf16[264,768]{1,0:T(8,128)(2,1)S(1)} %get-tuple-element.49), channel_id=1, source_target_pairs={{4,9},{6,11},{9,4},{11,6},{20,25},{22,27},{25,20},{27,22}} | collective-permute-start | bytes 1216520 | tf_op jit(solution)/shard_map/ppermute | solution.py:342
  13.9 3.3 %collective-permute-done.1.rest_2_.rest_1_ = bf16[264,768]{1,0:T(8,128)(2,1)S(1)} collective-permute-done((bf16[264,768]{1,0:T(8,128)(2,1)S(1)}, bf16[264,768]{1,0:T(8,128)(2,1)S(1)}, u32[]{:S(2)}, u32[]{:S(2)}) %collective-permute-start.1) | collective-permute-done | bytes 405536 | tf_op jit(solution)/shard_map/ppermute | solution.py:342
  17.2 0.7 %collective-permute-start.6 = (bf16[264,768]{1,0:T(8,128)(2,1)S(1)}, bf16[264,768]{1,0:T(8,128)(2,1)S(1)}, u32[]{:S(2)}, u32[]{:S(2)}) collective-permute-start(bf16[264,768]{1,0:T(8,128)(2,1)S(1)} %get-tuple-element.48.rest_1_.rest_0_), channel_id=1, source_target_pairs={{5,6},{7,4},{8,11},{10,9},{21,22},{23,20},{24,27},{26,25}} | collective-permute-start | bytes 1216520 | tf_op jit(solution)/shard_map/ppermute | solution.py:342
  17.8 8.0 %collective-permute-done.2.rest_3_.rest_2_ = bf16[264,768]{1,0:T(8,128)(2,1)S(1)} collective-permute-done((bf16[264,768]{1,0:T(8,128)(2,1)S(1)}, bf16[264,768]{1,0:T(8,128)(2,1)S(1)}, u32[]{:S(2)}, u32[]{:S(2)}) %collective-permute-start.2) | collective-permute-done | bytes 405536 | tf_op jit(solution)/shard_map/ppermute | solution.py:342
  25.8 0.7 %collective-permute-start.7 = (bf16[264,768]{1,0:T(8,128)(2,1)S(1)}, bf16[264,768]{1,0:T(8,128)(2,1)S(1)}, u32[]{:S(2)}, u32[]{:S(2)}) collective-permute-start(bf16[264,768]{1,0:T(8,128)(2,1)S(1)} %get-tuple-element.49), channel_id=1, source_target_pairs={{5,11},{7,9},{8,6},{10,4},{21,27},{23,25},{24,22},{26,20}} | collective-permute-start | bytes 1216520 | tf_op jit(solution)/shard_map/ppermute | solution.py:342
  26.5 0.0 copy-done.2
  26.5 0.6 %multiply_arrived.3 = (f32[256,128]{1,0:T(8,128)S(1)}, f32[256,128]{1,0:T(8,128)S(1)}, f32[256,128]{1,0:T(8,128)S(1)}, f32[256,128]{1,0:T(8,128)S(1)}, f32[256,1...) custom-call(s32[4]{0:T(128)S(1)} %copy-done.2, ...), custom_call_target="tpu_custom_call" | custom-call | tf_op jit(solution)/shard_map/multiply_arrived/pallas_call | solution.py:383
  27.1 0.0 collective-permute-done.3.rest_3_.rest_4_
  27.1 0.0 collective-permute-done.4.rest_4_.rest_5_
  27.2 0.0 collective-permute-done.5.rest_5_.rest_6_
  27.2 0.0 collective-permute-done.6.rest_6_.rest_7_
  27.2 0.1 multiply_arrived.5
  27.2 0.0 collective-permute-done.7.rest_8_
  27.3 0.1 multiply_last.1
  27.3 0.7 %collective-permute-start.8 = (f32[1,512]{1,0:T(1,128)S(1)}, f32[1,512]{1,0:T(1,128)S(1)}, u32[]{:S(2)}, u32[]{:S(2)}) collective-permute-start(f32[1,512]{1,0:T(1,128)S(1)} %get-tuple-element.82), channel_id=1, source_target_pairs={{4,8},{9,13},{6,10},{11,15},{20,24},{25,29},{22,26},{27,31}} | collective-permute-start | bytes 6152 | tf_op jit(solution)/shard_map/ppermute | solution.py:342
  28.0 0.7 %collective-permute-start.9 = (f32[1,512]{1,0:T(1,128)S(1)}, f32[1,512]{1,0:T(1,128)S(1)}, u32[]{:S(2)}, u32[]{:S(2)}) collective-permute-start(f32[1,512]{1,0:T(1,128)S(1)} %get-tuple-element.83), channel_id=1, source_target_pairs={{4,12},{9,1},{6,14},{11,3},{20,28},{25,17},{22,30},{27,19}} | collective-permute-start | bytes 6152 | tf_op jit(solution)/shard_map/ppermute | solution.py:342
  28.7 1.3 %collective-permute-start.10 = (f32[1,512]{1,0:T(1,128)S(1)}, f32[1,512]{1,0:T(1,128)S(1)}, u32[]{:S(2)}, u32[]{:S(2)}) collective-permute-start(f32[1,512]{1,0:T(1,128)S(1)} %get-tuple-element.84), channel_id=1, source_target_pairs={{4,0},{9,5},{6,2},{11,7},{20,16},{25,21},{22,18},{27,23}} | collective-permute-start | bytes 6152 | tf_op jit(solution)/shard_map/ppermute | solution.py:342
  30.0 0.0 collective-permute-done.8
  30.0 0.0 collective-permute-done.9
  30.0 16.0 %collective-permute-done.10 = f32[1,512]{1,0:T(1,128)S(1)} collective-permute-done((f32[1,512]{1,0:T(1,128)S(1)}, f32[1,512]{1,0:T(1,128)S(1)}, u32[]{:S(2)}, u32[]{:S(2)}) %collective-permute-start.10) | collective-permute-done | bytes 2080 | tf_op jit(solution)/shard_map/ppermute | solution.py:342
  46.0 0.6 %add_add_fusion = f32[1,512]{1,0:T(1,128)} fusion(f32[1,512]{1,0:T(1,128)S(1)} %collective-permute-done.10, f32[1,512]{1,0:T(1,128)S(1)} %collective-permute-done.9, f32[1,512]{1,0:T(1,128)S(1)} %get-tuple-element.81, f32[1,512]{1,0:T(1,128)S(1)} %collective-permute-done.8), kind=kLoop, calls=%fused_computation | loop fusion | flops 1536 | bytes 10240 | tf_op jit(solution)/shard_map/add | solution.py:400
  (1 shorter events, 0.0 us)
Async XLA Ops:
  0.0 1.1 %copy-start = (bf16[512,768]{1,0:T(8,128)(2,1)S(1)}, bf16[512,768]{1,0:T(8,128)(2,1)}, u32[]{:S(2)}) copy-start(bf16[512,768]{1,0:T(8,128)(2,1)} %rows_ref.1) | copy-start | bytes 2359300
  1.1 0.7 %copy-start.1 = (s32[512]{0:T(512)S(1)}, s32[512]{0:T(512)}, u32[]{:S(2)}) copy-start(s32[512]{0:T(512)} %param.4) | copy-start | bytes 6148
  2.9 1.9 %collective-permute-start = (bf16[264,768]{1,0:T(8,128)(2,1)S(1)}, bf16[264,768]{1,0:T(8,128)(2,1)S(1)}, u32[]{:S(2)}, u32[]{:S(2)}) collective-permute-start(bf16[264,768]{1,0:T(8,128)(2,1)S(1)} %get-tuple-element.47), channel_id=1, source_target_pairs={{0,1},{1,0},{2,3},{3,2},{4,5},{5,4},{6,7},{7,6},{8,9},{9,8},{10,11... | collective-permute-start | bytes 1216520 | tf_op jit(solution)/shard_map/ppermute | solution.py:342
  4.8 21.7 %copy-start.2 = (s32[4]{0:T(128)S(1)}, s32[4]{0:T(128)}, u32[]{:S(2)}) copy-start(s32[4]{0:T(128)} %rest_0_.1) | copy-start | bytes 52
  4.8 12.3 %collective-permute-start.1 = (bf16[264,768]{1,0:T(8,128)(2,1)S(1)}, bf16[264,768]{1,0:T(8,128)(2,1)S(1)}, u32[]{:S(2)}, u32[]{:S(2)}) collective-permute-start(bf16[264,768]{1,0:T(8,128)(2,1)S(1)} %get-tuple-element.49), channel_id=1, source_target_pairs={{0,9},{2,11},{13,4},{15,6},{16,25},{18,27},{29,20},{31,22}} | collective-permute-start | bytes 1216520 | tf_op jit(solution)/shard_map/ppermute | solution.py:342
  10.5 15.4 %collective-permute-start.2 = (bf16[264,768]{1,0:T(8,128)(2,1)S(1)}, bf16[264,768]{1,0:T(8,128)(2,1)S(1)}, u32[]{:S(2)}, u32[]{:S(2)}) collective-permute-start(bf16[264,768]{1,0:T(8,128)(2,1)S(1)} %get-tuple-element.48.rest_1_.rest_0_), channel_id=1, source_target_pairs={{0,4},{2,6},{13,9},{15,11},{16,20},{18,22},{29,25},{31,27}} | collective-permute-start | bytes 1216520 | tf_op jit(solution)/shard_map/ppermute | solution.py:342
  11.8 15.3 %collective-permute-start.3 = (bf16[264,768]{1,0:T(8,128)(2,1)S(1)}, bf16[264,768]{1,0:T(8,128)(2,1)S(1)}, u32[]{:S(2)}, u32[]{:S(2)}) collective-permute-start(bf16[264,768]{1,0:T(8,128)(2,1)S(1)} %get-tuple-element.49), channel_id=1, source_target_pairs={{1,11},{3,9},{12,6},{14,4},{17,27},{19,25},{28,22},{30,20}} | collective-permute-start | bytes 1216520 | tf_op jit(solution)/shard_map/ppermute | solution.py:342
  12.5 14.6 %collective-permute-start.4 = (bf16[264,768]{1,0:T(8,128)(2,1)S(1)}, bf16[264,768]{1,0:T(8,128)(2,1)S(1)}, u32[]{:S(2)}, u32[]{:S(2)}) collective-permute-start(bf16[264,768]{1,0:T(8,128)(2,1)S(1)} %get-tuple-element.48.rest_1_.rest_0_), channel_id=1, source_target_pairs={{1,6},{3,4},{12,11},{14,9},{17,22},{19,20},{28,27},{30,25}} | collective-permute-start | bytes 1216520 | tf_op jit(solution)/shard_map/ppermute | solution.py:342
  13.2 14.0 %collective-permute-start.5 = (bf16[264,768]{1,0:T(8,128)(2,1)S(1)}, bf16[264,768]{1,0:T(8,128)(2,1)S(1)}, u32[]{:S(2)}, u32[]{:S(2)}) collective-permute-start(bf16[264,768]{1,0:T(8,128)(2,1)S(1)} %get-tuple-element.49), channel_id=1, source_target_pairs={{4,9},{6,11},{9,4},{11,6},{20,25},{22,27},{25,20},{27,22}} | collective-permute-start | bytes 1216520 | tf_op jit(solution)/shard_map/ppermute | solution.py:342
  17.2 10.0 %collective-permute-start.6 = (bf16[264,768]{1,0:T(8,128)(2,1)S(1)}, bf16[264,768]{1,0:T(8,128)(2,1)S(1)}, u32[]{:S(2)}, u32[]{:S(2)}) collective-permute-start(bf16[264,768]{1,0:T(8,128)(2,1)S(1)} %get-tuple-element.48.rest_1_.rest_0_), channel_id=1, source_target_pairs={{5,6},{7,4},{8,11},{10,9},{21,22},{23,20},{24,27},{26,25}} | collective-permute-start | bytes 1216520 | tf_op jit(solution)/shard_map/ppermute | solution.py:342
  25.8 1.4 %collective-permute-start.7 = (bf16[264,768]{1,0:T(8,128)(2,1)S(1)}, bf16[264,768]{1,0:T(8,128)(2,1)S(1)}, u32[]{:S(2)}, u32[]{:S(2)}) collective-permute-start(bf16[264,768]{1,0:T(8,128)(2,1)S(1)} %get-tuple-element.49), channel_id=1, source_target_pairs={{5,11},{7,9},{8,6},{10,4},{21,27},{23,25},{24,22},{26,20}} | collective-permute-start | bytes 1216520 | tf_op jit(solution)/shard_map/ppermute | solution.py:342
  27.3 2.6 %collective-permute-start.8 = (f32[1,512]{1,0:T(1,128)S(1)}, f32[1,512]{1,0:T(1,128)S(1)}, u32[]{:S(2)}, u32[]{:S(2)}) collective-permute-start(f32[1,512]{1,0:T(1,128)S(1)} %get-tuple-element.82), channel_id=1, source_target_pairs={{4,8},{9,13},{6,10},{11,15},{20,24},{25,29},{22,26},{27,31}} | collective-permute-start | bytes 6152 | tf_op jit(solution)/shard_map/ppermute | solution.py:342
  28.0 2.0 %collective-permute-start.9 = (f32[1,512]{1,0:T(1,128)S(1)}, f32[1,512]{1,0:T(1,128)S(1)}, u32[]{:S(2)}, u32[]{:S(2)}) collective-permute-start(f32[1,512]{1,0:T(1,128)S(1)} %get-tuple-element.83), channel_id=1, source_target_pairs={{4,12},{9,1},{6,14},{11,3},{20,28},{25,17},{22,30},{27,19}} | collective-permute-start | bytes 6152 | tf_op jit(solution)/shard_map/ppermute | solution.py:342
  28.7 17.3 %collective-permute-start.10 = (f32[1,512]{1,0:T(1,128)S(1)}, f32[1,512]{1,0:T(1,128)S(1)}, u32[]{:S(2)}, u32[]{:S(2)}) collective-permute-start(f32[1,512]{1,0:T(1,128)S(1)} %get-tuple-element.84), channel_id=1, source_target_pairs={{4,0},{9,5},{6,2},{11,7},{20,16},{25,21},{22,18},{27,23}} | collective-permute-start | bytes 6152 | tf_op jit(solution)/shard_map/ppermute | solution.py:342

commit v7 on v6

--- a/solution.py
+++ b/solution.py
@@ -220,10 +220,13 @@
     return lax.axis_size("chain") // 2 - 1 + lax.axis_index("clus") % 2
 
 
-def stage_kernel(run_slots, old, new, last, *rest):
+def stage_kernel(run_slots, height, count, old, new, last, *rest):
     first = old == 0
     count_ref, rest = (rest[0], rest[1:]) if first or last else (None, rest)
-    refs, rest = rest[: old + new], rest[old + new :]
+    refs = []
+    for ref in rest[:count]:
+        refs += [ref.at[pl.ds(low, height)] for low in range(0, ref.shape[0], height)]
+    rest = rest[count:]
     old_states, rest = rest[: 2 * old], rest[2 * old :]
     if last:
         chunk_refs = rest[: -1 - 2 * (old + new)]
@@ -352,36 +355,40 @@
         name="merge_blocks",
     )(kept, slots, permute(given, swap))
 
-    def to_home(value, moves, across):
-        pairs = []
-        for a, b in moves:
-            for x in range(clus_len // 2):
-                source = 2 * x + (across ^ (a >= high))
-                pairs.append((a, source, b, 2 * (x ^ across) + (b - low)))
-        return permute(value, pairs)
-
-    nearer, farther = [(0, low), (top, high)], [(0, high), (top, low)]
-    middle, plane = [(low, high), (high, low)], [(low, low), (high, high)]
-    stages = [
-        [near, to_home(far, farther, 0), to_home(near, nearer, 0)],
-        [to_home(far, farther, 1), to_home(near, nearer, 1)],
-        [to_home(far, middle, 0), to_home(near, plane, 1)],
-        [to_home(far, middle, 1)],
-    ]
-    blocks, states = [], []
+    def flow(a, b, across, helper):
+        return [
+            (a, 2 * x + (across ^ (a >= high)), b, 2 * (x ^ across) + ((b - low) ^ helper))
+            for x in range(clus_len // 2)
+        ]
+
+    both = ((0, low, high, top), (top, high, low, 0))
+    from_far, from_near, across_near, from_middle, across_middle = [], [], [], [], []
+    for end, close, distant, _ in both:
+        from_far += flow(end, distant, 0, 0) + flow(end, distant, 1, 1)
+        from_near += flow(end, close, 0, 0) + flow(close, close, 1, 1)
+        across_near += flow(end, close, 1, 0)
+        from_middle += flow(close, distant, 0, 0)
+        across_middle += flow(close, distant, 1, 0)
+    from_far, from_near = permute(far, from_far), permute(near, from_near)
+    across_near = permute(near, across_near)
+    from_middle, across_middle = permute(far, from_middle), permute(far, across_middle)
+    forward = [(z, k ^ 1, z, k) for k in range(clus_len) for z in [low + k % 2]]
+    helped = [permute(from_near, forward), permute(from_far, forward)]
+    stages = [[near, from_far, from_near], [across_near, from_middle], [across_middle, helped[0]], [helped[1]]]
+    blocks, states, held = [], [], 0
     state = jax.ShapeDtypeStruct((half, LANES), jnp.float32)
     chunk = jax.ShapeDtypeStruct((1, rows), jnp.float32)
     for number, arrived in enumerate(stages):
         first, last = number == 0, number == len(stages) - 1
-        old, new = len(blocks), len(arrived)
-        blocks = blocks + arrived
-        outs = (chunk,) * chain_len if last else (state,) * (2 * len(blocks))
+        old, blocks = held, blocks + arrived
+        held = sum(value.shape[0] for value in blocks) // (half + TILE)
+        outs = (chunk,) * chain_len if last else (state,) * (2 * held)
         outs += (jax.ShapeDtypeStruct((TILE, LANES), jnp.float32),) * first
-        scratch = [pltpu.VMEM(state.shape, state.dtype)] * (2 * len(blocks))
+        scratch = [pltpu.VMEM(state.shape, state.dtype)] * (2 * held)
         scratch.append(pltpu.VMEM((chain_len, rows), jnp.float32))
         count = [sizes] if first else [members] if last else []
         states = pl.pallas_call(
-            functools.partial(stage_kernel, run_slots, old, new, last),
+            functools.partial(stage_kernel, run_slots, half + TILE, len(blocks), old, held - old, last),
             out_shape=outs,
             in_specs=[SMEM] * first + [VMEM] * (last + len(blocks) + len(states)),
             out_specs=(VMEM,) * len(outs),
@@ -393,10 +400,9 @@
             *states, members = states
     found = states[0]
     for step in range(1, chain_len):
-        moves = []
-        for k in range(clus_len):
-            home = low + k % 2
-            moves.append((home, k, (home + step) % chain_len, k))
+        moves = [
+            (z, k, (z + step) % chain_len, k) for z in range(chain_len) for k in range(clus_len)
+        ]
         found = found + permute(states[step], moves)
     return found
 

time: 46.9 us -> 44.4 us (0.947)
  waiting for transfers between devices: 28.7 us -> 14.2 us
  starting transfers between devices: 13.5 us -> 25.6 us
    ppermute x11, waiting for transfers between devices: 28.7 us -> 14.2 us  [permute(): return lax.ppermute(value, ('chain', 'clus'), pairs)]
    ppermute x11, starting transfers between devices: 13.5 us -> 25.6 us  [permute(): return lax.ppermute(value, ('chain', 'clus'), pairs)]
  transfers between devices with their start and end apart: 11 -> 11, of which waited for: 4 -> 5; matrix products, arithmetic and copies ran while one was open for 0% -> 0% of each run, Pallas kernels for 1% -> 1%
where the time goes in v7:
time: 44.4 us; the launch traced here: 44.2 us
  starting transfers between devices  25.6 us (58%)
  waiting for transfers between devices  14.2 us (32%)
  local copies, waits for them, and re-layouts  1.82 us (4%)
  Pallas kernels  1.79 us (4%)
  other arithmetic  0.58 us (1%)
    ppermute x11, starting transfers between devices, permute(): return lax.ppermute(value, ('chain', 'clus'), pairs)  25.6 us
    ppermute x11, waiting for transfers between devices, permute(): return lax.ppermute(value, ('chain', 'clus'), pairs)  14.2 us
    unnamed x6, local copies, waits for them, and re-layouts  1.82 us
    pallas_call x1, Pallas kernels, local_home(): pl.pallas_call(functools.partial(send_kernel, run_slots, rows // clus_len...  1.04 us
  transfers between devices with their start and end apart: 11, of which 5 were waited for; matrix products, arithmetic and copies ran while one was open for 0% of the time, Pallas kernels for 1%

profile of v7, /device:TPU:0, one launch (start us, length us, event | category | flops | bytes accessed | tf_op | source)
XLA Modules:
  0.0 44.2 jit_solution(1332095084470954794)
XLA Ops:
  0.0 0.0 copy-start
  0.0 1.1 %copy-done = bf16[512,768]{1,0:T(8,128)(2,1)S(1)} copy-done((bf16[512,768]{1,0:T(8,128)(2,1)S(1)}, bf16[512,768]{1,0:T(8,128)(2,1)}, u32[]{:S(2)}) %copy-start) | copy-done | bytes 786456
  1.1 0.0 copy-start.1
  1.1 0.7 %copy-done.1 = s32[512]{0:T(512)S(1)} copy-done((s32[512]{0:T(512)S(1)}, s32[512]{0:T(512)}, u32[]{:S(2)}) %copy-start.1) | copy-done | bytes 2072
  1.8 1.0 %send_blocks.1 = (bf16[256,768]{1,0:T(8,128)(2,1)S(1)}, f32[8,256]{1,0:T(8,128)S(1)}, bf16[264,768]{1,0:T(8,128)(2,1)S(1)}) custom-call(s32[1,512]{1,0:T(1,128)S(1)} %bitcast.1, bf16[512,768]{1,0:T(8,128)(2,1)S(1)} %copy-done), custom_call_target="tpu_custom_call" | custom-call | tf_op jit(solution)/shard_map/send_blocks/pallas_call | solution.py:330
  2.9 0.5 %collective-permute-start = (bf16[264,768]{1,0:T(8,128)(2,1)S(1)}, bf16[264,768]{1,0:T(8,128)(2,1)S(1)}, u32[]{:S(2)}, u32[]{:S(2)}) collective-permute-start(bf16[264,768]{1,0:T(8,128)(2,1)S(1)} %get-tuple-element.47), channel_id=1, source_target_pairs={{0,1},{1,0},{2,3},{3,2},{4,5},{5,4},{6,7},{7,6},{8,9},{9,8},{10,11... | collective-permute-start | bytes 1216520 | tf_op jit(solution)/shard_map/ppermute | solution.py:345
  3.4 1.4 %collective-permute-done.came_ref = bf16[264,768]{1,0:T(8,128)(2,1)S(1)} collective-permute-done((bf16[264,768]{1,0:T(8,128)(2,1)S(1)}, bf16[264,768]{1,0:T(8,128)(2,1)S(1)}, u32[]{:S(2)}, u32[]{:S(2)}) %collective-permute-start) | collective-permute-done | bytes 405536 | tf_op jit(solution)/shard_map/ppermute | solution.py:345
  4.7 0.1 merge_blocks.1
  4.8 0.0 copy-start.2
  4.8 4.9 %collective-permute-start.2 = (bf16[264,768]{1,0:T(8,128)(2,1)S(1)}, bf16[264,768]{1,0:T(8,128)(2,1)S(1)}, u32[]{:S(2)}, u32[]{:S(2)}) collective-permute-start(bf16[264,768]{1,0:T(8,128)(2,1)S(1)} %get-tuple-element.48.rest_1_.rest_0_), channel_id=1, source_target_pairs={{0,4},{2,6},{5,7},{7,5},{13,9},{15,11},{8,10},{10,8},{16,20},{18,2... | collective-permute-start | bytes 1216520 | tf_op jit(solution)/shard_map/ppermute | solution.py:345
  9.7 2.0 %collective-permute-start.1 = (bf16[264,768]{1,0:T(8,128)(2,1)S(1)}, bf16[264,768]{1,0:T(8,128)(2,1)S(1)}, u32[]{:S(2)}, u32[]{:S(2)}) collective-permute-start(bf16[264,768]{1,0:T(8,128)(2,1)S(1)} %get-tuple-element.49), channel_id=1, source_target_pairs={{0,9},{2,11},{1,10},{3,8},{13,4},{15,6},{12,7},{14,5},{16,25},{18,... | collective-permute-start | bytes 1216520 | tf_op jit(solution)/shard_map/ppermute | solution.py:345
  11.8 0.7 %collective-permute-start.3 = (bf16[264,768]{1,0:T(8,128)(2,1)S(1)}, bf16[264,768]{1,0:T(8,128)(2,1)S(1)}, u32[]{:S(2)}, u32[]{:S(2)}) collective-permute-start(bf16[264,768]{1,0:T(8,128)(2,1)S(1)} %get-tuple-element.48.rest_1_.rest_0_), channel_id=1, source_target_pairs={{1,6},{3,4},{12,11},{14,9},{17,22},{19,20},{28,27},{30,25}} | collective-permute-start | bytes 1216520 | tf_op jit(solution)/shard_map/ppermute | solution.py:345
  12.5 0.7 %collective-permute-start.4 = (bf16[264,768]{1,0:T(8,128)(2,1)S(1)}, bf16[264,768]{1,0:T(8,128)(2,1)S(1)}, u32[]{:S(2)}, u32[]{:S(2)}) collective-permute-start(bf16[264,768]{1,0:T(8,128)(2,1)S(1)} %get-tuple-element.49), channel_id=1, source_target_pairs={{4,9},{6,11},{9,4},{11,6},{20,25},{22,27},{25,20},{27,22}} | collective-permute-start | bytes 1216520 | tf_op jit(solution)/shard_map/ppermute | solution.py:345
  13.1 0.7 %collective-permute-start.5 = (bf16[264,768]{1,0:T(8,128)(2,1)S(1)}, bf16[264,768]{1,0:T(8,128)(2,1)S(1)}, u32[]{:S(2)}, u32[]{:S(2)}) collective-permute-start(bf16[264,768]{1,0:T(8,128)(2,1)S(1)} %get-tuple-element.49), channel_id=1, source_target_pairs={{5,11},{7,9},{8,6},{10,4},{21,27},{23,25},{24,22},{26,20}} | collective-permute-start | bytes 1216520 | tf_op jit(solution)/shard_map/ppermute | solution.py:345
  13.8 1.7 %collective-permute-done.2.rest_3_.rest_2_ = bf16[264,768]{1,0:T(8,128)(2,1)S(1)} collective-permute-done((bf16[264,768]{1,0:T(8,128)(2,1)S(1)}, bf16[264,768]{1,0:T(8,128)(2,1)S(1)}, u32[]{:S(2)}, u32[]{:S(2)}) %collective-permute-start.2) | collective-permute-done | bytes 405536 | tf_op jit(solution)/shard_map/ppermute | solution.py:345
  15.5 0.7 %collective-permute-start.6 = (bf16[264,768]{1,0:T(8,128)(2,1)S(1)}, bf16[264,768]{1,0:T(8,128)(2,1)S(1)}, u32[]{:S(2)}, u32[]{:S(2)}) collective-permute-start(bf16[264,768]{1,0:T(8,128)(2,1)S(1)} %collective-permute-done.2.rest_3_.rest_2_), channel_id=1, source_target_pairs={{5,4},{8,9},{7,6},{10,11},{21,20},{24,25},{23,22},{26,27}} | collective-permute-start | bytes 1216520 | tf_op jit(solution)/shard_map/ppermute | solution.py:345
  16.2 8.1 %collective-permute-done.1.rest_2_.rest_1_ = bf16[264,768]{1,0:T(8,128)(2,1)S(1)} collective-permute-done((bf16[264,768]{1,0:T(8,128)(2,1)S(1)}, bf16[264,768]{1,0:T(8,128)(2,1)S(1)}, u32[]{:S(2)}, u32[]{:S(2)}) %collective-permute-start.1) | collective-permute-done | bytes 405536 | tf_op jit(solution)/shard_map/ppermute | solution.py:345
  24.3 0.7 %collective-permute-start.7 = (bf16[264,768]{1,0:T(8,128)(2,1)S(1)}, bf16[264,768]{1,0:T(8,128)(2,1)S(1)}, u32[]{:S(2)}, u32[]{:S(2)}) collective-permute-start(bf16[264,768]{1,0:T(8,128)(2,1)S(1)} %collective-permute-done.1.rest_2_.rest_1_), channel_id=1, source_target_pairs={{5,4},{8,9},{7,6},{10,11},{21,20},{24,25},{23,22},{26,27}} | collective-permute-start | bytes 1216520 | tf_op jit(solution)/shard_map/ppermute | solution.py:345
  25.0 0.0 copy-done.2
  25.0 0.6 %multiply_arrived.3 = (f32[256,128]{1,0:T(8,128)S(1)}, f32[256,128]{1,0:T(8,128)S(1)}, f32[256,128]{1,0:T(8,128)S(1)}, f32[256,128]{1,0:T(8,128)S(1)}, f32[256,1...) custom-call(s32[4]{0:T(128)S(1)} %copy-done.2, ...), custom_call_target="tpu_custom_call" | custom-call | tf_op jit(solution)/shard_map/multiply_arrived/pallas_call | solution.py:390
  25.5 0.0 collective-permute-done.3.rest_3_.rest_4_
  25.6 0.0 collective-permute-done.4.rest_4_.rest_5_
  25.6 0.0 collective-permute-done.5.rest_5_.rest_6_
  25.6 0.0 collective-permute-done.6.rest_6_.rest_7_
  25.6 0.1 multiply_arrived.5
  25.7 0.0 collective-permute-done.7.rest_8_
  25.7 0.1 multiply_last.1
  25.8 5.8 %collective-permute-start.10 = (f32[1,512]{1,0:T(1,128)S(1)}, f32[1,512]{1,0:T(1,128)S(1)}, u32[]{:S(2)}, u32[]{:S(2)}) collective-permute-start(f32[1,512]{1,0:T(1,128)S(1)} %get-tuple-element.84), channel_id=1, source_target_pairs={{0,12},{1,13},{2,14},{3,15},{4,0},{5,1},{6,2},{7,3},{8,4},{9,5},{1... | collective-permute-start | bytes 6152 | tf_op jit(solution)/shard_map/ppermute | solution.py:345
  31.6 7.6 %collective-permute-start.8 = (f32[1,512]{1,0:T(1,128)S(1)}, f32[1,512]{1,0:T(1,128)S(1)}, u32[]{:S(2)}, u32[]{:S(2)}) collective-permute-start(f32[1,512]{1,0:T(1,128)S(1)} %get-tuple-element.82), channel_id=1, source_target_pairs={{0,4},{1,5},{2,6},{3,7},{4,8},{5,9},{6,10},{7,11},{8,12},{9,13},{1... | collective-permute-start | bytes 6152 | tf_op jit(solution)/shard_map/ppermute | solution.py:345
  39.1 1.4 %collective-permute-start.9 = (f32[1,512]{1,0:T(1,128)S(1)}, f32[1,512]{1,0:T(1,128)S(1)}, u32[]{:S(2)}, u32[]{:S(2)}) collective-permute-start(f32[1,512]{1,0:T(1,128)S(1)} %get-tuple-element.83), channel_id=1, source_target_pairs={{0,8},{1,9},{2,10},{3,11},{4,12},{5,13},{6,14},{7,15},{8,0},{9,1},... | collective-permute-start | bytes 6152 | tf_op jit(solution)/shard_map/ppermute | solution.py:345
  40.5 0.1 collective-permute-done.10
  40.6 0.0 collective-permute-done.8
  40.6 3.0 %collective-permute-done.9 = f32[1,512]{1,0:T(1,128)S(1)} collective-permute-done((f32[1,512]{1,0:T(1,128)S(1)}, f32[1,512]{1,0:T(1,128)S(1)}, u32[]{:S(2)}, u32[]{:S(2)}) %collective-permute-start.9) | collective-permute-done | bytes 2080 | tf_op jit(solution)/shard_map/ppermute | solution.py:345
  43.6 0.6 %add_add_fusion = f32[1,512]{1,0:T(1,128)} fusion(f32[1,512]{1,0:T(1,128)S(1)} %collective-permute-done.10, f32[1,512]{1,0:T(1,128)S(1)} %collective-permute-done.9, f32[1,512]{1,0:T(1,128)S(1)} %get-tuple-element.81, f32[1,512]{1,0:T(1,128)S(1)} %collective-permute-done.8), kind=kLoop, calls=%fused_computation | loop fusion | flops 1536 | bytes 10240 | tf_op jit(solution)/shard_map/add | solution.py:406
  (1 shorter events, 0.0 us)
Async XLA Ops:
  0.0 1.1 %copy-start = (bf16[512,768]{1,0:T(8,128)(2,1)S(1)}, bf16[512,768]{1,0:T(8,128)(2,1)}, u32[]{:S(2)}) copy-start(bf16[512,768]{1,0:T(8,128)(2,1)} %rows_ref.1) | copy-start | bytes 2359300
  1.1 0.7 %copy-start.1 = (s32[512]{0:T(512)S(1)}, s32[512]{0:T(512)}, u32[]{:S(2)}) copy-start(s32[512]{0:T(512)} %param.4) | copy-start | bytes 6148
  2.9 1.9 %collective-permute-start = (bf16[264,768]{1,0:T(8,128)(2,1)S(1)}, bf16[264,768]{1,0:T(8,128)(2,1)S(1)}, u32[]{:S(2)}, u32[]{:S(2)}) collective-permute-start(bf16[264,768]{1,0:T(8,128)(2,1)S(1)} %get-tuple-element.47), channel_id=1, source_target_pairs={{0,1},{1,0},{2,3},{3,2},{4,5},{5,4},{6,7},{7,6},{8,9},{9,8},{10,11... | collective-permute-start | bytes 1216520 | tf_op jit(solution)/shard_map/ppermute | solution.py:345
  4.8 20.2 %copy-start.2 = (s32[4]{0:T(128)S(1)}, s32[4]{0:T(128)}, u32[]{:S(2)}) copy-start(s32[4]{0:T(128)} %rest_0_.1) | copy-start | bytes 52
  4.8 10.7 %collective-permute-start.2 = (bf16[264,768]{1,0:T(8,128)(2,1)S(1)}, bf16[264,768]{1,0:T(8,128)(2,1)S(1)}, u32[]{:S(2)}, u32[]{:S(2)}) collective-permute-start(bf16[264,768]{1,0:T(8,128)(2,1)S(1)} %get-tuple-element.48.rest_1_.rest_0_), channel_id=1, source_target_pairs={{0,4},{2,6},{5,7},{7,5},{13,9},{15,11},{8,10},{10,8},{16,20},{18,2... | collective-permute-start | bytes 1216520 | tf_op jit(solution)/shard_map/ppermute | solution.py:345
  9.7 14.6 %collective-permute-start.1 = (bf16[264,768]{1,0:T(8,128)(2,1)S(1)}, bf16[264,768]{1,0:T(8,128)(2,1)S(1)}, u32[]{:S(2)}, u32[]{:S(2)}) collective-permute-start(bf16[264,768]{1,0:T(8,128)(2,1)S(1)} %get-tuple-element.49), channel_id=1, source_target_pairs={{0,9},{2,11},{1,10},{3,8},{13,4},{15,6},{12,7},{14,5},{16,25},{18,... | collective-permute-start | bytes 1216520 | tf_op jit(solution)/shard_map/ppermute | solution.py:345
  11.8 13.8 %collective-permute-start.3 = (bf16[264,768]{1,0:T(8,128)(2,1)S(1)}, bf16[264,768]{1,0:T(8,128)(2,1)S(1)}, u32[]{:S(2)}, u32[]{:S(2)}) collective-permute-start(bf16[264,768]{1,0:T(8,128)(2,1)S(1)} %get-tuple-element.48.rest_1_.rest_0_), channel_id=1, source_target_pairs={{1,6},{3,4},{12,11},{14,9},{17,22},{19,20},{28,27},{30,25}} | collective-permute-start | bytes 1216520 | tf_op jit(solution)/shard_map/ppermute | solution.py:345
  12.5 13.1 %collective-permute-start.4 = (bf16[264,768]{1,0:T(8,128)(2,1)S(1)}, bf16[264,768]{1,0:T(8,128)(2,1)S(1)}, u32[]{:S(2)}, u32[]{:S(2)}) collective-permute-start(bf16[264,768]{1,0:T(8,128)(2,1)S(1)} %get-tuple-element.49), channel_id=1, source_target_pairs={{4,9},{6,11},{9,4},{11,6},{20,25},{22,27},{25,20},{27,22}} | collective-permute-start | bytes 1216520 | tf_op jit(solution)/shard_map/ppermute | solution.py:345
  13.1 12.5 %collective-permute-start.5 = (bf16[264,768]{1,0:T(8,128)(2,1)S(1)}, bf16[264,768]{1,0:T(8,128)(2,1)S(1)}, u32[]{:S(2)}, u32[]{:S(2)}) collective-permute-start(bf16[264,768]{1,0:T(8,128)(2,1)S(1)} %get-tuple-element.49), channel_id=1, source_target_pairs={{5,11},{7,9},{8,6},{10,4},{21,27},{23,25},{24,22},{26,20}} | collective-permute-start | bytes 1216520 | tf_op jit(solution)/shard_map/ppermute | solution.py:345
  15.5 10.1 %collective-permute-start.6 = (bf16[264,768]{1,0:T(8,128)(2,1)S(1)}, bf16[264,768]{1,0:T(8,128)(2,1)S(1)}, u32[]{:S(2)}, u32[]{:S(2)}) collective-permute-start(bf16[264,768]{1,0:T(8,128)(2,1)S(1)} %collective-permute-done.2.rest_3_.rest_2_), channel_id=1, source_target_pairs={{5,4},{8,9},{7,6},{10,11},{21,20},{24,25},{23,22},{26,27}} | collective-permute-start | bytes 1216520 | tf_op jit(solution)/shard_map/ppermute | solution.py:345
  24.3 1.4 %collective-permute-start.7 = (bf16[264,768]{1,0:T(8,128)(2,1)S(1)}, bf16[264,768]{1,0:T(8,128)(2,1)S(1)}, u32[]{:S(2)}, u32[]{:S(2)}) collective-permute-start(bf16[264,768]{1,0:T(8,128)(2,1)S(1)} %collective-permute-done.1.rest_2_.rest_1_), channel_id=1, source_target_pairs={{5,4},{8,9},{7,6},{10,11},{21,20},{24,25},{23,22},{26,27}} | collective-permute-start | bytes 1216520 | tf_op jit(solution)/shard_map/ppermute | solution.py:345
  25.8 14.9 %collective-permute-start.10 = (f32[1,512]{1,0:T(1,128)S(1)}, f32[1,512]{1,0:T(1,128)S(1)}, u32[]{:S(2)}, u32[]{:S(2)}) collective-permute-start(f32[1,512]{1,0:T(1,128)S(1)} %get-tuple-element.84), channel_id=1, source_target_pairs={{0,12},{1,13},{2,14},{3,15},{4,0},{5,1},{6,2},{7,3},{8,4},{9,5},{1... | collective-permute-start | bytes 6152 | tf_op jit(solution)/shard_map/ppermute | solution.py:345
  31.6 9.1 %collective-permute-start.8 = (f32[1,512]{1,0:T(1,128)S(1)}, f32[1,512]{1,0:T(1,128)S(1)}, u32[]{:S(2)}, u32[]{:S(2)}) collective-permute-start(f32[1,512]{1,0:T(1,128)S(1)} %get-tuple-element.82), channel_id=1, source_target_pairs={{0,4},{1,5},{2,6},{3,7},{4,8},{5,9},{6,10},{7,11},{8,12},{9,13},{1... | collective-permute-start | bytes 6152 | tf_op jit(solution)/shard_map/ppermute | solution.py:345
  39.1 4.5 %collective-permute-start.9 = (f32[1,512]{1,0:T(1,128)S(1)}, f32[1,512]{1,0:T(1,128)S(1)}, u32[]{:S(2)}, u32[]{:S(2)}) collective-permute-start(f32[1,512]{1,0:T(1,128)S(1)} %get-tuple-element.83), channel_id=1, source_target_pairs={{0,8},{1,9},{2,10},{3,11},{4,12},{5,13},{6,14},{7,15},{8,0},{9,1},... | collective-permute-start | bytes 6152 | tf_op jit(solution)/shard_map/ppermute | solution.py:345

commit v8 on v7

--- a/solution.py
+++ b/solution.py
@@ -355,26 +355,30 @@
         name="merge_blocks",
     )(kept, slots, permute(given, swap))
 
-    def flow(a, b, across, helper):
-        return [
-            (a, 2 * x + (across ^ (a >= high)), b, 2 * (x ^ across) + ((b - low) ^ helper))
-            for x in range(clus_len // 2)
-        ]
-
-    both = ((0, low, high, top), (top, high, low, 0))
-    from_far, from_near, across_near, from_middle, across_middle = [], [], [], [], []
-    for end, close, distant, _ in both:
-        from_far += flow(end, distant, 0, 0) + flow(end, distant, 1, 1)
-        from_near += flow(end, close, 0, 0) + flow(close, close, 1, 1)
-        across_near += flow(end, close, 1, 0)
-        from_middle += flow(close, distant, 0, 0)
-        across_middle += flow(close, distant, 1, 0)
-    from_far, from_near = permute(far, from_far), permute(near, from_near)
-    across_near = permute(near, across_near)
-    from_middle, across_middle = permute(far, from_middle), permute(far, across_middle)
-    forward = [(z, k ^ 1, z, k) for k in range(clus_len) for z in [low + k % 2]]
-    helped = [permute(from_near, forward), permute(from_far, forward)]
-    stages = [[near, from_far, from_near], [across_near, from_middle], [across_middle, helped[0]], [helped[1]]]
+    def serving(z, across):
+        return across ^ (z >= high)
+
+    def to_home(value, moves):
+        columns = range(clus_len // 2)
+        return permute(
+            value, [(a, 2 * x + serving(a, 0), b, 2 * x + serving(b, 0)) for a, b in moves for x in columns]
+        )
+
+    def across(value):
+        return permute(
+            value,
+            [
+                (z, 2 * x + serving(z, 1), z, 2 * (x ^ 1) + serving(z, 0))
+                for z in range(chain_len)
+                for x in range(clus_len // 2)
+            ],
+        )
+
+    from_far = [(0, high), (top, low)]
+    from_near = [(0, low), (top, high)]
+    from_middle = [(low, high), (high, low)]
+    far_crossed, near_crossed = across(far), across(near)
+    stages = [[near, to_home(far, from_far), to_home(near, from_near), to_home(far, from_middle), near_crossed], [to_home(far_crossed, from_far)], [to_home(near_crossed, from_near), to_home(far_crossed, from_middle)]]
     blocks, states, held = [], [], 0
     state = jax.ShapeDtypeStruct((half, LANES), jnp.float32)
     chunk = jax.ShapeDtypeStruct((1, rows), jnp.float32)
@@ -400,9 +404,8 @@
             *states, members = states
     found = states[0]
     for step in range(1, chain_len):
-        moves = [
-            (z, k, (z + step) % chain_len, k) for z in range(chain_len) for k in range(clus_len)
-        ]
+        homes = [(low + k % 2, k) for k in range(clus_len)]
+        moves = [(home, k, (home + step) % chain_len, k) for home, k in homes]
         found = found + permute(states[step], moves)
     return found
 

time: 44.4 us -> 42.6 us (0.959)
  starting transfers between devices: 25.6 us -> 22.2 us
  waiting for transfers between devices: 14.2 us -> 15.8 us
    ppermute x11 -> x12, starting transfers between devices: 25.6 us -> 22.2 us  [permute(): return lax.ppermute(value, ('chain', 'clus'), pairs)]
    ppermute x11 -> x12, waiting for transfers between devices: 14.2 us -> 15.8 us  [permute(): return lax.ppermute(value, ('chain', 'clus'), pairs)]
  transfers between devices with their start and end apart: 11 -> 12, of which waited for: 5 -> 4; matrix products, arithmetic and copies ran while one was open for 0% -> 0% of each run, Pallas kernels for 1% -> 1%
where the time goes in v8:
time: 42.6 us; the launch traced here: 42.3 us
  starting transfers between devices  22.2 us (52%)
  waiting for transfers between devices  15.8 us (37%)
  local copies, waits for them, and re-layouts  1.82 us (4%)
  Pallas kernels  1.67 us (4%)
  other arithmetic  0.59 us (1%)
    ppermute x12, starting transfers between devices, permute(): return lax.ppermute(value, ('chain', 'clus'), pairs)  22.2 us
    ppermute x12, waiting for transfers between devices, permute(): return lax.ppermute(value, ('chain', 'clus'), pairs)  15.8 us
    unnamed x6, local copies, waits for them, and re-layouts  1.82 us
    pallas_call x1, Pallas kernels, local_home(): pl.pallas_call(functools.partial(send_kernel, run_slots, rows // clus_len...  1.04 us
  transfers between devices with their start and end apart: 12, of which 4 were waited for; matrix products, arithmetic and copies ran while one was open for 0% of the time, Pallas kernels for 1%

profile of v8, /device:TPU:0, one launch (start us, length us, event | category | flops | bytes accessed | tf_op | source)
XLA Modules:
  0.0 42.3 jit_solution(8394021344918003739)
XLA Ops:
  0.0 0.0 copy-start
  0.0 1.1 %copy-done = bf16[512,768]{1,0:T(8,128)(2,1)S(1)} copy-done((bf16[512,768]{1,0:T(8,128)(2,1)S(1)}, bf16[512,768]{1,0:T(8,128)(2,1)}, u32[]{:S(2)}) %copy-start) | copy-done | bytes 786456
  1.1 0.0 copy-start.1
  1.1 0.7 %copy-done.1 = s32[512]{0:T(512)S(1)} copy-done((s32[512]{0:T(512)S(1)}, s32[512]{0:T(512)}, u32[]{:S(2)}) %copy-start.1) | copy-done | bytes 2072
  1.8 1.0 %send_blocks.1 = (bf16[256,768]{1,0:T(8,128)(2,1)S(1)}, f32[8,256]{1,0:T(8,128)S(1)}, bf16[264,768]{1,0:T(8,128)(2,1)S(1)}) custom-call(s32[1,512]{1,0:T(1,128)S(1)} %bitcast.1, bf16[512,768]{1,0:T(8,128)(2,1)S(1)} %copy-done), custom_call_target="tpu_custom_call" | custom-call | tf_op jit(solution)/shard_map/send_blocks/pallas_call | solution.py:330
  2.9 0.5 %collective-permute-start = (bf16[264,768]{1,0:T(8,128)(2,1)S(1)}, bf16[264,768]{1,0:T(8,128)(2,1)S(1)}, u32[]{:S(2)}, u32[]{:S(2)}) collective-permute-start(bf16[264,768]{1,0:T(8,128)(2,1)S(1)} %get-tuple-element.39), channel_id=1, source_target_pairs={{0,1},{1,0},{2,3},{3,2},{4,5},{5,4},{6,7},{7,6},{8,9},{9,8},{10,11... | collective-permute-start | bytes 1216520 | tf_op jit(solution)/shard_map/ppermute | solution.py:345
  3.4 1.4 %collective-permute-done.came_ref = bf16[264,768]{1,0:T(8,128)(2,1)S(1)} collective-permute-done((bf16[264,768]{1,0:T(8,128)(2,1)S(1)}, bf16[264,768]{1,0:T(8,128)(2,1)S(1)}, u32[]{:S(2)}, u32[]{:S(2)}) %collective-permute-start) | collective-permute-done | bytes 405536 | tf_op jit(solution)/shard_map/ppermute | solution.py:345
  4.7 0.1 merge_blocks.1
  4.8 0.0 copy-start.2
  4.8 1.3 %collective-permute-start.5 = (bf16[264,768]{1,0:T(8,128)(2,1)S(1)}, bf16[264,768]{1,0:T(8,128)(2,1)S(1)}, u32[]{:S(2)}, u32[]{:S(2)}) collective-permute-start(bf16[264,768]{1,0:T(8,128)(2,1)S(1)} %get-tuple-element.41), channel_id=1, source_target_pairs={{1,2},{3,0},{5,6},{7,4},{8,11},{10,9},{12,15},{14,13},{17,18},{19,... | collective-permute-start | bytes 1216520 | tf_op jit(solution)/shard_map/ppermute | solution.py:345
  6.1 1.3 %collective-permute-start.4 = (bf16[264,768]{1,0:T(8,128)(2,1)S(1)}, bf16[264,768]{1,0:T(8,128)(2,1)S(1)}, u32[]{:S(2)}, u32[]{:S(2)}) collective-permute-start(bf16[264,768]{1,0:T(8,128)(2,1)S(1)} %get-tuple-element.40.rest_1_.rest_0_), channel_id=1, source_target_pairs={{1,2},{3,0},{5,6},{7,4},{8,11},{10,9},{12,15},{14,13},{17,18},{19,... | collective-permute-start | bytes 1216520 | tf_op jit(solution)/shard_map/ppermute | solution.py:345
  7.4 4.9 %collective-permute-start.2 = (bf16[264,768]{1,0:T(8,128)(2,1)S(1)}, bf16[264,768]{1,0:T(8,128)(2,1)S(1)}, u32[]{:S(2)}, u32[]{:S(2)}) collective-permute-start(bf16[264,768]{1,0:T(8,128)(2,1)S(1)} %get-tuple-element.40.rest_1_.rest_0_), channel_id=1, source_target_pairs={{0,4},{2,6},{13,9},{15,11},{16,20},{18,22},{29,25},{31,27}} | collective-permute-start | bytes 1216520 | tf_op jit(solution)/shard_map/ppermute | solution.py:345
  12.3 2.0 %collective-permute-start.1 = (bf16[264,768]{1,0:T(8,128)(2,1)S(1)}, bf16[264,768]{1,0:T(8,128)(2,1)S(1)}, u32[]{:S(2)}, u32[]{:S(2)}) collective-permute-start(bf16[264,768]{1,0:T(8,128)(2,1)S(1)} %get-tuple-element.41), channel_id=1, source_target_pairs={{0,9},{2,11},{13,4},{15,6},{16,25},{18,27},{29,20},{31,22}} | collective-permute-start | bytes 1216520 | tf_op jit(solution)/shard_map/ppermute | solution.py:345
  14.4 0.7 %collective-permute-start.3 = (bf16[264,768]{1,0:T(8,128)(2,1)S(1)}, bf16[264,768]{1,0:T(8,128)(2,1)S(1)}, u32[]{:S(2)}, u32[]{:S(2)}) collective-permute-start(bf16[264,768]{1,0:T(8,128)(2,1)S(1)} %get-tuple-element.41), channel_id=1, source_target_pairs={{4,9},{6,11},{9,4},{11,6},{20,25},{22,27},{25,20},{27,22}} | collective-permute-start | bytes 1216520 | tf_op jit(solution)/shard_map/ppermute | solution.py:345
  15.1 0.0 collective-permute-done.5
  15.1 4.6 %collective-permute-start.6 = (bf16[264,768]{1,0:T(8,128)(2,1)S(1)}, bf16[264,768]{1,0:T(8,128)(2,1)S(1)}, u32[]{:S(2)}, u32[]{:S(2)}) collective-permute-start(bf16[264,768]{1,0:T(8,128)(2,1)S(1)} %collective-permute-done.5), channel_id=1, source_target_pairs={{0,9},{2,11},{13,4},{15,6},{16,25},{18,27},{29,20},{31,22}} | collective-permute-start | bytes 1216520 | tf_op jit(solution)/shard_map/ppermute | solution.py:345
  19.7 0.0 collective-permute-done.4.rest_5_.rest_4_
  19.7 3.6 %collective-permute-start.7 = (bf16[264,768]{1,0:T(8,128)(2,1)S(1)}, bf16[264,768]{1,0:T(8,128)(2,1)S(1)}, u32[]{:S(2)}, u32[]{:S(2)}) collective-permute-start(bf16[264,768]{1,0:T(8,128)(2,1)S(1)} %collective-permute-done.4.rest_5_.rest_4_), channel_id=1, source_target_pairs={{0,4},{2,6},{13,9},{15,11},{16,20},{18,22},{29,25},{31,27}} | collective-permute-start | bytes 1216520 | tf_op jit(solution)/shard_map/ppermute | solution.py:345
  23.3 0.0 collective-permute-done.2.rest_3_.rest_2_
  23.3 0.7 %collective-permute-start.8 = (bf16[264,768]{1,0:T(8,128)(2,1)S(1)}, bf16[264,768]{1,0:T(8,128)(2,1)S(1)}, u32[]{:S(2)}, u32[]{:S(2)}) collective-permute-start(bf16[264,768]{1,0:T(8,128)(2,1)S(1)} %collective-permute-done.5), channel_id=1, source_target_pairs={{4,9},{6,11},{9,4},{11,6},{20,25},{22,27},{25,20},{27,22}} | collective-permute-start | bytes 1216520 | tf_op jit(solution)/shard_map/ppermute | solution.py:345
  24.0 0.0 collective-permute-done.1.rest_2_.rest_1_
  24.0 0.0 collective-permute-done.3.rest_4_.rest_3_
  24.0 0.0 copy-done.2
  24.0 0.6 %multiply_arrived.2 = (f32[256,128]{1,0:T(8,128)S(1)}, f32[256,128]{1,0:T(8,128)S(1)}, f32[256,128]{1,0:T(8,128)S(1)}, f32[256,128]{1,0:T(8,128)S(1)}, f32[256,1...) custom-call(s32[4]{0:T(128)S(1)} %copy-done.2, ...), custom_call_target="tpu_custom_call" | custom-call | tf_op jit(solution)/shard_map/multiply_arrived/pallas_call | solution.py:394
  24.6 1.8 %collective-permute-done.6.rest_5_.rest_6_ = bf16[264,768]{1,0:T(8,128)(2,1)S(1)} collective-permute-done((bf16[264,768]{1,0:T(8,128)(2,1)S(1)}, bf16[264,768]{1,0:T(8,128)(2,1)S(1)}, u32[]{:S(2)}, u32[]{:S(2)}) %collective-permute-start.6) | collective-permute-done | bytes 405536 | tf_op jit(solution)/shard_map/ppermute | solution.py:345
  26.4 4.3 %collective-permute-done.7.rest_7_ = bf16[264,768]{1,0:T(8,128)(2,1)S(1)} collective-permute-done((bf16[264,768]{1,0:T(8,128)(2,1)S(1)}, bf16[264,768]{1,0:T(8,128)(2,1)S(1)}, u32[]{:S(2)}, u32[]{:S(2)}) %collective-permute-start.7) | collective-permute-done | bytes 405536 | tf_op jit(solution)/shard_map/ppermute | solution.py:345
  30.8 0.0 collective-permute-done.8.rest_8_
  30.8 0.7 %collective-permute-start.10 = (f32[1,512]{1,0:T(1,128)S(1)}, f32[1,512]{1,0:T(1,128)S(1)}, u32[]{:S(2)}, u32[]{:S(2)}) collective-permute-start(f32[1,512]{1,0:T(1,128)S(1)} %get-tuple-element.67), channel_id=1, source_target_pairs={{4,12},{9,1},{6,14},{11,3},{20,28},{25,17},{22,30},{27,19}} | collective-permute-start | bytes 6152 | tf_op jit(solution)/shard_map/ppermute | solution.py:345
  31.4 1.3 %collective-permute-start.11 = (f32[1,512]{1,0:T(1,128)S(1)}, f32[1,512]{1,0:T(1,128)S(1)}, u32[]{:S(2)}, u32[]{:S(2)}) collective-permute-start(f32[1,512]{1,0:T(1,128)S(1)} %get-tuple-element.68), channel_id=1, source_target_pairs={{4,0},{9,5},{6,2},{11,7},{20,16},{25,21},{22,18},{27,23}} | collective-permute-start | bytes 6152 | tf_op jit(solution)/shard_map/ppermute | solution.py:345
  32.7 0.7 %collective-permute-start.9 = (f32[1,512]{1,0:T(1,128)S(1)}, f32[1,512]{1,0:T(1,128)S(1)}, u32[]{:S(2)}, u32[]{:S(2)}) collective-permute-start(f32[1,512]{1,0:T(1,128)S(1)} %get-tuple-element.66), channel_id=1, source_target_pairs={{4,8},{9,13},{6,10},{11,15},{20,24},{25,29},{22,26},{27,31}} | collective-permute-start | bytes 6152 | tf_op jit(solution)/shard_map/ppermute | solution.py:345
  33.4 0.0 collective-permute-done.10
  33.4 8.3 %collective-permute-done.11 = f32[1,512]{1,0:T(1,128)S(1)} collective-permute-done((f32[1,512]{1,0:T(1,128)S(1)}, f32[1,512]{1,0:T(1,128)S(1)}, u32[]{:S(2)}, u32[]{:S(2)}) %collective-permute-start.11) | collective-permute-done | bytes 2080 | tf_op jit(solution)/shard_map/ppermute | solution.py:345
  41.7 0.0 collective-permute-done.9
  41.7 0.6 %add_add_fusion = f32[1,512]{1,0:T(1,128)} fusion(f32[1,512]{1,0:T(1,128)S(1)} %collective-permute-done.11, f32[1,512]{1,0:T(1,128)S(1)} %collective-permute-done.10, f32[1,512]{1,0:T(1,128)S(1)} %get-tuple-element.65, f32[1,512]{1,0:T(1,128)S(1)} %collective-permute-done.9), kind=kLoop, calls=%fused_computation | loop fusion | flops 1536 | bytes 10240 | tf_op jit(solution)/shard_map/add | solution.py:409
  (2 shorter events, 0.0 us)
Async XLA Ops:
  0.0 1.1 %copy-start = (bf16[512,768]{1,0:T(8,128)(2,1)S(1)}, bf16[512,768]{1,0:T(8,128)(2,1)}, u32[]{:S(2)}) copy-start(bf16[512,768]{1,0:T(8,128)(2,1)} %rows_ref.1) | copy-start | bytes 2359300
  1.1 0.7 %copy-start.1 = (s32[512]{0:T(512)S(1)}, s32[512]{0:T(512)}, u32[]{:S(2)}) copy-start(s32[512]{0:T(512)} %param.4) | copy-start | bytes 6148
  2.9 1.9 %collective-permute-start = (bf16[264,768]{1,0:T(8,128)(2,1)S(1)}, bf16[264,768]{1,0:T(8,128)(2,1)S(1)}, u32[]{:S(2)}, u32[]{:S(2)}) collective-permute-start(bf16[264,768]{1,0:T(8,128)(2,1)S(1)} %get-tuple-element.39), channel_id=1, source_target_pairs={{0,1},{1,0},{2,3},{3,2},{4,5},{5,4},{6,7},{7,6},{8,9},{9,8},{10,11... | collective-permute-start | bytes 1216520 | tf_op jit(solution)/shard_map/ppermute | solution.py:345
  4.8 19.2 %copy-start.2 = (s32[4]{0:T(128)S(1)}, s32[4]{0:T(128)}, u32[]{:S(2)}) copy-start(s32[4]{0:T(128)} %rest_0_.1) | copy-start | bytes 52
  4.8 10.2 %collective-permute-start.5 = (bf16[264,768]{1,0:T(8,128)(2,1)S(1)}, bf16[264,768]{1,0:T(8,128)(2,1)S(1)}, u32[]{:S(2)}, u32[]{:S(2)}) collective-permute-start(bf16[264,768]{1,0:T(8,128)(2,1)S(1)} %get-tuple-element.41), channel_id=1, source_target_pairs={{1,2},{3,0},{5,6},{7,4},{8,11},{10,9},{12,15},{14,13},{17,18},{19,... | collective-permute-start | bytes 1216520 | tf_op jit(solution)/shard_map/ppermute | solution.py:345
  6.1 13.6 %collective-permute-start.4 = (bf16[264,768]{1,0:T(8,128)(2,1)S(1)}, bf16[264,768]{1,0:T(8,128)(2,1)S(1)}, u32[]{:S(2)}, u32[]{:S(2)}) collective-permute-start(bf16[264,768]{1,0:T(8,128)(2,1)S(1)} %get-tuple-element.40.rest_1_.rest_0_), channel_id=1, source_target_pairs={{1,2},{3,0},{5,6},{7,4},{8,11},{10,9},{12,15},{14,13},{17,18},{19,... | collective-permute-start | bytes 1216520 | tf_op jit(solution)/shard_map/ppermute | solution.py:345
  7.4 15.8 %collective-permute-start.2 = (bf16[264,768]{1,0:T(8,128)(2,1)S(1)}, bf16[264,768]{1,0:T(8,128)(2,1)S(1)}, u32[]{:S(2)}, u32[]{:S(2)}) collective-permute-start(bf16[264,768]{1,0:T(8,128)(2,1)S(1)} %get-tuple-element.40.rest_1_.rest_0_), channel_id=1, source_target_pairs={{0,4},{2,6},{13,9},{15,11},{16,20},{18,22},{29,25},{31,27}} | collective-permute-start | bytes 1216520 | tf_op jit(solution)/shard_map/ppermute | solution.py:345
  12.3 11.7 %collective-permute-start.1 = (bf16[264,768]{1,0:T(8,128)(2,1)S(1)}, bf16[264,768]{1,0:T(8,128)(2,1)S(1)}, u32[]{:S(2)}, u32[]{:S(2)}) collective-permute-start(bf16[264,768]{1,0:T(8,128)(2,1)S(1)} %get-tuple-element.41), channel_id=1, source_target_pairs={{0,9},{2,11},{13,4},{15,6},{16,25},{18,27},{29,20},{31,22}} | collective-permute-start | bytes 1216520 | tf_op jit(solution)/shard_map/ppermute | solution.py:345
  14.4 9.6 %collective-permute-start.3 = (bf16[264,768]{1,0:T(8,128)(2,1)S(1)}, bf16[264,768]{1,0:T(8,128)(2,1)S(1)}, u32[]{:S(2)}, u32[]{:S(2)}) collective-permute-start(bf16[264,768]{1,0:T(8,128)(2,1)S(1)} %get-tuple-element.41), channel_id=1, source_target_pairs={{4,9},{6,11},{9,4},{11,6},{20,25},{22,27},{25,20},{27,22}} | collective-permute-start | bytes 1216520 | tf_op jit(solution)/shard_map/ppermute | solution.py:345
  15.1 11.4 %collective-permute-start.6 = (bf16[264,768]{1,0:T(8,128)(2,1)S(1)}, bf16[264,768]{1,0:T(8,128)(2,1)S(1)}, u32[]{:S(2)}, u32[]{:S(2)}) collective-permute-start(bf16[264,768]{1,0:T(8,128)(2,1)S(1)} %collective-permute-done.5), channel_id=1, source_target_pairs={{0,9},{2,11},{13,4},{15,6},{16,25},{18,27},{29,20},{31,22}} | collective-permute-start | bytes 1216520 | tf_op jit(solution)/shard_map/ppermute | solution.py:345
  19.7 11.1 %collective-permute-start.7 = (bf16[264,768]{1,0:T(8,128)(2,1)S(1)}, bf16[264,768]{1,0:T(8,128)(2,1)S(1)}, u32[]{:S(2)}, u32[]{:S(2)}) collective-permute-start(bf16[264,768]{1,0:T(8,128)(2,1)S(1)} %collective-permute-done.4.rest_5_.rest_4_), channel_id=1, source_target_pairs={{0,4},{2,6},{13,9},{15,11},{16,20},{18,22},{29,25},{31,27}} | collective-permute-start | bytes 1216520 | tf_op jit(solution)/shard_map/ppermute | solution.py:345
  23.3 7.5 %collective-permute-start.8 = (bf16[264,768]{1,0:T(8,128)(2,1)S(1)}, bf16[264,768]{1,0:T(8,128)(2,1)S(1)}, u32[]{:S(2)}, u32[]{:S(2)}) collective-permute-start(bf16[264,768]{1,0:T(8,128)(2,1)S(1)} %collective-permute-done.5), channel_id=1, source_target_pairs={{4,9},{6,11},{9,4},{11,6},{20,25},{22,27},{25,20},{27,22}} | collective-permute-start | bytes 1216520 | tf_op jit(solution)/shard_map/ppermute | solution.py:345
  30.8 2.6 %collective-permute-start.10 = (f32[1,512]{1,0:T(1,128)S(1)}, f32[1,512]{1,0:T(1,128)S(1)}, u32[]{:S(2)}, u32[]{:S(2)}) collective-permute-start(f32[1,512]{1,0:T(1,128)S(1)} %get-tuple-element.67), channel_id=1, source_target_pairs={{4,12},{9,1},{6,14},{11,3},{20,28},{25,17},{22,30},{27,19}} | collective-permute-start | bytes 6152 | tf_op jit(solution)/shard_map/ppermute | solution.py:345
  31.4 10.2 %collective-permute-start.11 = (f32[1,512]{1,0:T(1,128)S(1)}, f32[1,512]{1,0:T(1,128)S(1)}, u32[]{:S(2)}, u32[]{:S(2)}) collective-permute-start(f32[1,512]{1,0:T(1,128)S(1)} %get-tuple-element.68), channel_id=1, source_target_pairs={{4,0},{9,5},{6,2},{11,7},{20,16},{25,21},{22,18},{27,23}} | collective-permute-start | bytes 6152 | tf_op jit(solution)/shard_map/ppermute | solution.py:345
  32.7 8.9 %collective-permute-start.9 = (f32[1,512]{1,0:T(1,128)S(1)}, f32[1,512]{1,0:T(1,128)S(1)}, u32[]{:S(2)}, u32[]{:S(2)}) collective-permute-start(f32[1,512]{1,0:T(1,128)S(1)} %get-tuple-element.66), channel_id=1, source_target_pairs={{4,8},{9,13},{6,10},{11,15},{20,24},{25,29},{22,26},{27,31}} | collective-permute-start | bytes 6152 | tf_op jit(solution)/shard_map/ppermute | solution.py:345

commit v9 on v8

--- a/solution.py
+++ b/solution.py
@@ -166,11 +166,10 @@
     return lax.ppermute(found, ("chain", "clus"), pairs)
 
 
-def send_kernel(run_slots, cluster_runs, dest_ref, rows_ref, kept_ref, slots_ref, given_ref):
-    rows, width = rows_ref.shape
+def place_kernel(run_slots, cluster_runs, dest_ref, hot_ref, kept_slots_ref, given_slots_ref):
+    rows = dest_ref.shape[1]
     runs = rows // PIECE
     half = rows // 2
-    depth = half // 2
     clus = lax.axis_index("clus")
     upper = (lax.axis_index("chain") >= lax.axis_size("chain") // 2).astype(jnp.int32)
     code = (clus // 2 ^ clus % 2 ^ upper) * 2 + upper
@@ -185,24 +184,29 @@
     earlier = jnp.dot(as_bf16(member), as_bf16(before), preferred_element_type=jnp.float32)
     rank = jnp.sum(jnp.where(member, earlier, 0.0), axis=0, keepdims=True).astype(jnp.int32)
     hot = as_bf16(lax.broadcasted_iota(jnp.int32, (rows, rows), 0) == run * PIECE + rank)
+    hot_ref[...] = hot
     moved = lax.dot_general(
         jnp.broadcast_to(within, (TILE, rows)).astype(jnp.float32).astype(jnp.bfloat16),
         hot,
         (((1,), (1,)), ((), ())),
         preferred_element_type=jnp.float32,
     )
+    line = lax.broadcasted_iota(jnp.int32, (TILE, half), 0)
+    kept_slots_ref[...] = jnp.where(line == 0, moved[:, 0:half], 0.0)
+    given_slots_ref[...] = jnp.where(line == 1, moved[:, half:rows], 0.0)
+
+
+def send_kernel(hot_ref, slots_ref, rows_ref, kept_ref, given_ref):
+    rows, width = rows_ref.shape
+    half = rows // 2
     x = rows_ref[...].astype(jnp.float32)
     units = (x * lax.rsqrt(jnp.sum(x * x, axis=1, keepdims=True) + 1e-06)).astype(jnp.bfloat16)
     for low, ref in ((0, kept_ref), (half, given_ref)):
         ref[0:half, :] = jnp.dot(
-            hot[low : low + half], units, preferred_element_type=jnp.float32
+            hot_ref[low : low + half, :], units, preferred_element_type=jnp.float32
         ).astype(jnp.bfloat16)
-    line = lax.broadcasted_iota(jnp.int32, (TILE, half), 0)
-    slots_ref[...] = jnp.where(line == 0, moved[:, 0:half], 0.0)
     given_ref[half : half + TILE, :] = jnp.zeros((TILE, width), jnp.bfloat16)
-    given_ref[half : half + TILE, 0:half] = jnp.where(line == 1, moved[:, half:rows], 0.0).astype(
-        jnp.bfloat16
-    )
+    given_ref[half : half + TILE, 0:half] = slots_ref[...].astype(jnp.bfloat16)
 
 
 def merge_kernel(kept_ref, slots_ref, came_ref, near_ref, far_ref):
@@ -327,18 +331,24 @@
     half = rows // 2
     run_slots = chain_len * clus_len * PIECE
     block = jax.ShapeDtypeStruct((half + TILE, width), jnp.bfloat16)
-    kept, slots, given = pl.pallas_call(
-        functools.partial(send_kernel, run_slots, rows // clus_len // PIECE),
-        out_shape=(
-            jax.ShapeDtypeStruct((half, width), jnp.bfloat16),
-            jax.ShapeDtypeStruct((TILE, half), jnp.float32),
-            block,
-        ),
-        in_specs=[VMEM, VMEM],
-        out_specs=(VMEM, VMEM, VMEM),
-        compiler_params=pltpu.CompilerParams(vmem_limit_bytes=32 * 2**20),
+    slots = jax.ShapeDtypeStruct((TILE, half), jnp.float32)
+    hot, slots, given_slots = pl.pallas_call(
+        functools.partial(place_kernel, run_slots, rows // clus_len // PIECE),
+        out_shape=(jax.ShapeDtypeStruct((rows, rows), jnp.bfloat16), slots, slots),
+        in_specs=[VMEM],
+        out_specs=(VMEM,) * 3,
+        cost_estimate=pl.CostEstimate(flops=0, bytes_accessed=8 * rows * width, transcendentals=0),
+        compiler_params=pltpu.CompilerParams(vmem_limit_bytes=16 * 2**20),
+        name="place_rows",
+    )(dest.reshape(1, rows))
+    kept, given = pl.pallas_call(
+        send_kernel,
+        out_shape=(jax.ShapeDtypeStruct((half, width), jnp.bfloat16), block),
+        in_specs=[VMEM] * 3,
+        out_specs=(VMEM, VMEM),
+        compiler_params=pltpu.CompilerParams(vmem_limit_bytes=16 * 2**20),
         name="send_blocks",
-    )(dest.reshape(1, rows), embeddings)
+    )(hot, given_slots, embeddings)
 
     def permute(value, moves):
         pairs = [(a * clus_len + b, c * clus_len + d) for a, b, c, d in moves]
@@ -360,25 +370,31 @@
 
     def to_home(value, moves):
         columns = range(clus_len // 2)
-        return permute(
-            value, [(a, 2 * x + serving(a, 0), b, 2 * x + serving(b, 0)) for a, b in moves for x in columns]
-        )
+        pairs = [(a, 2 * x + serving(a, 0), b, 2 * x + serving(b, 0)) for a, b in moves for x in columns]
+        if {a for a, _ in moves} == {b for _, b in moves}:
+            taken = {pair[:2] for pair in pairs}
+            everyone = [(z, k) for z in range(chain_len) for k in range(clus_len)]
+            pairs += [place + place for place in everyone if place not in taken]
+        return permute(value, pairs)
 
     def across(value):
-        return permute(
-            value,
-            [
-                (z, 2 * x + serving(z, 1), z, 2 * (x ^ 1) + serving(z, 0))
-                for z in range(chain_len)
-                for x in range(clus_len // 2)
-            ],
-        )
+        pairs = []
+        for z in range(chain_len):
+            for x in range(clus_len // 2):
+                own, other = serving(z, 0), serving(z, 1)
+                pairs.append((z, 2 * x + other, z, 2 * (x ^ 1) + own))
+                pairs.append((z, 2 * x + own, z, 2 * x + other))
+        return permute(value, pairs)
 
     from_far = [(0, high), (top, low)]
     from_near = [(0, low), (top, high)]
     from_middle = [(low, high), (high, low)]
     far_crossed, near_crossed = across(far), across(near)
-    stages = [[near, to_home(far, from_far), to_home(near, from_near), to_home(far, from_middle), near_crossed], [to_home(far_crossed, from_far)], [to_home(near_crossed, from_near), to_home(far_crossed, from_middle)]]
+    far_along, near_along = to_home(far, from_far), to_home(near, from_near)
+    middle_along = to_home(far, from_middle)
+    far_after, near_after = to_home(far_crossed, from_far), to_home(near_crossed, from_near)
+    middle_after = to_home(far_crossed, from_middle)
+    stages = [[near, near_crossed, near_along, far_along], [far_after, middle_along], [near_after, middle_after]]
     blocks, states, held = [], [], 0
     state = jax.ShapeDtypeStruct((half, LANES), jnp.float32)
     chunk = jax.ShapeDtypeStruct((1, rows), jnp.float32)

time: 42.6 us -> 41.9 us (0.984)
  starting transfers between devices: 22.2 us -> 20.3 us
  waiting for transfers between devices: 15.8 us -> 16.7 us
    ppermute x12, starting transfers between devices: 22.2 us -> 20.3 us  [permute(): return lax.ppermute(value, ('chain', 'clus'), pairs)]
    ppermute x12, waiting for transfers between devices: 15.8 us -> 16.7 us  [permute(): return lax.ppermute(value, ('chain', 'clus'), pairs)]
    pallas_call x1 -> x2, Pallas kernels: 1.04 us -> 1.29 us  [the longest x1 0.76 us: local_home(): pl.pallas_call(send_kernel, out_shape=(jax.ShapeDtypeStruct((half, width)...]
where the time goes in v9:
time: 41.9 us; the launch traced here: 41.6 us
  starting transfers between devices  20.3 us (48%)
  waiting for transfers between devices  16.7 us (40%)
  Pallas kernels  1.91 us (5%)
  local copies, waits for them, and re-layouts  1.83 us (4%)
  other arithmetic  0.59 us (1%)
    ppermute x12, starting transfers between devices, permute(): return lax.ppermute(value, ('chain', 'clus'), pairs)  20.3 us
    ppermute x12, waiting for transfers between devices, permute(): return lax.ppermute(value, ('chain', 'clus'), pairs)  16.7 us
    unnamed x6, local copies, waits for them, and re-layouts  1.83 us
  transfers between devices with their start and end apart: 12, of which 4 were waited for; matrix products, arithmetic and copies ran while one was open for 0% of the time, Pallas kernels for 1%

profile of v9, /device:TPU:0, one launch (start us, length us, event | category | flops | bytes accessed | tf_op | source)
XLA Modules:
  0.0 41.6 jit_solution(9338419614450131908)
XLA Ops:
  0.0 0.0 copy-start.1
  0.0 0.7 %copy-done.1 = s32[512]{0:T(512)S(1)} copy-done((s32[512]{0:T(512)S(1)}, s32[512]{0:T(512)}, u32[]{:S(2)}) %copy-start.1) | copy-done | bytes 2072
  0.7 0.5 %place_rows.1 = (bf16[512,512]{1,0:T(8,128)(2,1)S(1)}, f32[8,256]{1,0:T(8,128)S(1)}, f32[8,256]{1,0:T(8,128)S(1)}) custom-call(s32[1,512]{1,0:T(1,128)S(1)} %bitcast.1), custom_call_target="tpu_custom_call" | custom-call | bytes 3145728 | tf_op jit(solution)/shard_map/place_rows/pallas_call | solution.py:335
  1.2 0.0 copy-start
  1.2 1.1 %copy-done = bf16[512,768]{1,0:T(8,128)(2,1)S(1)} copy-done((bf16[512,768]{1,0:T(8,128)(2,1)S(1)}, bf16[512,768]{1,0:T(8,128)(2,1)}, u32[]{:S(2)}) %copy-start) | copy-done | bytes 786456
  2.4 0.8 %send_blocks.1 = (bf16[256,768]{1,0:T(8,128)(2,1)S(1)}, bf16[264,768]{1,0:T(8,128)(2,1)S(1)}) custom-call(bf16[512,512]{1,0:T(8,128)(2,1)S(1)} %get-tuple-element.37.hot_ref, f32[8,256]{1,0:T(8,128)S(1)} %get-tuple-element.38.slots_ref, bf16[512,768]{1,0:T(8,128)(2,1)S(1)} %copy-done), custom_call_target="tpu_custom_call" | custom-call | tf_op jit(solution)/shard_map/send_blocks/pallas_call | solution.py:344
  3.1 0.5 %collective-permute-start = (bf16[264,768]{1,0:T(8,128)(2,1)S(1)}, bf16[264,768]{1,0:T(8,128)(2,1)S(1)}, u32[]{:S(2)}, u32[]{:S(2)}) collective-permute-start(bf16[264,768]{1,0:T(8,128)(2,1)S(1)} %get-tuple-element.41), channel_id=1, source_target_pairs={{0,1},{1,0},{2,3},{3,2},{4,5},{5,4},{6,7},{7,6},{8,9},{9,8},{10,11... | collective-permute-start | bytes 1216520 | tf_op jit(solution)/shard_map/ppermute | solution.py:355
  3.6 1.4 %collective-permute-done.came_ref = bf16[264,768]{1,0:T(8,128)(2,1)S(1)} collective-permute-done((bf16[264,768]{1,0:T(8,128)(2,1)S(1)}, bf16[264,768]{1,0:T(8,128)(2,1)S(1)}, u32[]{:S(2)}, u32[]{:S(2)}) %collective-permute-start) | collective-permute-done | bytes 405536 | tf_op jit(solution)/shard_map/ppermute | solution.py:355
  5.0 0.1 merge_blocks.1
  5.1 0.0 copy-start.2
  5.1 0.4 %collective-permute-start.4 = (bf16[264,768]{1,0:T(8,128)(2,1)S(1)}, bf16[264,768]{1,0:T(8,128)(2,1)S(1)}, u32[]{:S(2)}, u32[]{:S(2)}) collective-permute-start(bf16[264,768]{1,0:T(8,128)(2,1)S(1)} %get-tuple-element.43), channel_id=1, source_target_pairs={{1,2},{0,1},{3,0},{2,3},{5,6},{4,5},{7,4},{6,7},{8,11},{9,8},{10,9... | collective-permute-start | bytes 1216520 | tf_op jit(solution)/shard_map/ppermute | solution.py:355
  5.5 2.6 %collective-permute-start.1 = (bf16[264,768]{1,0:T(8,128)(2,1)S(1)}, bf16[264,768]{1,0:T(8,128)(2,1)S(1)}, u32[]{:S(2)}, u32[]{:S(2)}) collective-permute-start(bf16[264,768]{1,0:T(8,128)(2,1)S(1)} %get-tuple-element.42.rest_1_.rest_0_), channel_id=1, source_target_pairs={{1,2},{0,1},{3,0},{2,3},{5,6},{4,5},{7,4},{6,7},{8,11},{9,8},{10,9... | collective-permute-start | bytes 1216520 | tf_op jit(solution)/shard_map/ppermute | solution.py:355
  8.1 3.5 %collective-permute-start.2 = (bf16[264,768]{1,0:T(8,128)(2,1)S(1)}, bf16[264,768]{1,0:T(8,128)(2,1)S(1)}, u32[]{:S(2)}, u32[]{:S(2)}) collective-permute-start(bf16[264,768]{1,0:T(8,128)(2,1)S(1)} %get-tuple-element.42.rest_1_.rest_0_), channel_id=1, source_target_pairs={{0,4},{2,6},{13,9},{15,11},{16,20},{18,22},{29,25},{31,27}} | collective-permute-start | bytes 1216520 | tf_op jit(solution)/shard_map/ppermute | solution.py:355
  11.6 2.0 %collective-permute-start.3 = (bf16[264,768]{1,0:T(8,128)(2,1)S(1)}, bf16[264,768]{1,0:T(8,128)(2,1)S(1)}, u32[]{:S(2)}, u32[]{:S(2)}) collective-permute-start(bf16[264,768]{1,0:T(8,128)(2,1)S(1)} %get-tuple-element.43), channel_id=1, source_target_pairs={{0,9},{2,11},{13,4},{15,6},{16,25},{18,27},{29,20},{31,22}} | collective-permute-start | bytes 1216520 | tf_op jit(solution)/shard_map/ppermute | solution.py:355
  13.7 0.7 %collective-permute-start.6 = (bf16[264,768]{1,0:T(8,128)(2,1)S(1)}, bf16[264,768]{1,0:T(8,128)(2,1)S(1)}, u32[]{:S(2)}, u32[]{:S(2)}) collective-permute-start(bf16[264,768]{1,0:T(8,128)(2,1)S(1)} %get-tuple-element.43), channel_id=1, source_target_pairs={{4,9},{6,11},{9,4},{11,6},{0,0},{1,1},{2,2},{3,3},{5,5},{7,7},{8,8... | collective-permute-start | bytes 1216520 | tf_op jit(solution)/shard_map/ppermute | solution.py:355
  14.4 0.0 collective-permute-done.4
  14.4 3.7 %collective-permute-start.5 = (bf16[264,768]{1,0:T(8,128)(2,1)S(1)}, bf16[264,768]{1,0:T(8,128)(2,1)S(1)}, u32[]{:S(2)}, u32[]{:S(2)}) collective-permute-start(bf16[264,768]{1,0:T(8,128)(2,1)S(1)} %collective-permute-done.4), channel_id=1, source_target_pairs={{0,9},{2,11},{13,4},{15,6},{16,25},{18,27},{29,20},{31,22}} | collective-permute-start | bytes 1216520 | tf_op jit(solution)/shard_map/ppermute | solution.py:355
  18.1 0.0 collective-permute-done.1.rest_2_.rest_1_
  18.1 3.6 %collective-permute-start.7 = (bf16[264,768]{1,0:T(8,128)(2,1)S(1)}, bf16[264,768]{1,0:T(8,128)(2,1)S(1)}, u32[]{:S(2)}, u32[]{:S(2)}) collective-permute-start(bf16[264,768]{1,0:T(8,128)(2,1)S(1)} %collective-permute-done.1.rest_2_.rest_1_), channel_id=1, source_target_pairs={{0,4},{2,6},{13,9},{15,11},{16,20},{18,22},{29,25},{31,27}} | collective-permute-start | bytes 1216520 | tf_op jit(solution)/shard_map/ppermute | solution.py:355
  21.7 0.0 collective-permute-done.2.rest_3_.rest_2_
  21.7 0.7 %collective-permute-start.8 = (bf16[264,768]{1,0:T(8,128)(2,1)S(1)}, bf16[264,768]{1,0:T(8,128)(2,1)S(1)}, u32[]{:S(2)}, u32[]{:S(2)}) collective-permute-start(bf16[264,768]{1,0:T(8,128)(2,1)S(1)} %collective-permute-done.4), channel_id=1, source_target_pairs={{4,9},{6,11},{9,4},{11,6},{0,0},{1,1},{2,2},{3,3},{5,5},{7,7},{8,8... | collective-permute-start | bytes 1216520 | tf_op jit(solution)/shard_map/ppermute | solution.py:355
  22.4 0.0 collective-permute-done.3.rest_4_.rest_3_
  22.4 0.0 copy-done.2
  22.4 0.6 %multiply_arrived.2 = (f32[256,128]{1,0:T(8,128)S(1)}, f32[256,128]{1,0:T(8,128)S(1)}, f32[256,128]{1,0:T(8,128)S(1)}, f32[256,128]{1,0:T(8,128)S(1)}, f32[256,1...) custom-call(s32[4]{0:T(128)S(1)} %copy-done.2, ...), custom_call_target="tpu_custom_call" | custom-call | tf_op jit(solution)/shard_map/multiply_arrived/pallas_call | solution.py:410
  23.0 0.0 collective-permute-done.6.rest_5_.rest_6_
  23.0 2.7 %collective-permute-done.5.rest_4_.rest_5_ = bf16[264,768]{1,0:T(8,128)(2,1)S(1)} collective-permute-done((bf16[264,768]{1,0:T(8,128)(2,1)S(1)}, bf16[264,768]{1,0:T(8,128)(2,1)S(1)}, u32[]{:S(2)}, u32[]{:S(2)}) %collective-permute-start.5) | collective-permute-done | bytes 405536 | tf_op jit(solution)/shard_map/ppermute | solution.py:355
  25.7 4.3 %collective-permute-done.7.rest_7_ = bf16[264,768]{1,0:T(8,128)(2,1)S(1)} collective-permute-done((bf16[264,768]{1,0:T(8,128)(2,1)S(1)}, bf16[264,768]{1,0:T(8,128)(2,1)S(1)}, u32[]{:S(2)}, u32[]{:S(2)}) %collective-permute-start.7) | collective-permute-done | bytes 405536 | tf_op jit(solution)/shard_map/ppermute | solution.py:355
  30.1 0.0 collective-permute-done.8.rest_8_
  30.1 0.7 %collective-permute-start.10 = (f32[1,512]{1,0:T(1,128)S(1)}, f32[1,512]{1,0:T(1,128)S(1)}, u32[]{:S(2)}, u32[]{:S(2)}) collective-permute-start(f32[1,512]{1,0:T(1,128)S(1)} %get-tuple-element.67), channel_id=1, source_target_pairs={{4,12},{9,1},{6,14},{11,3},{20,28},{25,17},{22,30},{27,19}} | collective-permute-start | bytes 6152 | tf_op jit(solution)/shard_map/ppermute | solution.py:355
  30.7 1.3 %collective-permute-start.11 = (f32[1,512]{1,0:T(1,128)S(1)}, f32[1,512]{1,0:T(1,128)S(1)}, u32[]{:S(2)}, u32[]{:S(2)}) collective-permute-start(f32[1,512]{1,0:T(1,128)S(1)} %get-tuple-element.68), channel_id=1, source_target_pairs={{4,0},{9,5},{6,2},{11,7},{20,16},{25,21},{22,18},{27,23}} | collective-permute-start | bytes 6152 | tf_op jit(solution)/shard_map/ppermute | solution.py:355
  32.0 0.7 %collective-permute-start.9 = (f32[1,512]{1,0:T(1,128)S(1)}, f32[1,512]{1,0:T(1,128)S(1)}, u32[]{:S(2)}, u32[]{:S(2)}) collective-permute-start(f32[1,512]{1,0:T(1,128)S(1)} %get-tuple-element.66), channel_id=1, source_target_pairs={{4,8},{9,13},{6,10},{11,15},{20,24},{25,29},{22,26},{27,31}} | collective-permute-start | bytes 6152 | tf_op jit(solution)/shard_map/ppermute | solution.py:355
  32.7 0.0 collective-permute-done.10
  32.7 8.3 %collective-permute-done.11 = f32[1,512]{1,0:T(1,128)S(1)} collective-permute-done((f32[1,512]{1,0:T(1,128)S(1)}, f32[1,512]{1,0:T(1,128)S(1)}, u32[]{:S(2)}, u32[]{:S(2)}) %collective-permute-start.11) | collective-permute-done | bytes 2080 | tf_op jit(solution)/shard_map/ppermute | solution.py:355
  41.0 0.0 collective-permute-done.9
  41.0 0.6 %add_add_fusion = f32[1,512]{1,0:T(1,128)} fusion(f32[1,512]{1,0:T(1,128)S(1)} %collective-permute-done.11, f32[1,512]{1,0:T(1,128)S(1)} %collective-permute-done.10, f32[1,512]{1,0:T(1,128)S(1)} %get-tuple-element.65, f32[1,512]{1,0:T(1,128)S(1)} %collective-permute-done.9), kind=kLoop, calls=%fused_computation | loop fusion | flops 1536 | bytes 10240 | tf_op jit(solution)/shard_map/add | solution.py:425
  (2 shorter events, 0.0 us)
Async XLA Ops:
  0.0 0.7 %copy-start.1 = (s32[512]{0:T(512)S(1)}, s32[512]{0:T(512)}, u32[]{:S(2)}) copy-start(s32[512]{0:T(512)} %param.4) | copy-start | bytes 6148
  1.2 1.1 %copy-start = (bf16[512,768]{1,0:T(8,128)(2,1)S(1)}, bf16[512,768]{1,0:T(8,128)(2,1)}, u32[]{:S(2)}) copy-start(bf16[512,768]{1,0:T(8,128)(2,1)} %rows_ref.1) | copy-start | bytes 2359300
  3.1 1.9 %collective-permute-start = (bf16[264,768]{1,0:T(8,128)(2,1)S(1)}, bf16[264,768]{1,0:T(8,128)(2,1)S(1)}, u32[]{:S(2)}, u32[]{:S(2)}) collective-permute-start(bf16[264,768]{1,0:T(8,128)(2,1)S(1)} %get-tuple-element.41), channel_id=1, source_target_pairs={{0,1},{1,0},{2,3},{3,2},{4,5},{5,4},{6,7},{7,6},{8,9},{9,8},{10,11... | collective-permute-start | bytes 1216520 | tf_op jit(solution)/shard_map/ppermute | solution.py:355
  5.1 17.3 %copy-start.2 = (s32[4]{0:T(128)S(1)}, s32[4]{0:T(128)}, u32[]{:S(2)}) copy-start(s32[4]{0:T(128)} %rest_0_.1) | copy-start | bytes 52
  5.1 9.3 %collective-permute-start.4 = (bf16[264,768]{1,0:T(8,128)(2,1)S(1)}, bf16[264,768]{1,0:T(8,128)(2,1)S(1)}, u32[]{:S(2)}, u32[]{:S(2)}) collective-permute-start(bf16[264,768]{1,0:T(8,128)(2,1)S(1)} %get-tuple-element.43), channel_id=1, source_target_pairs={{1,2},{0,1},{3,0},{2,3},{5,6},{4,5},{7,4},{6,7},{8,11},{9,8},{10,9... | collective-permute-start | bytes 1216520 | tf_op jit(solution)/shard_map/ppermute | solution.py:355
  5.5 12.6 %collective-permute-start.1 = (bf16[264,768]{1,0:T(8,128)(2,1)S(1)}, bf16[264,768]{1,0:T(8,128)(2,1)S(1)}, u32[]{:S(2)}, u32[]{:S(2)}) collective-permute-start(bf16[264,768]{1,0:T(8,128)(2,1)S(1)} %get-tuple-element.42.rest_1_.rest_0_), channel_id=1, source_target_pairs={{1,2},{0,1},{3,0},{2,3},{5,6},{4,5},{7,4},{6,7},{8,11},{9,8},{10,9... | collective-permute-start | bytes 1216520 | tf_op jit(solution)/shard_map/ppermute | solution.py:355
  8.1 13.6 %collective-permute-start.2 = (bf16[264,768]{1,0:T(8,128)(2,1)S(1)}, bf16[264,768]{1,0:T(8,128)(2,1)S(1)}, u32[]{:S(2)}, u32[]{:S(2)}) collective-permute-start(bf16[264,768]{1,0:T(8,128)(2,1)S(1)} %get-tuple-element.42.rest_1_.rest_0_), channel_id=1, source_target_pairs={{0,4},{2,6},{13,9},{15,11},{16,20},{18,22},{29,25},{31,27}} | collective-permute-start | bytes 1216520 | tf_op jit(solution)/shard_map/ppermute | solution.py:355
  11.6 10.8 %collective-permute-start.3 = (bf16[264,768]{1,0:T(8,128)(2,1)S(1)}, bf16[264,768]{1,0:T(8,128)(2,1)S(1)}, u32[]{:S(2)}, u32[]{:S(2)}) collective-permute-start(bf16[264,768]{1,0:T(8,128)(2,1)S(1)} %get-tuple-element.43), channel_id=1, source_target_pairs={{0,9},{2,11},{13,4},{15,6},{16,25},{18,27},{29,20},{31,22}} | collective-permute-start | bytes 1216520 | tf_op jit(solution)/shard_map/ppermute | solution.py:355
  13.7 9.3 %collective-permute-start.6 = (bf16[264,768]{1,0:T(8,128)(2,1)S(1)}, bf16[264,768]{1,0:T(8,128)(2,1)S(1)}, u32[]{:S(2)}, u32[]{:S(2)}) collective-permute-start(bf16[264,768]{1,0:T(8,128)(2,1)S(1)} %get-tuple-element.43), channel_id=1, source_target_pairs={{4,9},{6,11},{9,4},{11,6},{0,0},{1,1},{2,2},{3,3},{5,5},{7,7},{8,8... | collective-permute-start | bytes 1216520 | tf_op jit(solution)/shard_map/ppermute | solution.py:355
  14.4 11.4 %collective-permute-start.5 = (bf16[264,768]{1,0:T(8,128)(2,1)S(1)}, bf16[264,768]{1,0:T(8,128)(2,1)S(1)}, u32[]{:S(2)}, u32[]{:S(2)}) collective-permute-start(bf16[264,768]{1,0:T(8,128)(2,1)S(1)} %collective-permute-done.4), channel_id=1, source_target_pairs={{0,9},{2,11},{13,4},{15,6},{16,25},{18,27},{29,20},{31,22}} | collective-permute-start | bytes 1216520 | tf_op jit(solution)/shard_map/ppermute | solution.py:355
  18.1 12.0 %collective-permute-start.7 = (bf16[264,768]{1,0:T(8,128)(2,1)S(1)}, bf16[264,768]{1,0:T(8,128)(2,1)S(1)}, u32[]{:S(2)}, u32[]{:S(2)}) collective-permute-start(bf16[264,768]{1,0:T(8,128)(2,1)S(1)} %collective-permute-done.1.rest_2_.rest_1_), channel_id=1, source_target_pairs={{0,4},{2,6},{13,9},{15,11},{16,20},{18,22},{29,25},{31,27}} | collective-permute-start | bytes 1216520 | tf_op jit(solution)/shard_map/ppermute | solution.py:355
  21.7 8.4 %collective-permute-start.8 = (bf16[264,768]{1,0:T(8,128)(2,1)S(1)}, bf16[264,768]{1,0:T(8,128)(2,1)S(1)}, u32[]{:S(2)}, u32[]{:S(2)}) collective-permute-start(bf16[264,768]{1,0:T(8,128)(2,1)S(1)} %collective-permute-done.4), channel_id=1, source_target_pairs={{4,9},{6,11},{9,4},{11,6},{0,0},{1,1},{2,2},{3,3},{5,5},{7,7},{8,8... | collective-permute-start | bytes 1216520 | tf_op jit(solution)/shard_map/ppermute | solution.py:355
  30.1 2.6 %collective-permute-start.10 = (f32[1,512]{1,0:T(1,128)S(1)}, f32[1,512]{1,0:T(1,128)S(1)}, u32[]{:S(2)}, u32[]{:S(2)}) collective-permute-start(f32[1,512]{1,0:T(1,128)S(1)} %get-tuple-element.67), channel_id=1, source_target_pairs={{4,12},{9,1},{6,14},{11,3},{20,28},{25,17},{22,30},{27,19}} | collective-permute-start | bytes 6152 | tf_op jit(solution)/shard_map/ppermute | solution.py:355
  30.7 10.2 %collective-permute-start.11 = (f32[1,512]{1,0:T(1,128)S(1)}, f32[1,512]{1,0:T(1,128)S(1)}, u32[]{:S(2)}, u32[]{:S(2)}) collective-permute-start(f32[1,512]{1,0:T(1,128)S(1)} %get-tuple-element.68), channel_id=1, source_target_pairs={{4,0},{9,5},{6,2},{11,7},{20,16},{25,21},{22,18},{27,23}} | collective-permute-start | bytes 6152 | tf_op jit(solution)/shard_map/ppermute | solution.py:355
  32.0 8.9 %collective-permute-start.9 = (f32[1,512]{1,0:T(1,128)S(1)}, f32[1,512]{1,0:T(1,128)S(1)}, u32[]{:S(2)}, u32[]{:S(2)}) collective-permute-start(f32[1,512]{1,0:T(1,128)S(1)} %get-tuple-element.66), channel_id=1, source_target_pairs={{4,8},{9,13},{6,10},{11,15},{20,24},{25,29},{22,26},{27,31}} | collective-permute-start | bytes 6152 | tf_op jit(solution)/shard_map/ppermute | solution.py:355

commit v10 on v9

--- a/solution.py
+++ b/solution.py
@@ -394,7 +394,7 @@
     middle_along = to_home(far, from_middle)
     far_after, near_after = to_home(far_crossed, from_far), to_home(near_crossed, from_near)
     middle_after = to_home(far_crossed, from_middle)
-    stages = [[near, near_crossed, near_along, far_along], [far_after, middle_along], [near_after, middle_after]]
+    stages = [[near, near_crossed, near_along, far_along], [far_after, middle_along], [near_after], [middle_after]]
     blocks, states, held = [], [], 0
     state = jax.ShapeDtypeStruct((half, LANES), jnp.float32)
     chunk = jax.ShapeDtypeStruct((1, rows), jnp.float32)
@@ -420,8 +420,11 @@
             *states, members = states
     found = states[0]
     for step in range(1, chain_len):
-        homes = [(low + k % 2, k) for k in range(clus_len)]
-        moves = [(home, k, (home + step) % chain_len, k) for home, k in homes]
+        moves = []
+        for k in range(clus_len):
+            pair = (low + k % 2, (low + k % 2 + step) % chain_len)
+            for z in range(chain_len):
+                moves.append((z, k, pair[1 - pair.index(z)] if z in pair else z, k))
         found = found + permute(states[step], moves)
     return found
 

time: 41.9 us -> 44.2 us (1.055)
  starting transfers between devices: 20.3 us -> 28.5 us
  waiting for transfers between devices: 16.7 us -> 10.8 us
    ppermute x12, starting transfers between devices: 20.3 us -> 28.5 us  [permute(): return lax.ppermute(value, ('chain', 'clus'), pairs)]
    ppermute x12, waiting for transfers between devices: 16.7 us -> 10.8 us  [permute(): return lax.ppermute(value, ('chain', 'clus'), pairs)]
where the time goes in v10:
time: 44.2 us; the launch traced here: 43.8 us
  starting transfers between devices  28.5 us (64%)
  waiting for transfers between devices  10.8 us (24%)
  Pallas kernels  1.91 us (4%)
  local copies, waits for them, and re-layouts  1.83 us (4%)
  other arithmetic  0.58 us (1%)
    ppermute x12, starting transfers between devices, permute(): return lax.ppermute(value, ('chain', 'clus'), pairs)  28.5 us
    ppermute x12, waiting for transfers between devices, permute(): return lax.ppermute(value, ('chain', 'clus'), pairs)  10.8 us
    unnamed x6, local copies, waits for them, and re-layouts  1.83 us
  transfers between devices with their start and end apart: 12, of which 4 were waited for; matrix products, arithmetic and copies ran while one was open for 0% of the time, Pallas kernels for 1%

profile of v10, /device:TPU:0, one launch (start us, length us, event | category | flops | bytes accessed | tf_op | source)
XLA Modules:
  0.0 43.8 jit_solution(5779147517129136547)
XLA Ops:
  0.0 0.0 copy-start.1
  0.0 0.7 %copy-done.1 = s32[512]{0:T(512)S(1)} copy-done((s32[512]{0:T(512)S(1)}, s32[512]{0:T(512)}, u32[]{:S(2)}) %copy-start.1) | copy-done | bytes 2072
  0.7 0.5 %place_rows.1 = (bf16[512,512]{1,0:T(8,128)(2,1)S(1)}, f32[8,256]{1,0:T(8,128)S(1)}, f32[8,256]{1,0:T(8,128)S(1)}) custom-call(s32[1,512]{1,0:T(1,128)S(1)} %bitcast.1), custom_call_target="tpu_custom_call" | custom-call | bytes 3145728 | tf_op jit(solution)/shard_map/place_rows/pallas_call | solution.py:335
  1.2 0.0 copy-start
  1.2 1.1 %copy-done = bf16[512,768]{1,0:T(8,128)(2,1)S(1)} copy-done((bf16[512,768]{1,0:T(8,128)(2,1)S(1)}, bf16[512,768]{1,0:T(8,128)(2,1)}, u32[]{:S(2)}) %copy-start) | copy-done | bytes 786456
  2.4 0.8 %send_blocks.1 = (bf16[256,768]{1,0:T(8,128)(2,1)S(1)}, bf16[264,768]{1,0:T(8,128)(2,1)S(1)}) custom-call(bf16[512,512]{1,0:T(8,128)(2,1)S(1)} %get-tuple-element.51.hot_ref, f32[8,256]{1,0:T(8,128)S(1)} %get-tuple-element.52.slots_ref, bf16[512,768]{1,0:T(8,128)(2,1)S(1)} %copy-done), custom_call_target="tpu_custom_call" | custom-call | tf_op jit(solution)/shard_map/send_blocks/pallas_call | solution.py:344
  3.1 0.5 %collective-permute-start = (bf16[264,768]{1,0:T(8,128)(2,1)S(1)}, bf16[264,768]{1,0:T(8,128)(2,1)S(1)}, u32[]{:S(2)}, u32[]{:S(2)}) collective-permute-start(bf16[264,768]{1,0:T(8,128)(2,1)S(1)} %get-tuple-element.55), channel_id=1, source_target_pairs={{0,1},{1,0},{2,3},{3,2},{4,5},{5,4},{6,7},{7,6},{8,9},{9,8},{10,11... | collective-permute-start | bytes 1216520 | tf_op jit(solution)/shard_map/ppermute | solution.py:355
  3.6 1.4 %collective-permute-done.came_ref = bf16[264,768]{1,0:T(8,128)(2,1)S(1)} collective-permute-done((bf16[264,768]{1,0:T(8,128)(2,1)S(1)}, bf16[264,768]{1,0:T(8,128)(2,1)S(1)}, u32[]{:S(2)}, u32[]{:S(2)}) %collective-permute-start) | collective-permute-done | bytes 405536 | tf_op jit(solution)/shard_map/ppermute | solution.py:355
  5.0 0.1 merge_blocks.1
  5.1 0.0 copy-start.2
  5.1 0.4 collective-permute-start.4
  5.5 2.6 %collective-permute-start.1 = (bf16[264,768]{1,0:T(8,128)(2,1)S(1)}, bf16[264,768]{1,0:T(8,128)(2,1)S(1)}, u32[]{:S(2)}, u32[]{:S(2)}) collective-permute-start(bf16[264,768]{1,0:T(8,128)(2,1)S(1)} %get-tuple-element.56.rest_1_.rest_0_), channel_id=1, source_target_pairs={{1,2},{0,1},{3,0},{2,3},{5,6},{4,5},{7,4},{6,7},{8,11},{9,8},{10,9... | collective-permute-start | bytes 1216520 | tf_op jit(solution)/shard_map/ppermute | solution.py:355
  8.1 4.2 %collective-permute-start.3 = (bf16[264,768]{1,0:T(8,128)(2,1)S(1)}, bf16[264,768]{1,0:T(8,128)(2,1)S(1)}, u32[]{:S(2)}, u32[]{:S(2)}) collective-permute-start(bf16[264,768]{1,0:T(8,128)(2,1)S(1)} %get-tuple-element.57), channel_id=1, source_target_pairs={{0,9},{2,11},{13,4},{15,6},{16,25},{18,27},{29,20},{31,22}} | collective-permute-start | bytes 1216520 | tf_op jit(solution)/shard_map/ppermute | solution.py:355
  12.4 1.3 %collective-permute-start.2 = (bf16[264,768]{1,0:T(8,128)(2,1)S(1)}, bf16[264,768]{1,0:T(8,128)(2,1)S(1)}, u32[]{:S(2)}, u32[]{:S(2)}) collective-permute-start(bf16[264,768]{1,0:T(8,128)(2,1)S(1)} %get-tuple-element.56.rest_1_.rest_0_), channel_id=1, source_target_pairs={{0,4},{2,6},{13,9},{15,11},{16,20},{18,22},{29,25},{31,27}} | collective-permute-start | bytes 1216520 | tf_op jit(solution)/shard_map/ppermute | solution.py:355
  13.7 0.7 %collective-permute-start.6 = (bf16[264,768]{1,0:T(8,128)(2,1)S(1)}, bf16[264,768]{1,0:T(8,128)(2,1)S(1)}, u32[]{:S(2)}, u32[]{:S(2)}) collective-permute-start(bf16[264,768]{1,0:T(8,128)(2,1)S(1)} %get-tuple-element.57), channel_id=1, source_target_pairs={{4,9},{6,11},{9,4},{11,6},{0,0},{1,1},{2,2},{3,3},{5,5},{7,7},{8,8... | collective-permute-start | bytes 1216520 | tf_op jit(solution)/shard_map/ppermute | solution.py:355
  14.4 0.0 collective-permute-done.4
  14.4 3.7 %collective-permute-start.5 = (bf16[264,768]{1,0:T(8,128)(2,1)S(1)}, bf16[264,768]{1,0:T(8,128)(2,1)S(1)}, u32[]{:S(2)}, u32[]{:S(2)}) collective-permute-start(bf16[264,768]{1,0:T(8,128)(2,1)S(1)} %collective-permute-done.4), channel_id=1, source_target_pairs={{0,9},{2,11},{13,4},{15,6},{16,25},{18,27},{29,20},{31,22}} | collective-permute-start | bytes 1216520 | tf_op jit(solution)/shard_map/ppermute | solution.py:355
  18.1 0.0 collective-permute-done.1.rest_2_.rest_1_
  18.1 3.6 %collective-permute-start.7 = (bf16[264,768]{1,0:T(8,128)(2,1)S(1)}, bf16[264,768]{1,0:T(8,128)(2,1)S(1)}, u32[]{:S(2)}, u32[]{:S(2)}) collective-permute-start(bf16[264,768]{1,0:T(8,128)(2,1)S(1)} %collective-permute-done.1.rest_2_.rest_1_), channel_id=1, source_target_pairs={{0,4},{2,6},{13,9},{15,11},{16,20},{18,22},{29,25},{31,27}} | collective-permute-start | bytes 1216520 | tf_op jit(solution)/shard_map/ppermute | solution.py:355
  21.7 0.0 collective-permute-done.3.rest_4_.rest_3_
  21.7 0.7 %collective-permute-start.8 = (bf16[264,768]{1,0:T(8,128)(2,1)S(1)}, bf16[264,768]{1,0:T(8,128)(2,1)S(1)}, u32[]{:S(2)}, u32[]{:S(2)}) collective-permute-start(bf16[264,768]{1,0:T(8,128)(2,1)S(1)} %collective-permute-done.4), channel_id=1, source_target_pairs={{4,9},{6,11},{9,4},{11,6},{0,0},{1,1},{2,2},{3,3},{5,5},{7,7},{8,8... | collective-permute-start | bytes 1216520 | tf_op jit(solution)/shard_map/ppermute | solution.py:355
  22.4 0.0 collective-permute-done.2.rest_3_.rest_2_
  22.4 0.0 copy-done.2
  22.4 0.6 %multiply_arrived.3 = (f32[256,128]{1,0:T(8,128)S(1)}, f32[256,128]{1,0:T(8,128)S(1)}, f32[256,128]{1,0:T(8,128)S(1)}, f32[256,128]{1,0:T(8,128)S(1)}, f32[256,1...) custom-call(s32[4]{0:T(128)S(1)} %copy-done.2, ...), custom_call_target="tpu_custom_call" | custom-call | tf_op jit(solution)/shard_map/multiply_arrived/pallas_call | solution.py:410
  23.0 0.0 collective-permute-done.6.rest_5_.rest_6_
  23.0 3.5 %collective-permute-done.5.rest_4_.rest_5_ = bf16[264,768]{1,0:T(8,128)(2,1)S(1)} collective-permute-done((bf16[264,768]{1,0:T(8,128)(2,1)S(1)}, bf16[264,768]{1,0:T(8,128)(2,1)S(1)}, u32[]{:S(2)}, u32[]{:S(2)}) %collective-permute-start.5) | collective-permute-done | bytes 405536 | tf_op jit(solution)/shard_map/ppermute | solution.py:355
  26.5 4.3 %collective-permute-done.7.rest_6_.rest_7_ = bf16[264,768]{1,0:T(8,128)(2,1)S(1)} collective-permute-done((bf16[264,768]{1,0:T(8,128)(2,1)S(1)}, bf16[264,768]{1,0:T(8,128)(2,1)S(1)}, u32[]{:S(2)}, u32[]{:S(2)}) %collective-permute-start.7) | collective-permute-done | bytes 405536 | tf_op jit(solution)/shard_map/ppermute | solution.py:355
  30.9 0.0 collective-permute-done.8.rest_8_
  30.9 0.7 %collective-permute-start.9 = (f32[1,512]{1,0:T(1,128)S(1)}, f32[1,512]{1,0:T(1,128)S(1)}, u32[]{:S(2)}, u32[]{:S(2)}) collective-permute-start(f32[1,512]{1,0:T(1,128)S(1)} %get-tuple-element.94), channel_id=1, source_target_pairs={{0,0},{4,8},{8,4},{12,12},{1,1},{5,5},{9,13},{13,9},{2,2},{6,10},{... | collective-permute-start | bytes 6152 | tf_op jit(solution)/shard_map/ppermute | solution.py:355
  31.5 0.7 %collective-permute-start.10 = (f32[1,512]{1,0:T(1,128)S(1)}, f32[1,512]{1,0:T(1,128)S(1)}, u32[]{:S(2)}, u32[]{:S(2)}) collective-permute-start(f32[1,512]{1,0:T(1,128)S(1)} %get-tuple-element.95), channel_id=1, source_target_pairs={{0,0},{4,12},{8,8},{12,4},{1,9},{5,5},{9,1},{13,13},{2,2},{6,14},{... | collective-permute-start | bytes 6152 | tf_op jit(solution)/shard_map/ppermute | solution.py:355
  32.2 9.5 %collective-permute-start.11 = (f32[1,512]{1,0:T(1,128)S(1)}, f32[1,512]{1,0:T(1,128)S(1)}, u32[]{:S(2)}, u32[]{:S(2)}) collective-permute-start(f32[1,512]{1,0:T(1,128)S(1)} %get-tuple-element.96), channel_id=1, source_target_pairs={{0,4},{4,0},{8,8},{12,12},{1,1},{5,9},{9,5},{13,13},{2,6},{6,2},{1... | collective-permute-start | bytes 6152 | tf_op jit(solution)/shard_map/ppermute | solution.py:355
  41.7 0.0 collective-permute-done.9
  41.7 0.0 collective-permute-done.10
  41.7 1.5 %collective-permute-done.11 = f32[1,512]{1,0:T(1,128)S(1)} collective-permute-done((f32[1,512]{1,0:T(1,128)S(1)}, f32[1,512]{1,0:T(1,128)S(1)}, u32[]{:S(2)}, u32[]{:S(2)}) %collective-permute-start.11) | collective-permute-done | bytes 2080 | tf_op jit(solution)/shard_map/ppermute | solution.py:355
  43.2 0.6 %add_add_fusion = f32[1,512]{1,0:T(1,128)} fusion(f32[1,512]{1,0:T(1,128)S(1)} %collective-permute-done.11, f32[1,512]{1,0:T(1,128)S(1)} %collective-permute-done.10, f32[1,512]{1,0:T(1,128)S(1)} %get-tuple-element.93, f32[1,512]{1,0:T(1,128)S(1)} %collective-permute-done.9), kind=kLoop, calls=%fused_computation | loop fusion | flops 1536 | bytes 10240 | tf_op jit(solution)/shard_map/add | solution.py:428
  (3 shorter events, 0.0 us)
Async XLA Ops:
  0.0 0.7 %copy-start.1 = (s32[512]{0:T(512)S(1)}, s32[512]{0:T(512)}, u32[]{:S(2)}) copy-start(s32[512]{0:T(512)} %param.4) | copy-start | bytes 6148
  1.2 1.1 %copy-start = (bf16[512,768]{1,0:T(8,128)(2,1)S(1)}, bf16[512,768]{1,0:T(8,128)(2,1)}, u32[]{:S(2)}) copy-start(bf16[512,768]{1,0:T(8,128)(2,1)} %rows_ref.1) | copy-start | bytes 2359300
  3.1 1.9 %collective-permute-start = (bf16[264,768]{1,0:T(8,128)(2,1)S(1)}, bf16[264,768]{1,0:T(8,128)(2,1)S(1)}, u32[]{:S(2)}, u32[]{:S(2)}) collective-permute-start(bf16[264,768]{1,0:T(8,128)(2,1)S(1)} %get-tuple-element.55), channel_id=1, source_target_pairs={{0,1},{1,0},{2,3},{3,2},{4,5},{5,4},{6,7},{7,6},{8,9},{9,8},{10,11... | collective-permute-start | bytes 1216520 | tf_op jit(solution)/shard_map/ppermute | solution.py:355
  5.1 17.3 %copy-start.2 = (s32[4]{0:T(128)S(1)}, s32[4]{0:T(128)}, u32[]{:S(2)}) copy-start(s32[4]{0:T(128)} %rest_0_.1) | copy-start | bytes 52
  5.1 9.3 %collective-permute-start.4 = (bf16[264,768]{1,0:T(8,128)(2,1)S(1)}, bf16[264,768]{1,0:T(8,128)(2,1)S(1)}, u32[]{:S(2)}, u32[]{:S(2)}) collective-permute-start(bf16[264,768]{1,0:T(8,128)(2,1)S(1)} %get-tuple-element.57), channel_id=1, source_target_pairs={{1,2},{0,1},{3,0},{2,3},{5,6},{4,5},{7,4},{6,7},{8,11},{9,8},{10,9... | collective-permute-start | bytes 1216520 | tf_op jit(solution)/shard_map/ppermute | solution.py:355
  5.5 12.6 %collective-permute-start.1 = (bf16[264,768]{1,0:T(8,128)(2,1)S(1)}, bf16[264,768]{1,0:T(8,128)(2,1)S(1)}, u32[]{:S(2)}, u32[]{:S(2)}) collective-permute-start(bf16[264,768]{1,0:T(8,128)(2,1)S(1)} %get-tuple-element.56.rest_1_.rest_0_), channel_id=1, source_target_pairs={{1,2},{0,1},{3,0},{2,3},{5,6},{4,5},{7,4},{6,7},{8,11},{9,8},{10,9... | collective-permute-start | bytes 1216520 | tf_op jit(solution)/shard_map/ppermute | solution.py:355
  8.1 13.6 %collective-permute-start.3 = (bf16[264,768]{1,0:T(8,128)(2,1)S(1)}, bf16[264,768]{1,0:T(8,128)(2,1)S(1)}, u32[]{:S(2)}, u32[]{:S(2)}) collective-permute-start(bf16[264,768]{1,0:T(8,128)(2,1)S(1)} %get-tuple-element.57), channel_id=1, source_target_pairs={{0,9},{2,11},{13,4},{15,6},{16,25},{18,27},{29,20},{31,22}} | collective-permute-start | bytes 1216520 | tf_op jit(solution)/shard_map/ppermute | solution.py:355
  12.4 10.0 %collective-permute-start.2 = (bf16[264,768]{1,0:T(8,128)(2,1)S(1)}, bf16[264,768]{1,0:T(8,128)(2,1)S(1)}, u32[]{:S(2)}, u32[]{:S(2)}) collective-permute-start(bf16[264,768]{1,0:T(8,128)(2,1)S(1)} %get-tuple-element.56.rest_1_.rest_0_), channel_id=1, source_target_pairs={{0,4},{2,6},{13,9},{15,11},{16,20},{18,22},{29,25},{31,27}} | collective-permute-start | bytes 1216520 | tf_op jit(solution)/shard_map/ppermute | solution.py:355
  13.7 9.3 %collective-permute-start.6 = (bf16[264,768]{1,0:T(8,128)(2,1)S(1)}, bf16[264,768]{1,0:T(8,128)(2,1)S(1)}, u32[]{:S(2)}, u32[]{:S(2)}) collective-permute-start(bf16[264,768]{1,0:T(8,128)(2,1)S(1)} %get-tuple-element.57), channel_id=1, source_target_pairs={{4,9},{6,11},{9,4},{11,6},{0,0},{1,1},{2,2},{3,3},{5,5},{7,7},{8,8... | collective-permute-start | bytes 1216520 | tf_op jit(solution)/shard_map/ppermute | solution.py:355
  14.4 12.1 %collective-permute-start.5 = (bf16[264,768]{1,0:T(8,128)(2,1)S(1)}, bf16[264,768]{1,0:T(8,128)(2,1)S(1)}, u32[]{:S(2)}, u32[]{:S(2)}) collective-permute-start(bf16[264,768]{1,0:T(8,128)(2,1)S(1)} %collective-permute-done.4), channel_id=1, source_target_pairs={{0,9},{2,11},{13,4},{15,6},{16,25},{18,27},{29,20},{31,22}} | collective-permute-start | bytes 1216520 | tf_op jit(solution)/shard_map/ppermute | solution.py:355
  18.1 12.8 %collective-permute-start.7 = (bf16[264,768]{1,0:T(8,128)(2,1)S(1)}, bf16[264,768]{1,0:T(8,128)(2,1)S(1)}, u32[]{:S(2)}, u32[]{:S(2)}) collective-permute-start(bf16[264,768]{1,0:T(8,128)(2,1)S(1)} %collective-permute-done.1.rest_2_.rest_1_), channel_id=1, source_target_pairs={{0,4},{2,6},{13,9},{15,11},{16,20},{18,22},{29,25},{31,27}} | collective-permute-start | bytes 1216520 | tf_op jit(solution)/shard_map/ppermute | solution.py:355
  21.7 9.2 %collective-permute-start.8 = (bf16[264,768]{1,0:T(8,128)(2,1)S(1)}, bf16[264,768]{1,0:T(8,128)(2,1)S(1)}, u32[]{:S(2)}, u32[]{:S(2)}) collective-permute-start(bf16[264,768]{1,0:T(8,128)(2,1)S(1)} %collective-permute-done.4), channel_id=1, source_target_pairs={{4,9},{6,11},{9,4},{11,6},{0,0},{1,1},{2,2},{3,3},{5,5},{7,7},{8,8... | collective-permute-start | bytes 1216520 | tf_op jit(solution)/shard_map/ppermute | solution.py:355
  30.9 10.8 %collective-permute-start.9 = (f32[1,512]{1,0:T(1,128)S(1)}, f32[1,512]{1,0:T(1,128)S(1)}, u32[]{:S(2)}, u32[]{:S(2)}) collective-permute-start(f32[1,512]{1,0:T(1,128)S(1)} %get-tuple-element.94), channel_id=1, source_target_pairs={{0,0},{4,8},{8,4},{12,12},{1,1},{5,5},{9,13},{13,9},{2,2},{6,10},{... | collective-permute-start | bytes 6152 | tf_op jit(solution)/shard_map/ppermute | solution.py:355
  31.5 10.2 %collective-permute-start.10 = (f32[1,512]{1,0:T(1,128)S(1)}, f32[1,512]{1,0:T(1,128)S(1)}, u32[]{:S(2)}, u32[]{:S(2)}) collective-permute-start(f32[1,512]{1,0:T(1,128)S(1)} %get-tuple-element.95), channel_id=1, source_target_pairs={{0,0},{4,12},{8,8},{12,4},{1,9},{5,5},{9,1},{13,13},{2,2},{6,14},{... | collective-permute-start | bytes 6152 | tf_op jit(solution)/shard_map/ppermute | solution.py:355
  32.2 11.0 %collective-permute-start.11 = (f32[1,512]{1,0:T(1,128)S(1)}, f32[1,512]{1,0:T(1,128)S(1)}, u32[]{:S(2)}, u32[]{:S(2)}) collective-permute-start(f32[1,512]{1,0:T(1,128)S(1)} %get-tuple-element.96), channel_id=1, source_target_pairs={{0,4},{4,0},{8,8},{12,12},{1,1},{5,9},{9,5},{13,13},{2,6},{6,2},{1... | collective-permute-start | bytes 6152 | tf_op jit(solution)/shard_map/ppermute | solution.py:355

commit v11 on v9

--- a/solution.py
+++ b/solution.py
@@ -394,7 +394,7 @@
     middle_along = to_home(far, from_middle)
     far_after, near_after = to_home(far_crossed, from_far), to_home(near_crossed, from_near)
     middle_after = to_home(far_crossed, from_middle)
-    stages = [[near, near_crossed, near_along, far_along], [far_after, middle_along], [near_after, middle_after]]
+    stages = [[near, near_crossed, near_along, far_along], [far_after, middle_along], [near_after], [middle_after]]
     blocks, states, held = [], [], 0
     state = jax.ShapeDtypeStruct((half, LANES), jnp.float32)
     chunk = jax.ShapeDtypeStruct((1, rows), jnp.float32)

time: 41.9 us -> 42.3 us (level)
  no operation moved by 1% of the time
where the time goes in v11:
time: 42.3 us; the launch traced here: 41.9 us
  starting transfers between devices  20.3 us (48%)
  waiting for transfers between devices  17.1 us (40%)
  Pallas kernels  1.91 us (5%)
  local copies, waits for them, and re-layouts  1.83 us (4%)
  other arithmetic  0.58 us (1%)
    ppermute x12, starting transfers between devices, permute(): return lax.ppermute(value, ('chain', 'clus'), pairs)  20.3 us
    ppermute x12, waiting for transfers between devices, permute(): return lax.ppermute(value, ('chain', 'clus'), pairs)  17.1 us
    unnamed x6, local copies, waits for them, and re-layouts  1.83 us
  transfers between devices with their start and end apart: 12, of which 4 were waited for; matrix products, arithmetic and copies ran while one was open for 0% of the time, Pallas kernels for 1%

profile of v11, /device:TPU:0, one launch (start us, length us, event | category | flops | bytes accessed | tf_op | source)
XLA Modules:
  0.0 41.9 jit_solution(16930285930896033021)
XLA Ops:
  0.0 0.0 copy-start.1
  0.0 0.7 %copy-done.1 = s32[512]{0:T(512)S(1)} copy-done((s32[512]{0:T(512)S(1)}, s32[512]{0:T(512)}, u32[]{:S(2)}) %copy-start.1) | copy-done | bytes 2072
  0.7 0.5 %place_rows.1 = (bf16[512,512]{1,0:T(8,128)(2,1)S(1)}, f32[8,256]{1,0:T(8,128)S(1)}, f32[8,256]{1,0:T(8,128)S(1)}) custom-call(s32[1,512]{1,0:T(1,128)S(1)} %bitcast.1), custom_call_target="tpu_custom_call" | custom-call | bytes 3145728 | tf_op jit(solution)/shard_map/place_rows/pallas_call | solution.py:335
  1.2 0.0 copy-start
  1.2 1.1 %copy-done = bf16[512,768]{1,0:T(8,128)(2,1)S(1)} copy-done((bf16[512,768]{1,0:T(8,128)(2,1)S(1)}, bf16[512,768]{1,0:T(8,128)(2,1)}, u32[]{:S(2)}) %copy-start) | copy-done | bytes 786456
  2.4 0.8 %send_blocks.1 = (bf16[256,768]{1,0:T(8,128)(2,1)S(1)}, bf16[264,768]{1,0:T(8,128)(2,1)S(1)}) custom-call(bf16[512,512]{1,0:T(8,128)(2,1)S(1)} %get-tuple-element.51.hot_ref, f32[8,256]{1,0:T(8,128)S(1)} %get-tuple-element.52.slots_ref, bf16[512,768]{1,0:T(8,128)(2,1)S(1)} %copy-done), custom_call_target="tpu_custom_call" | custom-call | tf_op jit(solution)/shard_map/send_blocks/pallas_call | solution.py:344
  3.1 0.5 %collective-permute-start = (bf16[264,768]{1,0:T(8,128)(2,1)S(1)}, bf16[264,768]{1,0:T(8,128)(2,1)S(1)}, u32[]{:S(2)}, u32[]{:S(2)}) collective-permute-start(bf16[264,768]{1,0:T(8,128)(2,1)S(1)} %get-tuple-element.55), channel_id=1, source_target_pairs={{0,1},{1,0},{2,3},{3,2},{4,5},{5,4},{6,7},{7,6},{8,9},{9,8},{10,11... | collective-permute-start | bytes 1216520 | tf_op jit(solution)/shard_map/ppermute | solution.py:355
  3.6 1.4 %collective-permute-done.came_ref = bf16[264,768]{1,0:T(8,128)(2,1)S(1)} collective-permute-done((bf16[264,768]{1,0:T(8,128)(2,1)S(1)}, bf16[264,768]{1,0:T(8,128)(2,1)S(1)}, u32[]{:S(2)}, u32[]{:S(2)}) %collective-permute-start) | collective-permute-done | bytes 405536 | tf_op jit(solution)/shard_map/ppermute | solution.py:355
  5.0 0.1 merge_blocks.1
  5.1 0.0 copy-start.2
  5.1 0.4 %collective-permute-start.4 = (bf16[264,768]{1,0:T(8,128)(2,1)S(1)}, bf16[264,768]{1,0:T(8,128)(2,1)S(1)}, u32[]{:S(2)}, u32[]{:S(2)}) collective-permute-start(bf16[264,768]{1,0:T(8,128)(2,1)S(1)} %get-tuple-element.57), channel_id=1, source_target_pairs={{1,2},{0,1},{3,0},{2,3},{5,6},{4,5},{7,4},{6,7},{8,11},{9,8},{10,9... | collective-permute-start | bytes 1216520 | tf_op jit(solution)/shard_map/ppermute | solution.py:355
  5.5 2.6 %collective-permute-start.1 = (bf16[264,768]{1,0:T(8,128)(2,1)S(1)}, bf16[264,768]{1,0:T(8,128)(2,1)S(1)}, u32[]{:S(2)}, u32[]{:S(2)}) collective-permute-start(bf16[264,768]{1,0:T(8,128)(2,1)S(1)} %get-tuple-element.56.rest_1_.rest_0_), channel_id=1, source_target_pairs={{1,2},{0,1},{3,0},{2,3},{5,6},{4,5},{7,4},{6,7},{8,11},{9,8},{10,9... | collective-permute-start | bytes 1216520 | tf_op jit(solution)/shard_map/ppermute | solution.py:355
  8.1 4.2 %collective-permute-start.3 = (bf16[264,768]{1,0:T(8,128)(2,1)S(1)}, bf16[264,768]{1,0:T(8,128)(2,1)S(1)}, u32[]{:S(2)}, u32[]{:S(2)}) collective-permute-start(bf16[264,768]{1,0:T(8,128)(2,1)S(1)} %get-tuple-element.57), channel_id=1, source_target_pairs={{0,9},{2,11},{13,4},{15,6},{16,25},{18,27},{29,20},{31,22}} | collective-permute-start | bytes 1216520 | tf_op jit(solution)/shard_map/ppermute | solution.py:355
  12.4 1.3 %collective-permute-start.2 = (bf16[264,768]{1,0:T(8,128)(2,1)S(1)}, bf16[264,768]{1,0:T(8,128)(2,1)S(1)}, u32[]{:S(2)}, u32[]{:S(2)}) collective-permute-start(bf16[264,768]{1,0:T(8,128)(2,1)S(1)} %get-tuple-element.56.rest_1_.rest_0_), channel_id=1, source_target_pairs={{0,4},{2,6},{13,9},{15,11},{16,20},{18,22},{29,25},{31,27}} | collective-permute-start | bytes 1216520 | tf_op jit(solution)/shard_map/ppermute | solution.py:355
  13.7 0.7 %collective-permute-start.6 = (bf16[264,768]{1,0:T(8,128)(2,1)S(1)}, bf16[264,768]{1,0:T(8,128)(2,1)S(1)}, u32[]{:S(2)}, u32[]{:S(2)}) collective-permute-start(bf16[264,768]{1,0:T(8,128)(2,1)S(1)} %get-tuple-element.57), channel_id=1, source_target_pairs={{4,9},{6,11},{9,4},{11,6},{0,0},{1,1},{2,2},{3,3},{5,5},{7,7},{8,8... | collective-permute-start | bytes 1216520 | tf_op jit(solution)/shard_map/ppermute | solution.py:355
  14.4 0.0 collective-permute-done.4
  14.4 3.7 %collective-permute-start.5 = (bf16[264,768]{1,0:T(8,128)(2,1)S(1)}, bf16[264,768]{1,0:T(8,128)(2,1)S(1)}, u32[]{:S(2)}, u32[]{:S(2)}) collective-permute-start(bf16[264,768]{1,0:T(8,128)(2,1)S(1)} %collective-permute-done.4), channel_id=1, source_target_pairs={{0,9},{2,11},{13,4},{15,6},{16,25},{18,27},{29,20},{31,22}} | collective-permute-start | bytes 1216520 | tf_op jit(solution)/shard_map/ppermute | solution.py:355
  18.1 0.0 collective-permute-done.1.rest_2_.rest_1_
  18.1 3.6 %collective-permute-start.7 = (bf16[264,768]{1,0:T(8,128)(2,1)S(1)}, bf16[264,768]{1,0:T(8,128)(2,1)S(1)}, u32[]{:S(2)}, u32[]{:S(2)}) collective-permute-start(bf16[264,768]{1,0:T(8,128)(2,1)S(1)} %collective-permute-done.1.rest_2_.rest_1_), channel_id=1, source_target_pairs={{0,4},{2,6},{13,9},{15,11},{16,20},{18,22},{29,25},{31,27}} | collective-permute-start | bytes 1216520 | tf_op jit(solution)/shard_map/ppermute | solution.py:355
  21.7 0.0 collective-permute-done.3.rest_4_.rest_3_
  21.7 0.7 %collective-permute-start.8 = (bf16[264,768]{1,0:T(8,128)(2,1)S(1)}, bf16[264,768]{1,0:T(8,128)(2,1)S(1)}, u32[]{:S(2)}, u32[]{:S(2)}) collective-permute-start(bf16[264,768]{1,0:T(8,128)(2,1)S(1)} %collective-permute-done.4), channel_id=1, source_target_pairs={{4,9},{6,11},{9,4},{11,6},{0,0},{1,1},{2,2},{3,3},{5,5},{7,7},{8,8... | collective-permute-start | bytes 1216520 | tf_op jit(solution)/shard_map/ppermute | solution.py:355
  22.4 0.0 collective-permute-done.2.rest_3_.rest_2_
  22.4 0.0 copy-done.2
  22.4 0.6 %multiply_arrived.3 = (f32[256,128]{1,0:T(8,128)S(1)}, f32[256,128]{1,0:T(8,128)S(1)}, f32[256,128]{1,0:T(8,128)S(1)}, f32[256,128]{1,0:T(8,128)S(1)}, f32[256,1...) custom-call(s32[4]{0:T(128)S(1)} %copy-done.2, ...), custom_call_target="tpu_custom_call" | custom-call | tf_op jit(solution)/shard_map/multiply_arrived/pallas_call | solution.py:410
  23.0 0.0 collective-permute-done.6.rest_5_.rest_6_
  23.0 3.5 %collective-permute-done.5.rest_4_.rest_5_ = bf16[264,768]{1,0:T(8,128)(2,1)S(1)} collective-permute-done((bf16[264,768]{1,0:T(8,128)(2,1)S(1)}, bf16[264,768]{1,0:T(8,128)(2,1)S(1)}, u32[]{:S(2)}, u32[]{:S(2)}) %collective-permute-start.5) | collective-permute-done | bytes 405536 | tf_op jit(solution)/shard_map/ppermute | solution.py:355
  26.5 4.3 %collective-permute-done.7.rest_6_.rest_7_ = bf16[264,768]{1,0:T(8,128)(2,1)S(1)} collective-permute-done((bf16[264,768]{1,0:T(8,128)(2,1)S(1)}, bf16[264,768]{1,0:T(8,128)(2,1)S(1)}, u32[]{:S(2)}, u32[]{:S(2)}) %collective-permute-start.7) | collective-permute-done | bytes 405536 | tf_op jit(solution)/shard_map/ppermute | solution.py:355
  30.9 0.0 collective-permute-done.8.rest_8_
  30.9 0.7 %collective-permute-start.9 = (f32[1,512]{1,0:T(1,128)S(1)}, f32[1,512]{1,0:T(1,128)S(1)}, u32[]{:S(2)}, u32[]{:S(2)}) collective-permute-start(f32[1,512]{1,0:T(1,128)S(1)} %get-tuple-element.94), channel_id=1, source_target_pairs={{4,8},{9,13},{6,10},{11,15},{20,24},{25,29},{22,26},{27,31}} | collective-permute-start | bytes 6152 | tf_op jit(solution)/shard_map/ppermute | solution.py:355
  31.5 0.7 %collective-permute-start.10 = (f32[1,512]{1,0:T(1,128)S(1)}, f32[1,512]{1,0:T(1,128)S(1)}, u32[]{:S(2)}, u32[]{:S(2)}) collective-permute-start(f32[1,512]{1,0:T(1,128)S(1)} %get-tuple-element.95), channel_id=1, source_target_pairs={{4,12},{9,1},{6,14},{11,3},{20,28},{25,17},{22,30},{27,19}} | collective-permute-start | bytes 6152 | tf_op jit(solution)/shard_map/ppermute | solution.py:355
  32.2 1.3 %collective-permute-start.11 = (f32[1,512]{1,0:T(1,128)S(1)}, f32[1,512]{1,0:T(1,128)S(1)}, u32[]{:S(2)}, u32[]{:S(2)}) collective-permute-start(f32[1,512]{1,0:T(1,128)S(1)} %get-tuple-element.96), channel_id=1, source_target_pairs={{4,0},{9,5},{6,2},{11,7},{20,16},{25,21},{22,18},{27,23}} | collective-permute-start | bytes 6152 | tf_op jit(solution)/shard_map/ppermute | solution.py:355
  33.5 0.0 collective-permute-done.9
  33.5 0.0 collective-permute-done.10
  33.5 7.8 %collective-permute-done.11 = f32[1,512]{1,0:T(1,128)S(1)} collective-permute-done((f32[1,512]{1,0:T(1,128)S(1)}, f32[1,512]{1,0:T(1,128)S(1)}, u32[]{:S(2)}, u32[]{:S(2)}) %collective-permute-start.11) | collective-permute-done | bytes 2080 | tf_op jit(solution)/shard_map/ppermute | solution.py:355
  41.4 0.6 %add_add_fusion = f32[1,512]{1,0:T(1,128)} fusion(f32[1,512]{1,0:T(1,128)S(1)} %collective-permute-done.11, f32[1,512]{1,0:T(1,128)S(1)} %collective-permute-done.10, f32[1,512]{1,0:T(1,128)S(1)} %get-tuple-element.93, f32[1,512]{1,0:T(1,128)S(1)} %collective-permute-done.9), kind=kLoop, calls=%fused_computation | loop fusion | flops 1536 | bytes 10240 | tf_op jit(solution)/shard_map/add | solution.py:425
  (3 shorter events, 0.0 us)
Async XLA Ops:
  0.0 0.7 %copy-start.1 = (s32[512]{0:T(512)S(1)}, s32[512]{0:T(512)}, u32[]{:S(2)}) copy-start(s32[512]{0:T(512)} %param.4) | copy-start | bytes 6148
  1.2 1.1 %copy-start = (bf16[512,768]{1,0:T(8,128)(2,1)S(1)}, bf16[512,768]{1,0:T(8,128)(2,1)}, u32[]{:S(2)}) copy-start(bf16[512,768]{1,0:T(8,128)(2,1)} %rows_ref.1) | copy-start | bytes 2359300
  3.1 1.9 %collective-permute-start = (bf16[264,768]{1,0:T(8,128)(2,1)S(1)}, bf16[264,768]{1,0:T(8,128)(2,1)S(1)}, u32[]{:S(2)}, u32[]{:S(2)}) collective-permute-start(bf16[264,768]{1,0:T(8,128)(2,1)S(1)} %get-tuple-element.55), channel_id=1, source_target_pairs={{0,1},{1,0},{2,3},{3,2},{4,5},{5,4},{6,7},{7,6},{8,9},{9,8},{10,11... | collective-permute-start | bytes 1216520 | tf_op jit(solution)/shard_map/ppermute | solution.py:355
  5.1 17.3 %copy-start.2 = (s32[4]{0:T(128)S(1)}, s32[4]{0:T(128)}, u32[]{:S(2)}) copy-start(s32[4]{0:T(128)} %rest_0_.1) | copy-start | bytes 52
  5.1 9.3 %collective-permute-start.4 = (bf16[264,768]{1,0:T(8,128)(2,1)S(1)}, bf16[264,768]{1,0:T(8,128)(2,1)S(1)}, u32[]{:S(2)}, u32[]{:S(2)}) collective-permute-start(bf16[264,768]{1,0:T(8,128)(2,1)S(1)} %get-tuple-element.57), channel_id=1, source_target_pairs={{1,2},{0,1},{3,0},{2,3},{5,6},{4,5},{7,4},{6,7},{8,11},{9,8},{10,9... | collective-permute-start | bytes 1216520 | tf_op jit(solution)/shard_map/ppermute | solution.py:355
  5.5 12.6 %collective-permute-start.1 = (bf16[264,768]{1,0:T(8,128)(2,1)S(1)}, bf16[264,768]{1,0:T(8,128)(2,1)S(1)}, u32[]{:S(2)}, u32[]{:S(2)}) collective-permute-start(bf16[264,768]{1,0:T(8,128)(2,1)S(1)} %get-tuple-element.56.rest_1_.rest_0_), channel_id=1, source_target_pairs={{1,2},{0,1},{3,0},{2,3},{5,6},{4,5},{7,4},{6,7},{8,11},{9,8},{10,9... | collective-permute-start | bytes 1216520 | tf_op jit(solution)/shard_map/ppermute | solution.py:355
  8.1 13.6 %collective-permute-start.3 = (bf16[264,768]{1,0:T(8,128)(2,1)S(1)}, bf16[264,768]{1,0:T(8,128)(2,1)S(1)}, u32[]{:S(2)}, u32[]{:S(2)}) collective-permute-start(bf16[264,768]{1,0:T(8,128)(2,1)S(1)} %get-tuple-element.57), channel_id=1, source_target_pairs={{0,9},{2,11},{13,4},{15,6},{16,25},{18,27},{29,20},{31,22}} | collective-permute-start | bytes 1216520 | tf_op jit(solution)/shard_map/ppermute | solution.py:355
  12.4 10.0 %collective-permute-start.2 = (bf16[264,768]{1,0:T(8,128)(2,1)S(1)}, bf16[264,768]{1,0:T(8,128)(2,1)S(1)}, u32[]{:S(2)}, u32[]{:S(2)}) collective-permute-start(bf16[264,768]{1,0:T(8,128)(2,1)S(1)} %get-tuple-element.56.rest_1_.rest_0_), channel_id=1, source_target_pairs={{0,4},{2,6},{13,9},{15,11},{16,20},{18,22},{29,25},{31,27}} | collective-permute-start | bytes 1216520 | tf_op jit(solution)/shard_map/ppermute | solution.py:355
  13.7 9.3 %collective-permute-start.6 = (bf16[264,768]{1,0:T(8,128)(2,1)S(1)}, bf16[264,768]{1,0:T(8,128)(2,1)S(1)}, u32[]{:S(2)}, u32[]{:S(2)}) collective-permute-start(bf16[264,768]{1,0:T(8,128)(2,1)S(1)} %get-tuple-element.57), channel_id=1, source_target_pairs={{4,9},{6,11},{9,4},{11,6},{0,0},{1,1},{2,2},{3,3},{5,5},{7,7},{8,8... | collective-permute-start | bytes 1216520 | tf_op jit(solution)/shard_map/ppermute | solution.py:355
  14.4 12.1 %collective-permute-start.5 = (bf16[264,768]{1,0:T(8,128)(2,1)S(1)}, bf16[264,768]{1,0:T(8,128)(2,1)S(1)}, u32[]{:S(2)}, u32[]{:S(2)}) collective-permute-start(bf16[264,768]{1,0:T(8,128)(2,1)S(1)} %collective-permute-done.4), channel_id=1, source_target_pairs={{0,9},{2,11},{13,4},{15,6},{16,25},{18,27},{29,20},{31,22}} | collective-permute-start | bytes 1216520 | tf_op jit(solution)/shard_map/ppermute | solution.py:355
  18.1 12.8 %collective-permute-start.7 = (bf16[264,768]{1,0:T(8,128)(2,1)S(1)}, bf16[264,768]{1,0:T(8,128)(2,1)S(1)}, u32[]{:S(2)}, u32[]{:S(2)}) collective-permute-start(bf16[264,768]{1,0:T(8,128)(2,1)S(1)} %collective-permute-done.1.rest_2_.rest_1_), channel_id=1, source_target_pairs={{0,4},{2,6},{13,9},{15,11},{16,20},{18,22},{29,25},{31,27}} | collective-permute-start | bytes 1216520 | tf_op jit(solution)/shard_map/ppermute | solution.py:355
  21.7 9.2 %collective-permute-start.8 = (bf16[264,768]{1,0:T(8,128)(2,1)S(1)}, bf16[264,768]{1,0:T(8,128)(2,1)S(1)}, u32[]{:S(2)}, u32[]{:S(2)}) collective-permute-start(bf16[264,768]{1,0:T(8,128)(2,1)S(1)} %collective-permute-done.4), channel_id=1, source_target_pairs={{4,9},{6,11},{9,4},{11,6},{0,0},{1,1},{2,2},{3,3},{5,5},{7,7},{8,8... | collective-permute-start | bytes 1216520 | tf_op jit(solution)/shard_map/ppermute | solution.py:355
  30.9 2.6 %collective-permute-start.9 = (f32[1,512]{1,0:T(1,128)S(1)}, f32[1,512]{1,0:T(1,128)S(1)}, u32[]{:S(2)}, u32[]{:S(2)}) collective-permute-start(f32[1,512]{1,0:T(1,128)S(1)} %get-tuple-element.94), channel_id=1, source_target_pairs={{4,8},{9,13},{6,10},{11,15},{20,24},{25,29},{22,26},{27,31}} | collective-permute-start | bytes 6152 | tf_op jit(solution)/shard_map/ppermute | solution.py:355
  31.5 2.0 %collective-permute-start.10 = (f32[1,512]{1,0:T(1,128)S(1)}, f32[1,512]{1,0:T(1,128)S(1)}, u32[]{:S(2)}, u32[]{:S(2)}) collective-permute-start(f32[1,512]{1,0:T(1,128)S(1)} %get-tuple-element.95), channel_id=1, source_target_pairs={{4,12},{9,1},{6,14},{11,3},{20,28},{25,17},{22,30},{27,19}} | collective-permute-start | bytes 6152 | tf_op jit(solution)/shard_map/ppermute | solution.py:355
  32.2 9.1 %collective-permute-start.11 = (f32[1,512]{1,0:T(1,128)S(1)}, f32[1,512]{1,0:T(1,128)S(1)}, u32[]{:S(2)}, u32[]{:S(2)}) collective-permute-start(f32[1,512]{1,0:T(1,128)S(1)} %get-tuple-element.96), channel_id=1, source_target_pairs={{4,0},{9,5},{6,2},{11,7},{20,16},{25,21},{22,18},{27,23}} | collective-permute-start | bytes 6152 | tf_op jit(solution)/shard_map/ppermute | solution.py:355

commit v12 on v11

--- a/solution.py
+++ b/solution.py
@@ -166,13 +166,11 @@
     return lax.ppermute(found, ("chain", "clus"), pairs)
 
 
-def place_kernel(run_slots, cluster_runs, dest_ref, hot_ref, kept_slots_ref, given_slots_ref):
+def place_kernel(run_slots, cluster_runs, dest_ref, hot_ref, slots_ref):
     rows = dest_ref.shape[1]
     runs = rows // PIECE
-    half = rows // 2
-    clus = lax.axis_index("clus")
     upper = (lax.axis_index("chain") >= lax.axis_size("chain") // 2).astype(jnp.int32)
-    code = (clus // 2 ^ clus % 2 ^ upper) * 2 + upper
+    code = lax.axis_index("clus") // 2 * 2 + upper
     before = lax.broadcasted_iota(jnp.int32, (rows, rows), 0) < lax.broadcasted_iota(
         jnp.int32, (rows, rows), 1
     )
@@ -185,39 +183,44 @@
     rank = jnp.sum(jnp.where(member, earlier, 0.0), axis=0, keepdims=True).astype(jnp.int32)
     hot = as_bf16(lax.broadcasted_iota(jnp.int32, (rows, rows), 0) == run * PIECE + rank)
     hot_ref[...] = hot
-    moved = lax.dot_general(
+    slots_ref[...] = lax.dot_general(
         jnp.broadcast_to(within, (TILE, rows)).astype(jnp.float32).astype(jnp.bfloat16),
         hot,
         (((1,), (1,)), ((), ())),
         preferred_element_type=jnp.float32,
     )
-    line = lax.broadcasted_iota(jnp.int32, (TILE, half), 0)
-    kept_slots_ref[...] = jnp.where(line == 0, moved[:, 0:half], 0.0)
-    given_slots_ref[...] = jnp.where(line == 1, moved[:, half:rows], 0.0)
-
-
-def send_kernel(hot_ref, slots_ref, rows_ref, kept_ref, given_ref):
+
+
+def send_kernel(hot_ref, slots_ref, rows_ref, *block_refs):
     rows, width = rows_ref.shape
-    half = rows // 2
+    depth = rows // len(block_refs)
     x = rows_ref[...].astype(jnp.float32)
     units = (x * lax.rsqrt(jnp.sum(x * x, axis=1, keepdims=True) + 1e-06)).astype(jnp.bfloat16)
-    for low, ref in ((0, kept_ref), (half, given_ref)):
-        ref[0:half, :] = jnp.dot(
-            hot_ref[low : low + half, :], units, preferred_element_type=jnp.float32
+    for index, ref in enumerate(block_refs):
+        low = index * depth
+        ref[0:depth, :] = jnp.dot(
+            hot_ref[low : low + depth, :], units, preferred_element_type=jnp.float32
         ).astype(jnp.bfloat16)
-    given_ref[half : half + TILE, :] = jnp.zeros((TILE, width), jnp.bfloat16)
-    given_ref[half : half + TILE, 0:half] = slots_ref[...].astype(jnp.bfloat16)
-
-
-def merge_kernel(kept_ref, slots_ref, came_ref, near_ref, far_ref):
-    half, width = kept_ref.shape
-    depth = half // 2
-    slots = slots_ref[...] + came_ref[half : half + TILE, 0:half].astype(jnp.float32)
-    for low, ref in ((0, near_ref), (depth, far_ref)):
-        ref[0:depth, :] = kept_ref[low : low + depth, :]
-        ref[depth:half, :] = came_ref[low : low + depth, :]
-        ref[half : half + TILE, :] = jnp.zeros((TILE, width), jnp.bfloat16)
-        ref[half : half + TILE, 0:depth] = slots[:, low : low + depth].astype(jnp.bfloat16)
+        ref[depth : depth + TILE, :] = jnp.zeros((TILE, width), jnp.bfloat16)
+        ref[depth : depth + TILE, 0:depth] = slots_ref[:, low : low + depth].astype(jnp.bfloat16)
+
+
+def merge_kernel(mine_ref, came_ref, out_ref):
+    depth = mine_ref.shape[0] - TILE
+    out_ref[0:depth, :] = mine_ref[0:depth, :]
+    out_ref[depth : 2 * depth, :] = came_ref[0:depth, :]
+    line = lax.broadcasted_iota(jnp.int32, (TILE, out_ref.shape[1]), 0)
+    mine, came = (ref[depth : depth + TILE, :].astype(jnp.float32) for ref in (mine_ref, came_ref))
+    out_ref[2 * depth :, :] = jnp.where(line == 0, mine, came).astype(jnp.bfloat16)
+
+
+def helper_kernel(count, *refs):
+    out_ref = refs[-1]
+    depth = refs[0].shape[0] - TILE
+    for index, ref in enumerate(refs[:count]):
+        out_ref[index * depth : (index + 1) * depth, :] = ref[0:depth, :]
+        low = count * depth + index * TILE
+        out_ref[low : low + TILE, :] = ref[depth : depth + TILE, :]
 
 
 def home_chain():
@@ -227,9 +230,19 @@
 def stage_kernel(run_slots, height, count, old, new, last, *rest):
     first = old == 0
     count_ref, rest = (rest[0], rest[1:]) if first or last else (None, rest)
-    refs = []
+    depth = (height - TILE) // 2
+    parts = []
     for ref in rest[:count]:
-        refs += [ref.at[pl.ds(low, height)] for low in range(0, ref.shape[0], height)]
+        size = ref.shape[0] // depth
+        if ref.shape[0] == height:
+            parts += [(ref, 0, 2 * depth, TILE, 0), (ref, depth, 2 * depth, TILE, 1)]
+        elif size == 1:
+            parts.append((ref, 0, depth, TILE, 0))
+        else:
+            for at in range(size):
+                tile = size * depth + at // 2 * 2 * TILE
+                parts.append((ref, at * depth, tile, 2 * TILE, at % 2 * TILE))
+    refs = [parts[at : at + 2] for at in range(0, len(parts), 2)]
     rest = rest[count:]
     old_states, rest = rest[: 2 * old], rest[2 * old :]
     if last:
@@ -237,8 +250,7 @@
         states, found_ref = rest[len(chunk_refs) : -1], rest[-1]
     else:
         states = rest[: 2 * (old + new)]
-    rows = refs[0].shape[0] - TILE
-    depth = rows // 2
+    rows = 2 * depth
     runs = depth // PIECE
     is_home = lax.axis_index("chain") == home_chain()
 
@@ -251,6 +263,12 @@
     if first:
         members = count_ref[lax.axis_index("clus")].astype(jnp.float32)
         rest[-1][...] = jnp.full_like(rest[-1], members)
+
+    def load(index):
+        (ref, low, *_), (other, _, *_) = refs[index]
+        if ref is other:
+            return ref[low : low + rows, :]
+        return jnp.concatenate([part[0][0:depth, :] for part in refs[index]], axis=0)
 
     @pl.when(is_home)
     def _():
@@ -262,16 +280,21 @@
         )
         run_of = lax.broadcasted_iota(jnp.int32, (1, depth), 1) // PIECE
         for index in range(old, old + new):
-            slots = refs[index][rows : rows + TILE, 0:depth].astype(jnp.float32)
             start = (run_of * run_slots).astype(jnp.float32)
-            line = jnp.concatenate([slots[0:1] + start, slots[1:2] + start], axis=1)
+            line = jnp.concatenate(
+                [
+                    ref[at : at + size, 0:depth].astype(jnp.float32)[row : row + 1] + start
+                    for ref, _, at, size, row in refs[index]
+                ],
+                axis=1,
+            )
             column = jnp.sum(jnp.where(diagonal, line, 0.0), axis=1, keepdims=True)
             states[2 * index][...] = jnp.broadcast_to(column, (rows, LANES))
-            block = refs[index][0:rows, :]
+            block = load(index)
             best = jnp.full((8, rows), -1.0, jnp.float32)
             for other in range(index + 1):
                 scores = lax.dot_general(
-                    refs[other][0:rows, :],
+                    load(other),
                     block,
                     (((1,), (1,)), ((), ())),
                     preferred_element_type=jnp.float32,
@@ -320,7 +343,7 @@
             @pl.when(lax.axis_index("chain") == home)
             def _():
                 for step, ref in enumerate(chunk_refs):
-                    row = (home + step) % chain_len
+                    row = home ^ step
                     ref[...] = jnp.where(is_home, found_ref[row : row + 1, :], 0.0)
 
 
@@ -331,77 +354,83 @@
     half = rows // 2
     run_slots = chain_len * clus_len * PIECE
     block = jax.ShapeDtypeStruct((half + TILE, width), jnp.bfloat16)
-    slots = jax.ShapeDtypeStruct((TILE, half), jnp.float32)
-    hot, slots, given_slots = pl.pallas_call(
-        functools.partial(place_kernel, run_slots, rows // clus_len // PIECE),
-        out_shape=(jax.ShapeDtypeStruct((rows, rows), jnp.bfloat16), slots, slots),
+    depth = rows // clus_len
+    hot, slots = pl.pallas_call(
+        functools.partial(place_kernel, run_slots, depth // PIECE),
+        out_shape=(
+            jax.ShapeDtypeStruct((rows, rows), jnp.bfloat16),
+            jax.ShapeDtypeStruct((TILE, rows), jnp.float32),
+        ),
         in_specs=[VMEM],
-        out_specs=(VMEM,) * 3,
-        cost_estimate=pl.CostEstimate(flops=0, bytes_accessed=8 * rows * width, transcendentals=0),
+        out_specs=(VMEM, VMEM),
         compiler_params=pltpu.CompilerParams(vmem_limit_bytes=16 * 2**20),
         name="place_rows",
     )(dest.reshape(1, rows))
-    kept, given = pl.pallas_call(
+    near, far, near_other, far_other = pl.pallas_call(
         send_kernel,
-        out_shape=(jax.ShapeDtypeStruct((half, width), jnp.bfloat16), block),
+        out_shape=(jax.ShapeDtypeStruct((depth + TILE, width), jnp.bfloat16),) * clus_len,
         in_specs=[VMEM] * 3,
-        out_specs=(VMEM, VMEM),
+        out_specs=(VMEM,) * clus_len,
         compiler_params=pltpu.CompilerParams(vmem_limit_bytes=16 * 2**20),
         name="send_blocks",
-    )(hot, given_slots, embeddings)
+    )(hot, slots, embeddings)
 
     def permute(value, moves):
         pairs = [(a * clus_len + b, c * clus_len + d) for a, b, c, d in moves]
         return lax.ppermute(value, ("chain", "clus"), pairs)
 
     low, high, top = chain_len // 2 - 1, chain_len // 2, chain_len - 1
-    swap = [(z, k, z, k ^ 1) for z in range(chain_len) for k in range(clus_len)]
-    near, far = pl.pallas_call(
-        merge_kernel,
-        out_shape=(block, block),
-        in_specs=[VMEM, VMEM, VMEM],
-        out_specs=(VMEM, VMEM),
+    places = [(z, k) for z in range(chain_len) for k in range(clus_len)]
+
+    def swap(value):
+        return permute(value, [(z, k, z, k ^ 1) for z, k in places])
+
+    def along(value, steps):
+        return permute(value, [(z, k, steps[z], k) if z in steps else (z, k, z, k ^ 1) for z, k in places])
+
+    def crossed(value):
+        came = permute(value, [(z, k, z, k ^ 2) for z, k in places])
+        return pl.pallas_call(
+            merge_kernel,
+            out_shape=block,
+            in_specs=[VMEM, VMEM],
+            out_specs=VMEM,
+            compiler_params=pltpu.CompilerParams(vmem_limit_bytes=16 * 2**20),
+            name="merge_blocks",
+        )(came, swap(came)), came
+
+    def to_home(value, moves):
+        pairs = []
+        for a, b in moves:
+            pairs += [(a, k ^ (a >= high), b, k ^ (b >= high)) for k in range(0, clus_len, 2)]
+        return permute(value, pairs)
+
+    far_crossed, far_came = crossed(far_other)
+    near_crossed, near_came = crossed(near_other)
+    from_far = along(far, {0: high, high: top, top: low, low: 0})
+    from_middle = along(far, {low: high, high: low})
+    from_near = along(near, {0: low, low: 0, top: high, high: top})
+    own = (near, from_near, from_far, from_middle)
+    helped = pl.pallas_call(
+        functools.partial(helper_kernel, len(own)),
+        out_shape=jax.ShapeDtypeStruct((len(own) * (depth + TILE), width), jnp.bfloat16),
+        in_specs=[VMEM] * (len(own) + 2),
+        out_specs=VMEM,
         compiler_params=pltpu.CompilerParams(vmem_limit_bytes=16 * 2**20),
-        name="merge_blocks",
-    )(kept, slots, permute(given, swap))
-
-    def serving(z, across):
-        return across ^ (z >= high)
-
-    def to_home(value, moves):
-        columns = range(clus_len // 2)
-        pairs = [(a, 2 * x + serving(a, 0), b, 2 * x + serving(b, 0)) for a, b in moves for x in columns]
-        if {a for a, _ in moves} == {b for _, b in moves}:
-            taken = {pair[:2] for pair in pairs}
-            everyone = [(z, k) for z in range(chain_len) for k in range(clus_len)]
-            pairs += [place + place for place in everyone if place not in taken]
-        return permute(value, pairs)
-
-    def across(value):
-        pairs = []
-        for z in range(chain_len):
-            for x in range(clus_len // 2):
-                own, other = serving(z, 0), serving(z, 1)
-                pairs.append((z, 2 * x + other, z, 2 * (x ^ 1) + own))
-                pairs.append((z, 2 * x + own, z, 2 * x + other))
-        return permute(value, pairs)
-
-    from_far = [(0, high), (top, low)]
-    from_near = [(0, low), (top, high)]
-    from_middle = [(low, high), (high, low)]
-    far_crossed, near_crossed = across(far), across(near)
-    far_along, near_along = to_home(far, from_far), to_home(near, from_near)
-    middle_along = to_home(far, from_middle)
-    far_after, near_after = to_home(far_crossed, from_far), to_home(near_crossed, from_near)
-    middle_after = to_home(far_crossed, from_middle)
-    stages = [[near, near_crossed, near_along, far_along], [far_after, middle_along], [near_after], [middle_after]]
+        name="help_home",
+    )(*own, far_came, near_came)
+    helped = swap(helped)
+    far_after = to_home(far_crossed, [(0, high), (top, low)])
+    middle_after = to_home(far_crossed, [(low, high), (high, low)])
+    near_after = to_home(near_crossed, [(0, low), (top, high)])
+    stages = [[*own], [near_crossed, far_after], [helped], [near_after], [middle_after]]
     blocks, states, held = [], [], 0
     state = jax.ShapeDtypeStruct((half, LANES), jnp.float32)
     chunk = jax.ShapeDtypeStruct((1, rows), jnp.float32)
     for number, arrived in enumerate(stages):
         first, last = number == 0, number == len(stages) - 1
         old, blocks = held, blocks + arrived
-        held = sum(value.shape[0] for value in blocks) // (half + TILE)
+        held = sum(value.shape[0] // depth for value in blocks) // 2
         outs = (chunk,) * chain_len if last else (state,) * (2 * held)
         outs += (jax.ShapeDtypeStruct((TILE, LANES), jnp.float32),) * first
         scratch = [pltpu.VMEM(state.shape, state.dtype)] * (2 * held)
@@ -421,8 +450,7 @@
     found = states[0]
     for step in range(1, chain_len):
         homes = [(low + k % 2, k) for k in range(clus_len)]
-        moves = [(home, k, (home + step) % chain_len, k) for home, k in homes]
-        found = found + permute(states[step], moves)
+        found = found + permute(states[step], [(home, k, home ^ step, k) for home, k in homes])
     return found
 
 

time: 42.3 us -> 44.3 us (1.047)
  waiting for transfers between devices: 17.1 us -> 23.2 us
  starting transfers between devices: 20.3 us -> 16.3 us
    ppermute x12 -> x14, waiting for transfers between devices: 17.1 us -> 23.2 us  [permute(): return lax.ppermute(value, ('chain', 'clus'), pairs)]
    ppermute x12 -> x14, starting transfers between devices: 20.3 us -> 16.3 us  [permute(): return lax.ppermute(value, ('chain', 'clus'), pairs)]
    pallas_call x3 -> x5, Pallas kernels: 1.35 us -> 1.42 us  [the longest x1 0.76 us: local_home(): pl.pallas_call(send_kernel, out_shape=(jax.ShapeDtypeStruct((depth + TILE...]
  transfers between devices with their start and end apart: 12 -> 14, of which waited for: 4 -> 8; matrix products, arithmetic and copies ran while one was open for 0% -> 0% of each run, Pallas kernels for 1% -> 1%
where the time goes in v12:
time: 44.3 us; the launch traced here: 44.1 us
  waiting for transfers between devices  23.2 us (52%)
  starting transfers between devices  16.3 us (37%)
  Pallas kernels  1.99 us (4%)
  local copies, waits for them, and re-layouts  1.83 us (4%)
  other arithmetic  0.59 us (1%)
    ppermute x14, waiting for transfers between devices, permute(): return lax.ppermute(value, ('chain', 'clus'), pairs)  23.2 us
    ppermute x14, starting transfers between devices, permute(): return lax.ppermute(value, ('chain', 'clus'), pairs)  16.3 us
    unnamed x6, local copies, waits for them, and re-layouts  1.83 us
  transfers between devices with their start and end apart: 14, of which 8 were waited for; matrix products, arithmetic and copies ran while one was open for 0% of the time, Pallas kernels for 1%

profile of v12, /device:TPU:0, one launch (start us, length us, event | category | flops | bytes accessed | tf_op | source)
XLA Modules:
  0.0 44.1 jit_solution(4209756731806317731)
XLA Ops:
  0.0 0.0 copy-start.1
  0.0 0.7 %copy-done.1 = s32[512]{0:T(512)S(1)} copy-done((s32[512]{0:T(512)S(1)}, s32[512]{0:T(512)}, u32[]{:S(2)}) %copy-start.1) | copy-done | bytes 2072
  0.7 0.5 %place_rows.1 = (bf16[512,512]{1,0:T(8,128)(2,1)S(1)}, f32[8,512]{1,0:T(8,128)S(1)}) custom-call(s32[1,512]{1,0:T(1,128)S(1)} %bitcast.1), custom_call_target="tpu_custom_call" | custom-call | tf_op jit(solution)/shard_map/place_rows/pallas_call | solution.py:358
  1.2 0.0 copy-start
  1.2 1.1 %copy-done = bf16[512,768]{1,0:T(8,128)(2,1)S(1)} copy-done((bf16[512,768]{1,0:T(8,128)(2,1)S(1)}, bf16[512,768]{1,0:T(8,128)(2,1)}, u32[]{:S(2)}) %copy-start) | copy-done | bytes 786456
  2.4 0.8 %send_blocks.1 = (bf16[136,768]{1,0:T(8,128)(2,1)S(1)}, bf16[136,768]{1,0:T(8,128)(2,1)S(1)}, bf16[136,768]{1,0:T(8,128)(2,1)S(1)}, bf16[136,768]{1,0:T(8,128)(2,1)S(1)}) custom-call(bf16[512,512]{1,0:T(8,128)(2,1)S(1)} %get-tuple-element.54.hot_ref, f32[8,512]{1,0:T(8,128)S(1)} %get-tuple-element.55.slots_ref, bf16[512,768]{1,0:T(8,128)(2,1)S(1)} %copy-done), custom_call_target="tpu_custom_call" | custom-call | tf_op jit(solution)/shard_map/send_blocks/pallas_call | solution.py:369
  3.1 3.0 %collective-permute-start.3 = (bf16[136,768]{1,0:T(8,128)(2,1)S(1)}, bf16[136,768]{1,0:T(8,128)(2,1)S(1)}, u32[]{:S(2)}, u32[]{:S(2)}) collective-permute-start(bf16[136,768]{1,0:T(8,128)(2,1)S(1)} %get-tuple-element.59), channel_id=1, source_target_pairs={{0,2},{1,3},{2,0},{3,1},{4,6},{5,7},{6,4},{7,5},{8,10},{9,11},{10,... | collective-permute-start | bytes 626696 | tf_op jit(solution)/shard_map/ppermute | solution.py:380
  6.1 0.1 collective-permute-start.5
  6.2 0.0 collective-permute-start.2
  6.2 3.5 %collective-permute-start.1 = (bf16[136,768]{1,0:T(8,128)(2,1)S(1)}, bf16[136,768]{1,0:T(8,128)(2,1)S(1)}, u32[]{:S(2)}, u32[]{:S(2)}) collective-permute-start(bf16[136,768]{1,0:T(8,128)(2,1)S(1)} %get-tuple-element.57), channel_id=1, source_target_pairs={{0,8},{1,9},{2,10},{3,11},{4,0},{5,1},{6,2},{7,3},{8,12},{9,13},{1... | collective-permute-start | bytes 626696 | tf_op jit(solution)/shard_map/ppermute | solution.py:380
  9.7 0.1 collective-permute-start
  9.8 2.3 %collective-permute-done.3.mine_ref.refs_5_ = bf16[136,768]{1,0:T(8,128)(2,1)S(1)} collective-permute-done((bf16[136,768]{1,0:T(8,128)(2,1)S(1)}, bf16[136,768]{1,0:T(8,128)(2,1)S(1)}, u32[]{:S(2)}, u32[]{:S(2)}) %collective-permute-start.3) | collective-permute-done | bytes 208928 | tf_op jit(solution)/shard_map/ppermute | solution.py:380
  12.1 3.6 %collective-permute-done.5.mine_ref.refs_4_ = bf16[136,768]{1,0:T(8,128)(2,1)S(1)} collective-permute-done((bf16[136,768]{1,0:T(8,128)(2,1)S(1)}, bf16[136,768]{1,0:T(8,128)(2,1)S(1)}, u32[]{:S(2)}, u32[]{:S(2)}) %collective-permute-start.5) | collective-permute-done | bytes 208928 | tf_op jit(solution)/shard_map/ppermute | solution.py:380
  15.8 0.0 collective-permute-done.2.rest_4_.refs_3_.rest_3_
  15.8 0.1 collective-permute-done.1.rest_3_.refs_2_.rest_2_
  15.9 2.7 %collective-permute-done.rest_2_.refs_1_.rest_1_ = bf16[136,768]{1,0:T(8,128)(2,1)S(1)} collective-permute-done((bf16[136,768]{1,0:T(8,128)(2,1)S(1)}, bf16[136,768]{1,0:T(8,128)(2,1)S(1)}, u32[]{:S(2)}, u32[]{:S(2)}) %collective-permute-start) | collective-permute-done | bytes 208928 | tf_op jit(solution)/shard_map/ppermute | solution.py:380
  18.6 0.1 help_home.1
  18.7 0.1 collective-permute-start.8
  18.8 0.5 %collective-permute-start.6 = (bf16[136,768]{1,0:T(8,128)(2,1)S(1)}, bf16[136,768]{1,0:T(8,128)(2,1)S(1)}, u32[]{:S(2)}, u32[]{:S(2)}) collective-permute-start(bf16[136,768]{1,0:T(8,128)(2,1)S(1)} %collective-permute-done.5.mine_ref.refs_4_), channel_id=1, source_target_pairs={{0,1},{1,0},{2,3},{3,2},{4,5},{5,4},{6,7},{7,6},{8,9},{9,8},{10,11... | collective-permute-start | bytes 626696 | tf_op jit(solution)/shard_map/ppermute | solution.py:380
  19.3 0.1 collective-permute-start.4
  19.3 2.1 %collective-permute-done.6.came_ref = bf16[136,768]{1,0:T(8,128)(2,1)S(1)} collective-permute-done((bf16[136,768]{1,0:T(8,128)(2,1)S(1)}, bf16[136,768]{1,0:T(8,128)(2,1)S(1)}, u32[]{:S(2)}, u32[]{:S(2)}) %collective-permute-start.6) | collective-permute-done | bytes 208928 | tf_op jit(solution)/shard_map/ppermute | solution.py:380
  21.4 0.0 copy-start.2
  21.5 4.4 %collective-permute-start.7 = (bf16[264,768]{1,0:T(8,128)(2,1)S(1)}, bf16[264,768]{1,0:T(8,128)(2,1)S(1)}, u32[]{:S(2)}, u32[]{:S(2)}) collective-permute-start(bf16[264,768]{1,0:T(8,128)(2,1)S(1)} %merge_blocks.3), channel_id=1, source_target_pairs={{0,9},{2,11},{13,4},{15,6},{16,25},{18,27},{29,20},{31,22}} | collective-permute-start | bytes 1216520 | tf_op jit(solution)/shard_map/ppermute | solution.py:380
  25.8 0.0 collective-permute-done.4.came_ref
  25.9 1.3 %collective-permute-start.9 = (bf16[264,768]{1,0:T(8,128)(2,1)S(1)}, bf16[264,768]{1,0:T(8,128)(2,1)S(1)}, u32[]{:S(2)}, u32[]{:S(2)}) collective-permute-start(bf16[264,768]{1,0:T(8,128)(2,1)S(1)} %merge_blocks.2.rest_4_.rest_5_), channel_id=1, source_target_pairs={{0,4},{2,6},{13,9},{15,11},{16,20},{18,22},{29,25},{31,27}} | collective-permute-start | bytes 1216520 | tf_op jit(solution)/shard_map/ppermute | solution.py:380
  27.2 0.7 %collective-permute-start.10 = (bf16[264,768]{1,0:T(8,128)(2,1)S(1)}, bf16[264,768]{1,0:T(8,128)(2,1)S(1)}, u32[]{:S(2)}, u32[]{:S(2)}) collective-permute-start(bf16[264,768]{1,0:T(8,128)(2,1)S(1)} %merge_blocks.3), channel_id=1, source_target_pairs={{4,9},{6,11},{9,4},{11,6},{20,25},{22,27},{25,20},{27,22}} | collective-permute-start | bytes 1216520 | tf_op jit(solution)/shard_map/ppermute | solution.py:380
  27.9 0.0 copy-done.2
  27.9 0.6 %multiply_arrived.4 = (f32[256,128]{1,0:T(8,128)S(1)}, f32[256,128]{1,0:T(8,128)S(1)}, f32[256,128]{1,0:T(8,128)S(1)}, f32[256,128]{1,0:T(8,128)S(1)}, f32[8,128]{1,0:T(8,128)S(1)}) custom-call(s32[4]{0:T(128)S(1)} %copy-done.2, bf16[136,768]{1,0:T(8,128)(2,1)S(1)} %get-tuple-element.56.rest_1_.refs_0_.rest_0_, ...), custom_call_target="tpu_custom_call" | custom-call | tf_op jit(solution)/shard_map/multiply_arrived/pallas_call | solution.py:439
  28.5 2.8 %collective-permute-done.7.rest_5_.rest_6_ = bf16[264,768]{1,0:T(8,128)(2,1)S(1)} collective-permute-done((bf16[264,768]{1,0:T(8,128)(2,1)S(1)}, bf16[264,768]{1,0:T(8,128)(2,1)S(1)}, u32[]{:S(2)}, u32[]{:S(2)}) %collective-permute-start.7) | collective-permute-done | bytes 405536 | tf_op jit(solution)/shard_map/ppermute | solution.py:380
  31.2 0.0 collective-permute-done.8.rest_6_.rest_7_
  31.2 4.3 %collective-permute-done.9.rest_7_.rest_8_ = bf16[264,768]{1,0:T(8,128)(2,1)S(1)} collective-permute-done((bf16[264,768]{1,0:T(8,128)(2,1)S(1)}, bf16[264,768]{1,0:T(8,128)(2,1)S(1)}, u32[]{:S(2)}, u32[]{:S(2)}) %collective-permute-start.9) | collective-permute-done | bytes 405536 | tf_op jit(solution)/shard_map/ppermute | solution.py:380
  35.6 0.0 collective-permute-done.10.rest_9_
  35.6 1.3 %collective-permute-start.11 = (f32[1,512]{1,0:T(1,128)S(1)}, f32[1,512]{1,0:T(1,128)S(1)}, u32[]{:S(2)}, u32[]{:S(2)}) collective-permute-start(f32[1,512]{1,0:T(1,128)S(1)} %get-tuple-element.100), channel_id=1, source_target_pairs={{4,0},{9,13},{6,2},{11,15},{20,16},{25,29},{22,18},{27,31}} | collective-permute-start | bytes 6152 | tf_op jit(solution)/shard_map/ppermute | solution.py:380
  36.9 0.7 %collective-permute-start.12 = (f32[1,512]{1,0:T(1,128)S(1)}, f32[1,512]{1,0:T(1,128)S(1)}, u32[]{:S(2)}, u32[]{:S(2)}) collective-permute-start(f32[1,512]{1,0:T(1,128)S(1)} %get-tuple-element.101), channel_id=1, source_target_pairs={{4,12},{9,1},{6,14},{11,3},{20,28},{25,17},{22,30},{27,19}} | collective-permute-start | bytes 6152 | tf_op jit(solution)/shard_map/ppermute | solution.py:380
  37.6 0.7 %collective-permute-start.13 = (f32[1,512]{1,0:T(1,128)S(1)}, f32[1,512]{1,0:T(1,128)S(1)}, u32[]{:S(2)}, u32[]{:S(2)}) collective-permute-start(f32[1,512]{1,0:T(1,128)S(1)} %get-tuple-element.102), channel_id=1, source_target_pairs={{4,8},{9,5},{6,10},{11,7},{20,24},{25,21},{22,26},{27,23}} | collective-permute-start | bytes 6152 | tf_op jit(solution)/shard_map/ppermute | solution.py:380
  38.2 5.2 %collective-permute-done.11 = f32[1,512]{1,0:T(1,128)S(1)} collective-permute-done((f32[1,512]{1,0:T(1,128)S(1)}, f32[1,512]{1,0:T(1,128)S(1)}, u32[]{:S(2)}, u32[]{:S(2)}) %collective-permute-start.11) | collective-permute-done | bytes 2080 | tf_op jit(solution)/shard_map/ppermute | solution.py:380
  43.5 0.0 collective-permute-done.12
  43.5 0.0 collective-permute-done.13
  43.5 0.6 %add_add_fusion = f32[1,512]{1,0:T(1,128)} fusion(f32[1,512]{1,0:T(1,128)S(1)} %collective-permute-done.13, f32[1,512]{1,0:T(1,128)S(1)} %collective-permute-done.12, f32[1,512]{1,0:T(1,128)S(1)} %get-tuple-element.99, f32[1,512]{1,0:T(1,128)S(1)} %collective-permute-done.11), kind=kLoop, calls=%fused_computation | loop fusion | flops 1536 | bytes 10240 | tf_op jit(solution)/shard_map/add | solution.py:453
  (6 shorter events, 0.1 us)
Async XLA Ops:
  0.0 0.7 %copy-start.1 = (s32[512]{0:T(512)S(1)}, s32[512]{0:T(512)}, u32[]{:S(2)}) copy-start(s32[512]{0:T(512)} %param.4) | copy-start | bytes 6148
  1.2 1.1 %copy-start = (bf16[512,768]{1,0:T(8,128)(2,1)S(1)}, bf16[512,768]{1,0:T(8,128)(2,1)}, u32[]{:S(2)}) copy-start(bf16[512,768]{1,0:T(8,128)(2,1)} %rows_ref.1) | copy-start | bytes 2359300
  3.1 9.0 %collective-permute-start.3 = (bf16[136,768]{1,0:T(8,128)(2,1)S(1)}, bf16[136,768]{1,0:T(8,128)(2,1)S(1)}, u32[]{:S(2)}, u32[]{:S(2)}) collective-permute-start(bf16[136,768]{1,0:T(8,128)(2,1)S(1)} %get-tuple-element.59), channel_id=1, source_target_pairs={{0,2},{1,3},{2,0},{3,1},{4,6},{5,7},{6,4},{7,5},{8,10},{9,11},{10,... | collective-permute-start | bytes 626696 | tf_op jit(solution)/shard_map/ppermute | solution.py:380
  6.1 9.6 %collective-permute-start.5 = (bf16[136,768]{1,0:T(8,128)(2,1)S(1)}, bf16[136,768]{1,0:T(8,128)(2,1)S(1)}, u32[]{:S(2)}, u32[]{:S(2)}) collective-permute-start(bf16[136,768]{1,0:T(8,128)(2,1)S(1)} %get-tuple-element.60), channel_id=1, source_target_pairs={{0,2},{1,3},{2,0},{3,1},{4,6},{5,7},{6,4},{7,5},{8,10},{9,11},{10,... | collective-permute-start | bytes 626696 | tf_op jit(solution)/shard_map/ppermute | solution.py:380
  6.2 9.6 %collective-permute-start.2 = (bf16[136,768]{1,0:T(8,128)(2,1)S(1)}, bf16[136,768]{1,0:T(8,128)(2,1)S(1)}, u32[]{:S(2)}, u32[]{:S(2)}) collective-permute-start(bf16[136,768]{1,0:T(8,128)(2,1)S(1)} %get-tuple-element.57), channel_id=1, source_target_pairs={{0,1},{1,0},{2,3},{3,2},{4,8},{5,9},{6,10},{7,11},{8,4},{9,5},{10,... | collective-permute-start | bytes 626696 | tf_op jit(solution)/shard_map/ppermute | solution.py:380
  6.2 9.7 %collective-permute-start.1 = (bf16[136,768]{1,0:T(8,128)(2,1)S(1)}, bf16[136,768]{1,0:T(8,128)(2,1)S(1)}, u32[]{:S(2)}, u32[]{:S(2)}) collective-permute-start(bf16[136,768]{1,0:T(8,128)(2,1)S(1)} %get-tuple-element.57), channel_id=1, source_target_pairs={{0,8},{1,9},{2,10},{3,11},{4,0},{5,1},{6,2},{7,3},{8,12},{9,13},{1... | collective-permute-start | bytes 626696 | tf_op jit(solution)/shard_map/ppermute | solution.py:380
  9.7 8.9 %collective-permute-start = (bf16[136,768]{1,0:T(8,128)(2,1)S(1)}, bf16[136,768]{1,0:T(8,128)(2,1)S(1)}, u32[]{:S(2)}, u32[]{:S(2)}) collective-permute-start(bf16[136,768]{1,0:T(8,128)(2,1)S(1)} %get-tuple-element.56.rest_1_.refs_0_.rest_0_), channel_id=1, source_target_pairs={{0,4},{1,5},{2,6},{3,7},{4,0},{5,1},{6,2},{7,3},{8,12},{9,13},{10,... | collective-permute-start | bytes 626696 | tf_op jit(solution)/shard_map/ppermute | solution.py:380
  18.7 12.6 %collective-permute-start.8 = (bf16[544,768]{1,0:T(8,128)(2,1)S(1)}, bf16[544,768]{1,0:T(8,128)(2,1)S(1)}, u32[]{:S(2)}, u32[]{:S(2)}) collective-permute-start(bf16[544,768]{1,0:T(8,128)(2,1)S(1)} %help_home.1), channel_id=1, source_target_pairs={{0,1},{1,0},{2,3},{3,2},{4,5},{5,4},{6,7},{7,6},{8,9},{9,8},{10,11... | collective-permute-start | bytes 2506760 | tf_op jit(solution)/shard_map/ppermute | solution.py:380
  18.8 2.6 %collective-permute-start.6 = (bf16[136,768]{1,0:T(8,128)(2,1)S(1)}, bf16[136,768]{1,0:T(8,128)(2,1)S(1)}, u32[]{:S(2)}, u32[]{:S(2)}) collective-permute-start(bf16[136,768]{1,0:T(8,128)(2,1)S(1)} %collective-permute-done.5.mine_ref.refs_4_), channel_id=1, source_target_pairs={{0,1},{1,0},{2,3},{3,2},{4,5},{5,4},{6,7},{7,6},{8,9},{9,8},{10,11... | collective-permute-start | bytes 626696 | tf_op jit(solution)/shard_map/ppermute | solution.py:380
  19.3 6.6 %collective-permute-start.4 = (bf16[136,768]{1,0:T(8,128)(2,1)S(1)}, bf16[136,768]{1,0:T(8,128)(2,1)S(1)}, u32[]{:S(2)}, u32[]{:S(2)}) collective-permute-start(bf16[136,768]{1,0:T(8,128)(2,1)S(1)} %collective-permute-done.3.mine_ref.refs_5_), channel_id=1, source_target_pairs={{0,1},{1,0},{2,3},{3,2},{4,5},{5,4},{6,7},{7,6},{8,9},{9,8},{10,11... | collective-permute-start | bytes 626696 | tf_op jit(solution)/shard_map/ppermute | solution.py:380
  21.4 6.4 %copy-start.2 = (s32[4]{0:T(128)S(1)}, s32[4]{0:T(128)}, u32[]{:S(2)}) copy-start(s32[4]{0:T(128)} %rest_0_.1) | copy-start | bytes 52
  21.5 9.8 %collective-permute-start.7 = (bf16[264,768]{1,0:T(8,128)(2,1)S(1)}, bf16[264,768]{1,0:T(8,128)(2,1)S(1)}, u32[]{:S(2)}, u32[]{:S(2)}) collective-permute-start(bf16[264,768]{1,0:T(8,128)(2,1)S(1)} %merge_blocks.3), channel_id=1, source_target_pairs={{0,9},{2,11},{13,4},{15,6},{16,25},{18,27},{29,20},{31,22}} | collective-permute-start | bytes 1216520 | tf_op jit(solution)/shard_map/ppermute | solution.py:380
  25.9 9.7 %collective-permute-start.9 = (bf16[264,768]{1,0:T(8,128)(2,1)S(1)}, bf16[264,768]{1,0:T(8,128)(2,1)S(1)}, u32[]{:S(2)}, u32[]{:S(2)}) collective-permute-start(bf16[264,768]{1,0:T(8,128)(2,1)S(1)} %merge_blocks.2.rest_4_.rest_5_), channel_id=1, source_target_pairs={{0,4},{2,6},{13,9},{15,11},{16,20},{18,22},{29,25},{31,27}} | collective-permute-start | bytes 1216520 | tf_op jit(solution)/shard_map/ppermute | solution.py:380
  27.2 8.4 %collective-permute-start.10 = (bf16[264,768]{1,0:T(8,128)(2,1)S(1)}, bf16[264,768]{1,0:T(8,128)(2,1)S(1)}, u32[]{:S(2)}, u32[]{:S(2)}) collective-permute-start(bf16[264,768]{1,0:T(8,128)(2,1)S(1)} %merge_blocks.3), channel_id=1, source_target_pairs={{4,9},{6,11},{9,4},{11,6},{20,25},{22,27},{25,20},{27,22}} | collective-permute-start | bytes 1216520 | tf_op jit(solution)/shard_map/ppermute | solution.py:380
  35.6 7.9 %collective-permute-start.11 = (f32[1,512]{1,0:T(1,128)S(1)}, f32[1,512]{1,0:T(1,128)S(1)}, u32[]{:S(2)}, u32[]{:S(2)}) collective-permute-start(f32[1,512]{1,0:T(1,128)S(1)} %get-tuple-element.100), channel_id=1, source_target_pairs={{4,0},{9,13},{6,2},{11,15},{20,16},{25,29},{22,18},{27,31}} | collective-permute-start | bytes 6152 | tf_op jit(solution)/shard_map/ppermute | solution.py:380
  36.9 6.6 %collective-permute-start.12 = (f32[1,512]{1,0:T(1,128)S(1)}, f32[1,512]{1,0:T(1,128)S(1)}, u32[]{:S(2)}, u32[]{:S(2)}) collective-permute-start(f32[1,512]{1,0:T(1,128)S(1)} %get-tuple-element.101), channel_id=1, source_target_pairs={{4,12},{9,1},{6,14},{11,3},{20,28},{25,17},{22,30},{27,19}} | collective-permute-start | bytes 6152 | tf_op jit(solution)/shard_map/ppermute | solution.py:380
  37.6 5.9 %collective-permute-start.13 = (f32[1,512]{1,0:T(1,128)S(1)}, f32[1,512]{1,0:T(1,128)S(1)}, u32[]{:S(2)}, u32[]{:S(2)}) collective-permute-start(f32[1,512]{1,0:T(1,128)S(1)} %get-tuple-element.102), channel_id=1, source_target_pairs={{4,8},{9,5},{6,10},{11,7},{20,24},{25,21},{22,26},{27,23}} | collective-permute-start | bytes 6152 | tf_op jit(solution)/shard_map/ppermute | solution.py:380

commit v13 on v8

--- a/solution.py
+++ b/solution.py
@@ -365,20 +365,27 @@
         )
 
     def across(value):
-        return permute(
-            value,
-            [
-                (z, 2 * x + serving(z, 1), z, 2 * (x ^ 1) + serving(z, 0))
-                for z in range(chain_len)
-                for x in range(clus_len // 2)
-            ],
-        )
+        pairs = []
+        for z in range(chain_len):
+            for x in range(clus_len // 2):
+                own, other = serving(z, 0), serving(z, 1)
+                pairs.append((z, 2 * x + other, z, 2 * (x ^ 1) + own))
+                pairs.append((z, 2 * x + own, z, 2 * x + other))
+        return permute(value, pairs)
 
     from_far = [(0, high), (top, low)]
     from_near = [(0, low), (top, high)]
     from_middle = [(low, high), (high, low)]
     far_crossed, near_crossed = across(far), across(near)
-    stages = [[near, to_home(far, from_far), to_home(near, from_near), to_home(far, from_middle), near_crossed], [to_home(far_crossed, from_far)], [to_home(near_crossed, from_near), to_home(far_crossed, from_middle)]]
+    far_along, near_along = to_home(far, from_far), to_home(near, from_near)
+    middle_along = to_home(far, from_middle)
+    far_after, near_after = to_home(far_crossed, from_far), to_home(near_crossed, from_near)
+    middle_after = to_home(far_crossed, from_middle)
+    stages = [
+        [near, near_crossed, near_along, far_along],
+        [far_after, middle_along],
+        [near_after, middle_after],
+    ]
     blocks, states, held = [], [], 0
     state = jax.ShapeDtypeStruct((half, LANES), jnp.float32)
     chunk = jax.ShapeDtypeStruct((1, rows), jnp.float32)

time: 42.6 us -> 41.6 us (0.977)
  starting transfers between devices: 22.2 us -> 20.4 us
  waiting for transfers between devices: 15.8 us -> 16.7 us
    ppermute x12, starting transfers between devices: 22.2 us -> 20.4 us  [permute(): return lax.ppermute(value, ('chain', 'clus'), pairs)]
    ppermute x12, waiting for transfers between devices: 15.8 us -> 16.7 us  [permute(): return lax.ppermute(value, ('chain', 'clus'), pairs)]
where the time goes in v13:
time: 41.6 us; the launch traced here: 41.3 us
  starting transfers between devices  20.4 us (49%)
  waiting for transfers between devices  16.7 us (40%)
  local copies, waits for them, and re-layouts  1.82 us (4%)
  Pallas kernels  1.66 us (4%)
  other arithmetic  0.59 us (1%)
    ppermute x12, starting transfers between devices, permute(): return lax.ppermute(value, ('chain', 'clus'), pairs)  20.4 us
    ppermute x12, waiting for transfers between devices, permute(): return lax.ppermute(value, ('chain', 'clus'), pairs)  16.7 us
    unnamed x6, local copies, waits for them, and re-layouts  1.82 us
    pallas_call x1, Pallas kernels, local_home(): pl.pallas_call(functools.partial(send_kernel, run_slots, rows // clus_len...  1.04 us
  transfers between devices with their start and end apart: 12, of which 4 were waited for; matrix products, arithmetic and copies ran while one was open for 0% of the time, Pallas kernels for 1%

profile of v13, /device:TPU:0, one launch (start us, length us, event | category | flops | bytes accessed | tf_op | source)
XLA Modules:
  0.0 41.3 jit_solution(17279721839098769100)
XLA Ops:
  0.0 0.0 copy-start
  0.0 1.1 %copy-done = bf16[512,768]{1,0:T(8,128)(2,1)S(1)} copy-done((bf16[512,768]{1,0:T(8,128)(2,1)S(1)}, bf16[512,768]{1,0:T(8,128)(2,1)}, u32[]{:S(2)}) %copy-start) | copy-done | bytes 786456
  1.1 0.0 copy-start.1
  1.1 0.7 %copy-done.1 = s32[512]{0:T(512)S(1)} copy-done((s32[512]{0:T(512)S(1)}, s32[512]{0:T(512)}, u32[]{:S(2)}) %copy-start.1) | copy-done | bytes 2072
  1.8 1.0 %send_blocks.1 = (bf16[256,768]{1,0:T(8,128)(2,1)S(1)}, f32[8,256]{1,0:T(8,128)S(1)}, bf16[264,768]{1,0:T(8,128)(2,1)S(1)}) custom-call(s32[1,512]{1,0:T(1,128)S(1)} %bitcast.1, bf16[512,768]{1,0:T(8,128)(2,1)S(1)} %copy-done), custom_call_target="tpu_custom_call" | custom-call | tf_op jit(solution)/shard_map/send_blocks/pallas_call | solution.py:330
  2.9 0.5 %collective-permute-start = (bf16[264,768]{1,0:T(8,128)(2,1)S(1)}, bf16[264,768]{1,0:T(8,128)(2,1)S(1)}, u32[]{:S(2)}, u32[]{:S(2)}) collective-permute-start(bf16[264,768]{1,0:T(8,128)(2,1)S(1)} %get-tuple-element.37), channel_id=1, source_target_pairs={{0,1},{1,0},{2,3},{3,2},{4,5},{5,4},{6,7},{7,6},{8,9},{9,8},{10,11... | collective-permute-start | bytes 1216520 | tf_op jit(solution)/shard_map/ppermute | solution.py:345
  3.4 1.4 %collective-permute-done.came_ref = bf16[264,768]{1,0:T(8,128)(2,1)S(1)} collective-permute-done((bf16[264,768]{1,0:T(8,128)(2,1)S(1)}, bf16[264,768]{1,0:T(8,128)(2,1)S(1)}, u32[]{:S(2)}, u32[]{:S(2)}) %collective-permute-start) | collective-permute-done | bytes 405536 | tf_op jit(solution)/shard_map/ppermute | solution.py:345
  4.7 0.1 merge_blocks.1
  4.8 0.0 copy-start.2
  4.8 0.4 %collective-permute-start.4 = (bf16[264,768]{1,0:T(8,128)(2,1)S(1)}, bf16[264,768]{1,0:T(8,128)(2,1)S(1)}, u32[]{:S(2)}, u32[]{:S(2)}) collective-permute-start(bf16[264,768]{1,0:T(8,128)(2,1)S(1)} %get-tuple-element.39), channel_id=1, source_target_pairs={{1,2},{0,1},{3,0},{2,3},{5,6},{4,5},{7,4},{6,7},{8,11},{9,8},{10,9... | collective-permute-start | bytes 1216520 | tf_op jit(solution)/shard_map/ppermute | solution.py:345
  5.2 2.6 %collective-permute-start.1 = (bf16[264,768]{1,0:T(8,128)(2,1)S(1)}, bf16[264,768]{1,0:T(8,128)(2,1)S(1)}, u32[]{:S(2)}, u32[]{:S(2)}) collective-permute-start(bf16[264,768]{1,0:T(8,128)(2,1)S(1)} %get-tuple-element.38.rest_1_.rest_0_), channel_id=1, source_target_pairs={{1,2},{0,1},{3,0},{2,3},{5,6},{4,5},{7,4},{6,7},{8,11},{9,8},{10,9... | collective-permute-start | bytes 1216520 | tf_op jit(solution)/shard_map/ppermute | solution.py:345
  7.8 3.5 %collective-permute-start.2 = (bf16[264,768]{1,0:T(8,128)(2,1)S(1)}, bf16[264,768]{1,0:T(8,128)(2,1)S(1)}, u32[]{:S(2)}, u32[]{:S(2)}) collective-permute-start(bf16[264,768]{1,0:T(8,128)(2,1)S(1)} %get-tuple-element.38.rest_1_.rest_0_), channel_id=1, source_target_pairs={{0,4},{2,6},{13,9},{15,11},{16,20},{18,22},{29,25},{31,27}} | collective-permute-start | bytes 1216520 | tf_op jit(solution)/shard_map/ppermute | solution.py:345
  11.3 2.1 %collective-permute-start.3 = (bf16[264,768]{1,0:T(8,128)(2,1)S(1)}, bf16[264,768]{1,0:T(8,128)(2,1)S(1)}, u32[]{:S(2)}, u32[]{:S(2)}) collective-permute-start(bf16[264,768]{1,0:T(8,128)(2,1)S(1)} %get-tuple-element.39), channel_id=1, source_target_pairs={{0,9},{2,11},{13,4},{15,6},{16,25},{18,27},{29,20},{31,22}} | collective-permute-start | bytes 1216520 | tf_op jit(solution)/shard_map/ppermute | solution.py:345
  13.4 0.7 %collective-permute-start.6 = (bf16[264,768]{1,0:T(8,128)(2,1)S(1)}, bf16[264,768]{1,0:T(8,128)(2,1)S(1)}, u32[]{:S(2)}, u32[]{:S(2)}) collective-permute-start(bf16[264,768]{1,0:T(8,128)(2,1)S(1)} %get-tuple-element.39), channel_id=1, source_target_pairs={{4,9},{6,11},{9,4},{11,6},{20,25},{22,27},{25,20},{27,22}} | collective-permute-start | bytes 1216520 | tf_op jit(solution)/shard_map/ppermute | solution.py:345
  14.1 0.0 collective-permute-done.4
  14.1 3.7 %collective-permute-start.5 = (bf16[264,768]{1,0:T(8,128)(2,1)S(1)}, bf16[264,768]{1,0:T(8,128)(2,1)S(1)}, u32[]{:S(2)}, u32[]{:S(2)}) collective-permute-start(bf16[264,768]{1,0:T(8,128)(2,1)S(1)} %collective-permute-done.4), channel_id=1, source_target_pairs={{0,9},{2,11},{13,4},{15,6},{16,25},{18,27},{29,20},{31,22}} | collective-permute-start | bytes 1216520 | tf_op jit(solution)/shard_map/ppermute | solution.py:345
  17.8 0.0 collective-permute-done.1.rest_2_.rest_1_
  17.8 3.6 %collective-permute-start.7 = (bf16[264,768]{1,0:T(8,128)(2,1)S(1)}, bf16[264,768]{1,0:T(8,128)(2,1)S(1)}, u32[]{:S(2)}, u32[]{:S(2)}) collective-permute-start(bf16[264,768]{1,0:T(8,128)(2,1)S(1)} %collective-permute-done.1.rest_2_.rest_1_), channel_id=1, source_target_pairs={{0,4},{2,6},{13,9},{15,11},{16,20},{18,22},{29,25},{31,27}} | collective-permute-start | bytes 1216520 | tf_op jit(solution)/shard_map/ppermute | solution.py:345
  21.4 0.0 collective-permute-done.2.rest_3_.rest_2_
  21.4 0.7 %collective-permute-start.8 = (bf16[264,768]{1,0:T(8,128)(2,1)S(1)}, bf16[264,768]{1,0:T(8,128)(2,1)S(1)}, u32[]{:S(2)}, u32[]{:S(2)}) collective-permute-start(bf16[264,768]{1,0:T(8,128)(2,1)S(1)} %collective-permute-done.4), channel_id=1, source_target_pairs={{4,9},{6,11},{9,4},{11,6},{20,25},{22,27},{25,20},{27,22}} | collective-permute-start | bytes 1216520 | tf_op jit(solution)/shard_map/ppermute | solution.py:345
  22.1 0.0 collective-permute-done.3.rest_4_.rest_3_
  22.1 0.0 copy-done.2
  22.1 0.6 %multiply_arrived.2 = (f32[256,128]{1,0:T(8,128)S(1)}, f32[256,128]{1,0:T(8,128)S(1)}, f32[256,128]{1,0:T(8,128)S(1)}, f32[256,128]{1,0:T(8,128)S(1)}, f32[256,1...) custom-call(s32[4]{0:T(128)S(1)} %copy-done.2, ...), custom_call_target="tpu_custom_call" | custom-call | tf_op jit(solution)/shard_map/multiply_arrived/pallas_call | solution.py:401
  22.7 0.0 collective-permute-done.6.rest_5_.rest_6_
  22.7 2.7 %collective-permute-done.5.rest_4_.rest_5_ = bf16[264,768]{1,0:T(8,128)(2,1)S(1)} collective-permute-done((bf16[264,768]{1,0:T(8,128)(2,1)S(1)}, bf16[264,768]{1,0:T(8,128)(2,1)S(1)}, u32[]{:S(2)}, u32[]{:S(2)}) %collective-permute-start.5) | collective-permute-done | bytes 405536 | tf_op jit(solution)/shard_map/ppermute | solution.py:345
  25.5 4.3 %collective-permute-done.7.rest_7_ = bf16[264,768]{1,0:T(8,128)(2,1)S(1)} collective-permute-done((bf16[264,768]{1,0:T(8,128)(2,1)S(1)}, bf16[264,768]{1,0:T(8,128)(2,1)S(1)}, u32[]{:S(2)}, u32[]{:S(2)}) %collective-permute-start.7) | collective-permute-done | bytes 405536 | tf_op jit(solution)/shard_map/ppermute | solution.py:345
  29.8 0.0 collective-permute-done.8.rest_8_
  29.8 0.7 %collective-permute-start.10 = (f32[1,512]{1,0:T(1,128)S(1)}, f32[1,512]{1,0:T(1,128)S(1)}, u32[]{:S(2)}, u32[]{:S(2)}) collective-permute-start(f32[1,512]{1,0:T(1,128)S(1)} %get-tuple-element.63), channel_id=1, source_target_pairs={{4,12},{9,1},{6,14},{11,3},{20,28},{25,17},{22,30},{27,19}} | collective-permute-start | bytes 6152 | tf_op jit(solution)/shard_map/ppermute | solution.py:345
  30.5 1.3 %collective-permute-start.11 = (f32[1,512]{1,0:T(1,128)S(1)}, f32[1,512]{1,0:T(1,128)S(1)}, u32[]{:S(2)}, u32[]{:S(2)}) collective-permute-start(f32[1,512]{1,0:T(1,128)S(1)} %get-tuple-element.64), channel_id=1, source_target_pairs={{4,0},{9,5},{6,2},{11,7},{20,16},{25,21},{22,18},{27,23}} | collective-permute-start | bytes 6152 | tf_op jit(solution)/shard_map/ppermute | solution.py:345
  31.8 0.7 %collective-permute-start.9 = (f32[1,512]{1,0:T(1,128)S(1)}, f32[1,512]{1,0:T(1,128)S(1)}, u32[]{:S(2)}, u32[]{:S(2)}) collective-permute-start(f32[1,512]{1,0:T(1,128)S(1)} %get-tuple-element.62), channel_id=1, source_target_pairs={{4,8},{9,13},{6,10},{11,15},{20,24},{25,29},{22,26},{27,31}} | collective-permute-start | bytes 6152 | tf_op jit(solution)/shard_map/ppermute | solution.py:345
  32.4 0.0 collective-permute-done.10
  32.5 8.3 %collective-permute-done.11 = f32[1,512]{1,0:T(1,128)S(1)} collective-permute-done((f32[1,512]{1,0:T(1,128)S(1)}, f32[1,512]{1,0:T(1,128)S(1)}, u32[]{:S(2)}, u32[]{:S(2)}) %collective-permute-start.11) | collective-permute-done | bytes 2080 | tf_op jit(solution)/shard_map/ppermute | solution.py:345
  40.7 0.0 collective-permute-done.9
  40.7 0.6 %add_add_fusion = f32[1,512]{1,0:T(1,128)} fusion(f32[1,512]{1,0:T(1,128)S(1)} %collective-permute-done.11, f32[1,512]{1,0:T(1,128)S(1)} %collective-permute-done.10, f32[1,512]{1,0:T(1,128)S(1)} %get-tuple-element.61, f32[1,512]{1,0:T(1,128)S(1)} %collective-permute-done.9), kind=kLoop, calls=%fused_computation | loop fusion | flops 1536 | bytes 10240 | tf_op jit(solution)/shard_map/add | solution.py:416
  (2 shorter events, 0.0 us)
Async XLA Ops:
  0.0 1.1 %copy-start = (bf16[512,768]{1,0:T(8,128)(2,1)S(1)}, bf16[512,768]{1,0:T(8,128)(2,1)}, u32[]{:S(2)}) copy-start(bf16[512,768]{1,0:T(8,128)(2,1)} %rows_ref.1) | copy-start | bytes 2359300
  1.1 0.7 %copy-start.1 = (s32[512]{0:T(512)S(1)}, s32[512]{0:T(512)}, u32[]{:S(2)}) copy-start(s32[512]{0:T(512)} %param.4) | copy-start | bytes 6148
  2.9 1.9 %collective-permute-start = (bf16[264,768]{1,0:T(8,128)(2,1)S(1)}, bf16[264,768]{1,0:T(8,128)(2,1)S(1)}, u32[]{:S(2)}, u32[]{:S(2)}) collective-permute-start(bf16[264,768]{1,0:T(8,128)(2,1)S(1)} %get-tuple-element.37), channel_id=1, source_target_pairs={{0,1},{1,0},{2,3},{3,2},{4,5},{5,4},{6,7},{7,6},{8,9},{9,8},{10,11... | collective-permute-start | bytes 1216520 | tf_op jit(solution)/shard_map/ppermute | solution.py:345
  4.8 17.3 %copy-start.2 = (s32[4]{0:T(128)S(1)}, s32[4]{0:T(128)}, u32[]{:S(2)}) copy-start(s32[4]{0:T(128)} %rest_0_.1) | copy-start | bytes 52
  4.8 9.3 %collective-permute-start.4 = (bf16[264,768]{1,0:T(8,128)(2,1)S(1)}, bf16[264,768]{1,0:T(8,128)(2,1)S(1)}, u32[]{:S(2)}, u32[]{:S(2)}) collective-permute-start(bf16[264,768]{1,0:T(8,128)(2,1)S(1)} %get-tuple-element.39), channel_id=1, source_target_pairs={{1,2},{0,1},{3,0},{2,3},{5,6},{4,5},{7,4},{6,7},{8,11},{9,8},{10,9... | collective-permute-start | bytes 1216520 | tf_op jit(solution)/shard_map/ppermute | solution.py:345
  5.2 12.6 %collective-permute-start.1 = (bf16[264,768]{1,0:T(8,128)(2,1)S(1)}, bf16[264,768]{1,0:T(8,128)(2,1)S(1)}, u32[]{:S(2)}, u32[]{:S(2)}) collective-permute-start(bf16[264,768]{1,0:T(8,128)(2,1)S(1)} %get-tuple-element.38.rest_1_.rest_0_), channel_id=1, source_target_pairs={{1,2},{0,1},{3,0},{2,3},{5,6},{4,5},{7,4},{6,7},{8,11},{9,8},{10,9... | collective-permute-start | bytes 1216520 | tf_op jit(solution)/shard_map/ppermute | solution.py:345
  7.8 13.6 %collective-permute-start.2 = (bf16[264,768]{1,0:T(8,128)(2,1)S(1)}, bf16[264,768]{1,0:T(8,128)(2,1)S(1)}, u32[]{:S(2)}, u32[]{:S(2)}) collective-permute-start(bf16[264,768]{1,0:T(8,128)(2,1)S(1)} %get-tuple-element.38.rest_1_.rest_0_), channel_id=1, source_target_pairs={{0,4},{2,6},{13,9},{15,11},{16,20},{18,22},{29,25},{31,27}} | collective-permute-start | bytes 1216520 | tf_op jit(solution)/shard_map/ppermute | solution.py:345
  11.3 10.8 %collective-permute-start.3 = (bf16[264,768]{1,0:T(8,128)(2,1)S(1)}, bf16[264,768]{1,0:T(8,128)(2,1)S(1)}, u32[]{:S(2)}, u32[]{:S(2)}) collective-permute-start(bf16[264,768]{1,0:T(8,128)(2,1)S(1)} %get-tuple-element.39), channel_id=1, source_target_pairs={{0,9},{2,11},{13,4},{15,6},{16,25},{18,27},{29,20},{31,22}} | collective-permute-start | bytes 1216520 | tf_op jit(solution)/shard_map/ppermute | solution.py:345
  13.4 9.3 %collective-permute-start.6 = (bf16[264,768]{1,0:T(8,128)(2,1)S(1)}, bf16[264,768]{1,0:T(8,128)(2,1)S(1)}, u32[]{:S(2)}, u32[]{:S(2)}) collective-permute-start(bf16[264,768]{1,0:T(8,128)(2,1)S(1)} %get-tuple-element.39), channel_id=1, source_target_pairs={{4,9},{6,11},{9,4},{11,6},{20,25},{22,27},{25,20},{27,22}} | collective-permute-start | bytes 1216520 | tf_op jit(solution)/shard_map/ppermute | solution.py:345
  14.1 11.3 %collective-permute-start.5 = (bf16[264,768]{1,0:T(8,128)(2,1)S(1)}, bf16[264,768]{1,0:T(8,128)(2,1)S(1)}, u32[]{:S(2)}, u32[]{:S(2)}) collective-permute-start(bf16[264,768]{1,0:T(8,128)(2,1)S(1)} %collective-permute-done.4), channel_id=1, source_target_pairs={{0,9},{2,11},{13,4},{15,6},{16,25},{18,27},{29,20},{31,22}} | collective-permute-start | bytes 1216520 | tf_op jit(solution)/shard_map/ppermute | solution.py:345
  17.8 12.0 %collective-permute-start.7 = (bf16[264,768]{1,0:T(8,128)(2,1)S(1)}, bf16[264,768]{1,0:T(8,128)(2,1)S(1)}, u32[]{:S(2)}, u32[]{:S(2)}) collective-permute-start(bf16[264,768]{1,0:T(8,128)(2,1)S(1)} %collective-permute-done.1.rest_2_.rest_1_), channel_id=1, source_target_pairs={{0,4},{2,6},{13,9},{15,11},{16,20},{18,22},{29,25},{31,27}} | collective-permute-start | bytes 1216520 | tf_op jit(solution)/shard_map/ppermute | solution.py:345
  21.4 8.4 %collective-permute-start.8 = (bf16[264,768]{1,0:T(8,128)(2,1)S(1)}, bf16[264,768]{1,0:T(8,128)(2,1)S(1)}, u32[]{:S(2)}, u32[]{:S(2)}) collective-permute-start(bf16[264,768]{1,0:T(8,128)(2,1)S(1)} %collective-permute-done.4), channel_id=1, source_target_pairs={{4,9},{6,11},{9,4},{11,6},{20,25},{22,27},{25,20},{27,22}} | collective-permute-start | bytes 1216520 | tf_op jit(solution)/shard_map/ppermute | solution.py:345
  29.8 2.6 %collective-permute-start.10 = (f32[1,512]{1,0:T(1,128)S(1)}, f32[1,512]{1,0:T(1,128)S(1)}, u32[]{:S(2)}, u32[]{:S(2)}) collective-permute-start(f32[1,512]{1,0:T(1,128)S(1)} %get-tuple-element.63), channel_id=1, source_target_pairs={{4,12},{9,1},{6,14},{11,3},{20,28},{25,17},{22,30},{27,19}} | collective-permute-start | bytes 6152 | tf_op jit(solution)/shard_map/ppermute | solution.py:345
  30.5 10.2 %collective-permute-start.11 = (f32[1,512]{1,0:T(1,128)S(1)}, f32[1,512]{1,0:T(1,128)S(1)}, u32[]{:S(2)}, u32[]{:S(2)}) collective-permute-start(f32[1,512]{1,0:T(1,128)S(1)} %get-tuple-element.64), channel_id=1, source_target_pairs={{4,0},{9,5},{6,2},{11,7},{20,16},{25,21},{22,18},{27,23}} | collective-permute-start | bytes 6152 | tf_op jit(solution)/shard_map/ppermute | solution.py:345
  31.8 8.9 %collective-permute-start.9 = (f32[1,512]{1,0:T(1,128)S(1)}, f32[1,512]{1,0:T(1,128)S(1)}, u32[]{:S(2)}, u32[]{:S(2)}) collective-permute-start(f32[1,512]{1,0:T(1,128)S(1)} %get-tuple-element.62), channel_id=1, source_target_pairs={{4,8},{9,13},{6,10},{11,15},{20,24},{25,29},{22,26},{27,31}} | collective-permute-start | bytes 6152 | tf_op jit(solution)/shard_map/ppermute | solution.py:345
